TPU v7x, 128 devices: a whole 4x4x4 slice. The times are simulated.
128 devices in a mesh: seq: 32 (over y, z, core), chan: 4 (over x).
Axes of the slice: x: 4, y: 4, z: 4, core: 2. Of those that a mesh axis runs over, the one named last changes fastest.
Arguments:
- features: bfloat16 [4096, 3, 4096], P('seq', None, 'chan'), may hold values from -6 to 6
- short_taps: float32 [3, 3, 4096], P(None, None, 'chan'), may hold values from -4 to 4
- skip_gain: float32 [4096], P('chan'), may hold values from 0.5 to 1.5
- long_filter: float32 [4096, 4096], P('seq', 'chan'), may hold values from -0.09375 to 0.09375
- out_weight: bfloat16 [4096, 8192], P('chan'), may hold values from -0.125 to 0.125
Outputs:
- layer_out: bfloat16 [4096, 8192], P('seq', 'chan')
All inputs are finite; a program needn't handle non-finite values.
Results may differ from a plain program's by a relative error of at most 0.02.
Values may be sent and summed in bfloat16 or wider, within the bound.
No kernel may reach another device: no remote copies, remote signals or barrier semaphores. Data moves between devices by JAX's collectives and lax.ppermute only.
A program may use at most 128 MiB of HBM per device.

v0:
```python
import math

import jax
import jax.numpy as jnp
import ml_dtypes
import numpy as np
from jax import lax
from jax.experimental import pallas as pl
from jax.experimental.pallas import tpu as pltpu
from jax.sharding import PartitionSpec as P

GROUP = 16


def whole():
    return pl.BlockSpec(memory_space=pltpu.VMEM)


def transform_table(blocks, length):
    total = blocks * length
    k1 = np.arange(blocks)[:, None] + 0.25
    outer = 2.0 * math.pi * k1 * np.arange(blocks)[None, :] / blocks
    eye = np.eye(GROUP)
    ahead = np.concatenate([np.kron(np.cos(outer), eye), np.kron(-np.sin(outer), eye)], axis=0)
    back = np.concatenate([np.kron(np.cos(outer).T, eye), np.kron(-np.sin(outer).T, eye)], axis=0) / total
    inner = 2.0 * math.pi * np.outer(np.arange(length), np.arange(length)) / length
    cosine, sine = np.cos(inner), np.sin(inner)
    inner_ahead = np.concatenate([cosine, -sine, sine, cosine], axis=1)
    inner_back = np.concatenate([cosine, sine, -sine, cosine], axis=1)
    twist = 2.0 * math.pi * k1 * np.arange(length)[None, :] / total
    twist = np.concatenate([np.cos(twist), np.sin(twist)], axis=1).astype(np.float32)
    high = twist.astype(ml_dtypes.bfloat16)
    low = (twist - high.astype(np.float32)).astype(ml_dtypes.bfloat16)
    parts = [ahead, back, inner_ahead, inner_back, np.concatenate([high, low], axis=1)]
    return jnp.asarray(np.concatenate([part.astype(ml_dtypes.bfloat16) for part in parts], axis=0))


def read_table(table, blocks, length):
    size = blocks * GROUP
    at = 4 * size
    inner_ahead = jnp.concatenate([table[at : at + length, : 2 * length], table[at : at + length, 2 * length :]], axis=0)
    at += length
    inner_back = jnp.concatenate([table[at : at + length, : 2 * length], table[at : at + length, 2 * length :]], axis=0)
    at += length
    twist = table[at : at + blocks, :].astype(jnp.float32)
    twist = twist[:, : 2 * length] + twist[:, 2 * length :]
    spread = lambda part: jnp.broadcast_to(part[:, None, :], (blocks, GROUP, length)).reshape(size, length)
    return inner_ahead, inner_back, spread(twist[:, :length]), spread(twist[:, length:])


def start_all(pairs, sems):
    copies = [pltpu.make_async_copy(source, target, sems.at[i]) for i, (source, target) in enumerate(pairs)]
    for copy in copies:
        copy.start()
    return copies


def store_turned(target, first_row, value, start):
    parts, _, length = target.shape
    lanes = 1024 // parts // 2
    first = start % (parts * lanes) // lanes
    count = 128 // lanes
    row = first_row + start // (parts * lanes) * lanes
    turned = value.T.astype(jnp.bfloat16).reshape(count, lanes, length)
    target[first : first + count, row : row + lanes, :] = turned


def mixed(features, taps, slot, feature, columns):
    own = features[slot, :, columns].astype(jnp.float32)
    row = lax.broadcasted_iota(jnp.int32, own.shape, 0)
    one = jnp.where(row < 1, 0.0, pltpu.roll(own, 1, 0))
    two = jnp.where(row < 2, 0.0, pltpu.roll(own, 2, 0))
    tap = lambda lag: taps[lag, feature : feature + 1, columns]
    return tap(0) * own + tap(1) * one + tap(2) * two


def halo(prior, taps, feature, columns):
    row = lax.broadcasted_iota(jnp.int32, (8, 128), 0)
    before = prior[feature, :, columns].astype(jnp.float32)
    far, near = before[0:1], before[1:2]
    tap = lambda lag: taps[lag, feature : feature + 1, columns]
    first = tap(1) * near + tap(2) * far
    second = tap(2) * near
    return jnp.where(row == 0, first, 0.0) + jnp.where(row == 1, second, 0.0)


def whole_mixed(held, prior, taps, slot, feature, columns):
    value = mixed(held, taps, slot, feature, columns)
    return jnp.concatenate([value[0:8] + halo(prior, taps, feature, columns), value[8:]], axis=0)


def mix_kernel(features, taps, long_filter, prior, send, held, held_taps, held_filter, sems):
    width = held.shape[2]
    lanes = send.shape[1] // 2
    copies = start_all(
        [(long_filter, held_filter), (taps, held_taps), (features.at[1], held.at[0]), (features.at[2], held.at[1])],
        sems,
    )
    copies[0].wait()
    for start in range(0, width, 128):
        store_turned(send, lanes, held_filter[:, start : start + 128], start)
    for copy in copies[1:]:
        copy.wait()
    for start in range(0, width, 128):
        columns = slice(start, start + 128)
        product = whole_mixed(held, prior, held_taps, 0, 1, columns) * whole_mixed(
            held, prior, held_taps, 1, 2, columns
        )
        store_turned(send, 0, product, start)


def table_kernel(token, table, out, sems):
    del token
    start_all([(table, out)], sems)[0].wait()


def stage_kernel(where, token, weight, features, taps, skip, prior, query, direct, chunk, held, held_taps, held_skip, sems):
    del token
    width = query.shape[1]
    copies = start_all([(taps, held_taps), (skip, held_skip), (features, held)], sems)
    pieces = fetch_chunk(weight, where[0], chunk, sems, 3)
    for copy in copies:
        copy.wait()
    for start in range(0, width, 128):
        columns = slice(start, start + 128)
        part = [whole_mixed(held, prior, held_taps, i, i, columns) for i in range(3)]
        query[:, columns] = part[0]
        direct[:, columns] = held_skip[:, columns] * (part[1] * part[2])
    for copy in pieces:
        copy.wait()


def spectrum(received, table, first, inner_ahead, cosine, sine):
    blocks, _, length = received.shape
    size = blocks * GROUP
    group = lambda row: received[:, row : row + GROUP, :].reshape(size, length)
    signal = jnp.concatenate([group(first), group(first + GROUP)], axis=1)
    both = jnp.dot(table[: 2 * size, :], signal, preferred_element_type=jnp.float32)
    result = []
    for columns in (slice(0, length), slice(length, 2 * length)):
        real, imag = both[:size, columns], both[size:, columns]
        turned = jnp.concatenate([real * cosine + imag * sine, imag * cosine - real * sine], axis=1)
        result.append(jnp.dot(turned.astype(jnp.bfloat16), inner_ahead, preferred_element_type=jnp.float32))
    return result


def conv_kernel(table, received, out):
    blocks, rows, length = received.shape
    lanes = rows // 2
    size = blocks * GROUP
    inner_ahead, inner_back, cosine, sine = read_table(table, blocks, length)
    reals, imags = [], []
    signal_parts = spectrum(received, table, 0, inner_ahead, cosine, sine)
    filter_parts = spectrum(received, table, lanes, inner_ahead, cosine, sine)
    for part, other in zip(signal_parts, filter_parts):
        xr, xi = part[:, :length], part[:, length:]
        hr, hi = other[:, :length], other[:, length:]
        joined = jnp.concatenate([xr * hr - xi * hi, xr * hi + xi * hr], axis=1)
        both = jnp.dot(joined.astype(jnp.bfloat16), inner_back, preferred_element_type=jnp.float32)
        real, imag = both[:, :length], both[:, length:]
        reals.append((real * cosine - imag * sine).astype(jnp.bfloat16))
        imags.append((real * sine + imag * cosine).astype(jnp.bfloat16))
    both = jnp.dot(table[2 * size : 3 * size, :], jnp.concatenate(reals, axis=1), preferred_element_type=jnp.float32)
    both += jnp.dot(table[3 * size : 4 * size, :], jnp.concatenate(imags, axis=1), preferred_element_type=jnp.float32)
    for i in range(lanes // GROUP):
        part = both[:, i * length : (i + 1) * length].astype(jnp.bfloat16)
        out[:, i * GROUP : (i + 1) * GROUP, :] = part.reshape(blocks, GROUP, length)


PIECE = 256


def fetch_chunk(weight, index, held, sems, first_sem):
    depth, size = held.shape
    copies = []
    for piece in range(depth // PIECE):
        rows = pl.ds(piece * PIECE, PIECE)
        columns = pl.ds(pl.multiple_of(index * size, size), size)
        copy = pltpu.make_async_copy(weight.at[rows, columns], held.at[rows], sems.at[first_sem + piece])
        copy.start()
        copies.append(copy)
    return copies


def project(gated, held, copies):
    total = None
    for piece, copy in enumerate(copies):
        copy.wait()
        rows = slice(piece * PIECE, (piece + 1) * PIECE)
        part = jnp.dot(gated[:, rows], held[rows, :], preferred_element_type=jnp.float32)
        total = part if total is None else total + part
    return total


def far_kernel(query, direct, chunk, conv, gated_out, first_out, second_out):
    length, width = query.shape
    parts, lanes, _ = conv.shape
    half = lanes // 2
    count = 128 // half
    for start in range(0, width, 128):
        columns = slice(start, start + 128)
        first = start % (parts * half) // half
        row = start // (parts * half) * half
        turned = conv[first : first + count, row : row + half, :].reshape(128, length).astype(jnp.float32).T
        gated_out[:, columns] = (query[:, columns] * (turned + direct[:, columns])).astype(jnp.bfloat16)
    part = jnp.dot(gated_out[...], chunk[...], preferred_element_type=jnp.float32)
    top = length // 2
    first_out[...] = part[:top].astype(jnp.bfloat16)
    second_out[...] = part[top:].astype(jnp.bfloat16)


def near_kernel(where, weight, gated, ahead_held, ahead_out, behind_out, behind_held, held, sems):
    half = ahead_out.shape[0]
    count = held.shape[1] // PIECE
    ahead_pieces = fetch_chunk(weight, where[1], held.at[0], sems, 0)
    behind_pieces = fetch_chunk(weight, where[2], held.at[1], sems, count)
    part = project(gated, held.at[0], ahead_pieces)
    ahead_held[...] = part[:half].astype(jnp.bfloat16)
    ahead_out[...] = part[half:].astype(jnp.bfloat16)
    part = project(gated, held.at[1], behind_pieces)
    behind_out[...] = part[:half].astype(jnp.bfloat16)
    behind_held[...] = part[half:].astype(jnp.bfloat16)


def own_kernel(where, weight, gated, out, held, sems):
    out[...] = project(gated, held, fetch_chunk(weight, where[3], held, sems, 0))


def add_kernel(one, two, out):
    out[...] = (one[...].astype(jnp.float32) + two[...].astype(jnp.float32)).astype(jnp.bfloat16)


def last_kernel(own, first_one, first_two, second_one, second_two, out):
    half = out.shape[0] // 2
    wide = lambda ref: ref[...].astype(jnp.float32)
    out[:half] = (own[:half] + wide(first_one) + wide(first_two)).astype(jnp.bfloat16)
    out[half:] = (own[half:] + wide(second_one) + wide(second_two)).astype(jnp.bfloat16)


def call(kernel, outs, specs, name, scratch=(), out_specs=None, mebibytes=16):
    return pl.pallas_call(
        kernel,
        out_shape=outs,
        in_specs=specs,
        out_specs=jax.tree.map(lambda _: whole(), outs) if out_specs is None else out_specs,
        scratch_shapes=scratch,
        name=name,
        compiler_params=pltpu.CompilerParams(vmem_limit_bytes=mebibytes * 1024 * 1024),
    )


def shards(features, short_taps, skip_gain, long_filter, out_weight):
    length, width = long_filter.shape
    members = lax.axis_size("seq")
    groups = lax.axis_size("chan")
    lanes = width // members
    half = length // 2
    size = out_weight.shape[1] // groups
    bf16, f32 = jnp.bfloat16, jnp.float32
    shape = jax.ShapeDtypeStruct
    away = pl.BlockSpec(memory_space=pltpu.HBM)
    loose = pl.BlockSpec(memory_space=pl.ANY)
    scalar = pl.BlockSpec(memory_space=pltpu.SMEM)
    inside = whole()
    plain = shape((length, width), f32)
    turned_shape = shape((members, lanes, length), bf16)
    vmem = lambda dims, dtype: pltpu.VMEM(dims, dtype)
    flags = lambda count: pltpu.SemaphoreType.DMA((count,))

    prior = lax.ppermute(features[length - 2 :], "seq", [(i, i + 1) for i in range(members - 1)])
    prior = jnp.transpose(prior, (1, 0, 2))
    by_feature = jnp.transpose(features, (1, 0, 2))
    skip = skip_gain[None]
    send = call(
        mix_kernel,
        shape((members, 2 * lanes, length), bf16),
        [away] * 3 + [inside],
        "mix",
        [vmem((2, length, width), bf16), vmem(short_taps.shape, f32), vmem((length, width), f32), flags(4)],
        mebibytes=60,
    )(by_feature, short_taps, long_filter, prior)
    received = lax.all_to_all(send, "seq", 0, 0, tiled=True)
    table = transform_table(members, length)
    table = call(table_kernel, shape(table.shape, bf16), [loose, away], "table", [flags(1)])(send, table)
    spectral = call(conv_kernel, turned_shape, [inside] * 2, "conv")(table, received)
    conv = lax.all_to_all(spectral, "seq", 0, 0, tiled=True)

    side = lax.axis_index("seq") % 2
    me = lax.axis_index("chan")
    step = 1 - 2 * side
    where = jnp.stack([me + 2, me + step, me - step, me]).astype(jnp.int32) % groups

    def route(sign):
        pairs = []
        for s in range(members):
            for c in range(groups):
                move = sign * (1 - 2 * (s % 2))
                pairs.append((s * groups + c, s * groups + (c + move) % groups))
        return pairs

    def ahead(value):
        return lax.ppermute(value, ("seq", "chan"), route(1))

    def behind(value):
        return lax.ppermute(value, ("seq", "chan"), route(-1))

    part = shape((half, size), bf16)
    chunk = vmem((width, size), bf16)
    pieces = width // PIECE
    query, direct, far_chunk = call(
        stage_kernel,
        (plain, plain, shape((width, size), bf16)),
        [scalar, loose] + [away] * 4 + [inside],
        "stage",
        [vmem((3, length, width), bf16), vmem(short_taps.shape, f32), vmem(skip.shape, f32), flags(3 + pieces)],
        mebibytes=48,
    )(where, spectral, out_weight, by_feature, short_taps, skip, prior)
    gated, far_first, far_second = call(
        far_kernel, (shape((length, width), bf16), part, part), [inside] * 4, "far"
    )(query, direct, far_chunk, conv)
    got_first = ahead(far_first)
    got_second = behind(far_second)
    ahead_held, ahead_out, behind_out, behind_held = call(
        near_kernel,
        (part,) * 4,
        [scalar, away, inside],
        "near",
        [vmem((2, width, size), bf16), flags(2 * pieces)],
        mebibytes=48,
    )(where, out_weight, gated)
    ahead_got = ahead(ahead_out)
    behind_got = behind(behind_out)
    own = call(
        own_kernel, shape((length, size), f32), [scalar, away, inside], "own", [chunk, flags(pieces)], mebibytes=48
    )(where, out_weight, gated)
    first_got = ahead(call(add_kernel, part, [inside] * 2, "add_first")(got_first, ahead_held))
    second_got = behind(call(add_kernel, part, [inside] * 2, "add_second")(got_second, behind_held))
    return call(last_kernel, shape((length, size), bf16), [inside] * 5, "last")(
        own, first_got, behind_got, ahead_got, second_got
    )


def solution(mesh):
    in_specs = (
        P("seq", None, "chan"),
        P(None, None, "chan"),
        P("chan"),
        P("seq", "chan"),
        P("chan", None),
    )
    out_specs = P("seq", "chan")
    return jax.shard_map(shards, mesh=mesh, in_specs=in_specs, out_specs=out_specs, check_vma=False)
```

profile of v0, /device:TPU:0, one launch (start us, length us, event | category | flops | bytes accessed | tf_op | source)
XLA Modules:
  0.0 72.8 jit_solution(13192725347912904813)
XLA Ops:
  0.0 0.8 %slice.3 = bf16[2,3,1024]{2,0,1:T(2,128)(2,1)S(1)} slice(bf16[128,3,1024]{2,0,1:T(8,128)(2,1)} %param.6), slice={[126:128], [0:3], [0:1024]} | slice | bytes 24576 | tf_op jit(solution)/shard_map/slice | solution.py:270
  0.8 1.3 %collective-permute-start = (bf16[2,3,1024]{2,0,1:T(2,128)(2,1)S(1)}, bf16[2,3,1024]{2,0,1:T(2,128)(2,1)S(1)}, u32[]{:S(2)}, u32[]{:S(2)}) collective-permute-start(bf16[2,3,1024]{2,0,1:T(2,128)(2,1)S(1)} %slice.3), channel_id=1, source_target_pairs={{0,4},{4,8},{8,12},{12,16},{16,20},{20,24},{24,28},{28,32},{32,36}... | collective-permute-start | bytes 36872 | tf_op jit(solution)/shard_map/ppermute | solution.py:270
  2.1 0.8 %collective-permute-done = bf16[2,3,1024]{2,0,1:T(2,128)(2,1)S(1)} collective-permute-done((bf16[2,3,1024]{2,0,1:T(2,128)(2,1)S(1)}, bf16[2,3,1024]{2,0,1:T(2,128)(2,1)S(1)}, u32[]{:S(2)}, u32[]{:S(2)}) %collective-permute-start) | collective-permute-done | bytes 12320 | tf_op jit(solution)/shard_map/ppermute | solution.py:270
  2.9 0.0 copy-start.5
  2.9 0.6 copy-done.5
  3.5 3.2 %mix.1.token = bf16[32,64,128]{2,1,0:T(8,128)(2,1)} custom-call(bf16[3,128,1024]{2,1,0:T(8,128)(2,1)} %bitcast.7, f32[3,3,1024]{2,1,0:T(4,128)} %taps.3, f32[128,1024]{1,0:T(8,128)} %long_filter.1, bf16[3,2,1024]{2,1,0:T(2,128)(2,1)} %bitcast.9), custom_call_target="tpu_custom_call" | custom-call | tf_op jit(solution)/shard_map/mix/pallas_call | solution.py:274
  6.8 11.5 %all-to-all-start = ((bf16[32,64,128]{2,1,0:T(8,128)(2,1)}), bf16[32,64,128]{2,1,0:T(8,128)(2,1)}, u32[]{:S(2)}, u32[]{:S(2)}) async-start(bf16[32,64,128]{2,1,0:T(8,128)(2,1)} %mix.1.token), calls=%async_computation | async-start | bytes 1048576 | tf_op jit(solution)/shard_map/all_to_all | solution.py:282
  18.2 0.0 copy-start
  18.2 1.1 %copy-done = bf16[32,64,128]{2,1,0:T(8,128)(2,1)S(1)} copy-done((bf16[32,64,128]{2,1,0:T(8,128)(2,1)S(1)}, bf16[32,64,128]{2,1,0:T(8,128)(2,1)}, u32[]{:S(2)}) %copy-start) | copy-done | bytes 524312
  19.3 0.0 copy-start.3
  19.3 1.7 %copy-done.3 = bf16[2336,512]{1,0:T(8,128)(2,1)S(1)} copy-done((bf16[2336,512]{1,0:T(8,128)(2,1)S(1)}, bf16[2336,512]{1,0:T(8,128)(2,1)}, u32[]{:S(2)}) %copy-start.3) | copy-done | bytes 2392088
  21.0 0.0 copy-start.2
  21.0 0.0 copy-start.4
  21.0 0.0 copy-start.6
  21.0 0.0 copy-start.7
  21.0 0.2 table.2
  21.2 8.2 %all-to-all-done.received = bf16[32,64,128]{2,1,0:T(8,128)(2,1)} async-done(((bf16[32,64,128]{2,1,0:T(8,128)(2,1)}), bf16[32,64,128]{2,1,0:T(8,128)(2,1)}, u32[]{:S(2)}, u32[]{:S(2)}) %all-to-all-start) | async-done | bytes 524320 | tf_op jit(solution)/shard_map/all_to_all | solution.py:282
  29.4 4.0 %conv.1.token = bf16[32,32,128]{2,1,0:T(8,128)(2,1)} custom-call(bf16[2336,512]{1,0:T(8,128)(2,1)S(1)} %table.2, bf16[32,64,128]{2,1,0:T(8,128)(2,1)} %all-to-all-done.received), custom_call_target="tpu_custom_call" | custom-call | tf_op jit(solution)/shard_map/conv/pallas_call | solution.py:285
  33.4 4.1 %all-to-all-start.1 = ((bf16[32,32,128]{2,1,0:T(8,128)(2,1)}), bf16[32,32,128]{2,1,0:T(8,128)(2,1)S(1)}, u32[]{:S(2)}, u32[]{:S(2)}) async-start(bf16[32,32,128]{2,1,0:T(8,128)(2,1)} %conv.1.token), calls=%async_computation.1 | async-start | bytes 524288 | tf_op jit(solution)/shard_map/all_to_all | solution.py:286
  37.5 0.1 and_select_fusion.where
  37.6 0.0 copy-done.2
  37.6 0.0 copy-done.4
  37.6 0.0 copy-done.6
  37.6 0.0 copy-done.7
  37.6 4.8 %stage.1 = (f32[128,1024]{1,0:T(8,128)S(1)}, f32[128,1024]{1,0:T(8,128)S(1)}, bf16[1024,2048]{1,0:T(8,128)(2,1)}) custom-call(s32[4]{0:T(128)S(1)} %and_select_fusion.where, bf16[32,32,128]{2,1,0:T(8,128)(2,1)} %conv.1.token, bf16[1024,8192]{1,0:T(8,128)(2,1)} %weight.5, bf16[3,128,1024]{2,1,0:T(8,128)(2,1)S(1)} %bitcast.8, f32[3,3,1024]{2,1,0:T(4,128)S(1)} %copy-done.4, ...), custom_call_target="tpu_custom_call" | custom-call | tf_op jit(solution)/shard_map/stage/pallas_call | solution.py:310
  42.4 4.0 %all-to-all-done.1.conv = bf16[32,32,128]{2,1,0:T(8,128)(2,1)S(1)} async-done(((bf16[32,32,128]{2,1,0:T(8,128)(2,1)}), bf16[32,32,128]{2,1,0:T(8,128)(2,1)S(1)}, u32[]{:S(2)}, u32[]{:S(2)}) %all-to-all-start.1) | async-done | bytes 262176 | tf_op jit(solution)/shard_map/all_to_all | solution.py:286
  46.4 0.0 copy-start.1
  46.4 2.2 %copy-done.1 = bf16[1024,2048]{1,0:T(8,128)(2,1)S(1)} copy-done((bf16[1024,2048]{1,0:T(8,128)(2,1)S(1)}, bf16[1024,2048]{1,0:T(8,128)(2,1)}, u32[]{:S(2)}) %copy-start.1) | copy-done | bytes 4194328
  48.6 0.8 %far.1 = (bf16[128,1024]{1,0:T(8,128)(2,1)S(1)}, bf16[64,2048]{1,0:T(8,128)(2,1)S(1)}, bf16[64,2048]{1,0:T(8,128)(2,1)S(1)}) custom-call(f32[128,1024]{1,0:T(8,128)S(1)} %get-tuple-element.15.query, f32[128,1024]{1,0:T(8,128)S(1)} %get-tuple-element.16.direct, bf16[1024,2048]{1,0:T(8,128)(2,1)S(1)} %copy-done.1, bf16[32,32,128]{2,1,0:T(8,128)(2,1)S(1)} %all-to-all-done.1.conv), custom_call_target="tpu_custom_call" | custom-call | tf_op jit(solution)/shard_map/far/pallas_call | solution.py:318
  49.4 1.6 %collective-permute-start.1 = (bf16[64,2048]{1,0:T(8,128)(2,1)S(1)}, bf16[64,2048]{1,0:T(8,128)(2,1)S(1)}, u32[]{:S(2)}, u32[]{:S(2)}) collective-permute-start(bf16[64,2048]{1,0:T(8,128)(2,1)S(1)} %get-tuple-element.19), channel_id=1, source_target_pairs={{0,1},{1,2},{2,3},{3,0},{4,7},{5,4},{6,5},{7,6},{8,9},{9,10},{10,1... | collective-permute-start | bytes 786440 | tf_op jit(solution)/shard_map/ppermute | solution.py:302
  50.9 1.7 %collective-permute-start.5 = (bf16[64,2048]{1,0:T(8,128)(2,1)S(1)}, bf16[64,2048]{1,0:T(8,128)(2,1)S(1)}, u32[]{:S(2)}, u32[]{:S(2)}) collective-permute-start(bf16[64,2048]{1,0:T(8,128)(2,1)S(1)} %get-tuple-element.23), channel_id=1, source_target_pairs={{0,3},{1,0},{2,1},{3,2},{4,5},{5,6},{6,7},{7,4},{8,11},{9,8},{10,9... | collective-permute-start | bytes 786440 | tf_op jit(solution)/shard_map/ppermute | solution.py:305
  52.7 4.3 %near.1 = (bf16[64,2048]{1,0:T(8,128)(2,1)S(1)}, bf16[64,2048]{1,0:T(8,128)(2,1)S(1)}, bf16[64,2048]{1,0:T(8,128)(2,1)S(1)}, bf16[64,2048]{1,0:T(8,128)(2,1)S(1)}) custom-call(s32[4]{0:T(128)S(1)} %and_select_fusion.where, bf16[1024,8192]{1,0:T(8,128)(2,1)} %weight.5, bf16[128,1024]{1,0:T(8,128)(2,1)S(1)} %get-tuple-element.18.gated), custom_call_target="tpu_custom_call" | custom-call | tf_op jit(solution)/shard_map/near/pallas_call | solution.py:323
  57.0 1.6 %collective-permute-start.3 = (bf16[64,2048]{1,0:T(8,128)(2,1)S(1)}, bf16[64,2048]{1,0:T(8,128)(2,1)S(1)}, u32[]{:S(2)}, u32[]{:S(2)}) collective-permute-start(bf16[64,2048]{1,0:T(8,128)(2,1)S(1)} %get-tuple-element.21), channel_id=1, source_target_pairs={{0,3},{1,0},{2,1},{3,2},{4,5},{5,6},{6,7},{7,4},{8,11},{9,8},{10,9... | collective-permute-start | bytes 786440 | tf_op jit(solution)/shard_map/ppermute | solution.py:305
  58.6 0.5 collective-permute-start.4
  59.1 0.0 collective-permute-done.1.one
  59.1 0.1 add_first.1
  59.2 0.5 collective-permute-start.2
  59.7 0.0 collective-permute-done.5.one
  59.7 0.1 add_second.1
  59.8 2.9 %collective-permute-start.6 = (bf16[64,2048]{1,0:T(8,128)(2,1)S(1)}, bf16[64,2048]{1,0:T(8,128)(2,1)S(1)}, u32[]{:S(2)}, u32[]{:S(2)}) collective-permute-start(bf16[64,2048]{1,0:T(8,128)(2,1)S(1)} %add_second.1), channel_id=1, source_target_pairs={{0,3},{1,0},{2,1},{3,2},{4,5},{5,6},{6,7},{7,4},{8,11},{9,8},{10,9... | collective-permute-start | bytes 786440 | tf_op jit(solution)/shard_map/ppermute | solution.py:305
  62.6 3.1 %own.1 = f32[128,2048]{1,0:T(8,128)S(1)} custom-call(s32[4]{0:T(128)S(1)} %and_select_fusion.where, bf16[1024,8192]{1,0:T(8,128)(2,1)} %weight.5, bf16[128,1024]{1,0:T(8,128)(2,1)S(1)} %get-tuple-element.18.gated), custom_call_target="tpu_custom_call" | custom-call | tf_op jit(solution)/shard_map/own/pallas_call | solution.py:333
  65.7 0.6 collective-permute-done.3.first_two
  66.3 1.2 %collective-permute-done.4.second_one = bf16[64,2048]{1,0:T(8,128)(2,1)S(1)} collective-permute-done((bf16[64,2048]{1,0:T(8,128)(2,1)S(1)}, bf16[64,2048]{1,0:T(8,128)(2,1)S(1)}, u32[]{:S(2)}, u32[]{:S(2)}) %collective-permute-start.4) | collective-permute-done | bytes 262176 | tf_op jit(solution)/shard_map/ppermute | solution.py:302
  67.5 4.4 %collective-permute-done.2.first_one = bf16[64,2048]{1,0:T(8,128)(2,1)S(1)} collective-permute-done((bf16[64,2048]{1,0:T(8,128)(2,1)S(1)}, bf16[64,2048]{1,0:T(8,128)(2,1)S(1)}, u32[]{:S(2)}, u32[]{:S(2)}) %collective-permute-start.2) | collective-permute-done | bytes 262176 | tf_op jit(solution)/shard_map/ppermute | solution.py:302
  71.8 0.0 collective-permute-done.6.second_two
  71.8 1.0 %last.1 = bf16[128,2048]{1,0:T(8,128)(2,1)} custom-call(f32[128,2048]{1,0:T(8,128)S(1)} %own.1, bf16[64,2048]{1,0:T(8,128)(2,1)S(1)} %collective-permute-done.2.first_one, bf16[64,2048]{1,0:T(8,128)(2,1)S(1)} %collective-permute-done.3.first_two, bf16[64,2048]{1,0:T(8,128)(2,1)S(1)} %collective-permute-done.4.second_one, ...), custom_call_target="tpu_custom_call" | custom-call | tf_op jit(solution)/shard_map/last/pallas_call | solution.py:338
Async XLA Ops:
  0.8 2.1 %collective-permute-start = (bf16[2,3,1024]{2,0,1:T(2,128)(2,1)S(1)}, bf16[2,3,1024]{2,0,1:T(2,128)(2,1)S(1)}, u32[]{:S(2)}, u32[]{:S(2)}) collective-permute-start(bf16[2,3,1024]{2,0,1:T(2,128)(2,1)S(1)} %slice.3), channel_id=1, source_target_pairs={{0,4},{4,8},{8,12},{12,16},{16,20},{20,24},{24,28},{28,32},{32,36}... | collective-permute-start | bytes 36872 | tf_op jit(solution)/shard_map/ppermute | solution.py:270
  2.9 0.6 copy-start.5
  6.8 22.6 %all-to-all-start = ((bf16[32,64,128]{2,1,0:T(8,128)(2,1)}), bf16[32,64,128]{2,1,0:T(8,128)(2,1)}, u32[]{:S(2)}, u32[]{:S(2)}) async-start(bf16[32,64,128]{2,1,0:T(8,128)(2,1)} %mix.1.token), calls=%async_computation | async-start | bytes 1048576 | tf_op jit(solution)/shard_map/all_to_all | solution.py:282
  18.2 1.1 %copy-start = (bf16[32,64,128]{2,1,0:T(8,128)(2,1)S(1)}, bf16[32,64,128]{2,1,0:T(8,128)(2,1)}, u32[]{:S(2)}) copy-start(bf16[32,64,128]{2,1,0:T(8,128)(2,1)} %mix.1.token) | copy-start | bytes 1572868
  19.3 1.7 %copy-start.3 = (bf16[2336,512]{1,0:T(8,128)(2,1)S(1)}, bf16[2336,512]{1,0:T(8,128)(2,1)}, u32[]{:S(2)}) copy-start(bf16[2336,512]{1,0:T(8,128)(2,1)} %constant.39.clone.table) | copy-start | bytes 7176196
  21.0 16.6 %copy-start.2 = (bf16[128,3,1024]{2,0,1:T(8,128)(2,1)S(1)}, bf16[128,3,1024]{2,0,1:T(8,128)(2,1)}, u32[]{:S(2)}) copy-start(bf16[128,3,1024]{2,0,1:T(8,128)(2,1)} %param.6) | copy-start | bytes 2359300
  21.0 16.6 %copy-start.4 = (f32[3,3,1024]{2,1,0:T(4,128)S(1)}, f32[3,3,1024]{2,1,0:T(4,128)}, u32[]{:S(2)}) copy-start(f32[3,3,1024]{2,1,0:T(4,128)} %taps.3) | copy-start | bytes 110596
  21.0 16.6 %copy-start.6 = (bf16[2,3,1024]{2,0,1:T(2,128)(2,1)S(1)}, bf16[2,3,1024]{2,0,1:T(2,128)(2,1)}, u32[]{:S(2)}) copy-start(bf16[2,3,1024]{2,0,1:T(2,128)(2,1)} %copy-done.5) | copy-start | bytes 36868
  21.0 16.6 %copy-start.7 = (f32[1024]{0:T(1024)S(1)}, f32[1024]{0:T(1024)}, u32[]{:S(2)}) copy-start(f32[1024]{0:T(1024)} %param.8) | copy-start | bytes 12292
  33.4 13.0 %all-to-all-start.1 = ((bf16[32,32,128]{2,1,0:T(8,128)(2,1)}), bf16[32,32,128]{2,1,0:T(8,128)(2,1)S(1)}, u32[]{:S(2)}, u32[]{:S(2)}) async-start(bf16[32,32,128]{2,1,0:T(8,128)(2,1)} %conv.1.token), calls=%async_computation.1 | async-start | bytes 524288 | tf_op jit(solution)/shard_map/all_to_all | solution.py:286
  46.4 2.2 %copy-start.1 = (bf16[1024,2048]{1,0:T(8,128)(2,1)S(1)}, bf16[1024,2048]{1,0:T(8,128)(2,1)}, u32[]{:S(2)}) copy-start(bf16[1024,2048]{1,0:T(8,128)(2,1)} %get-tuple-element.17.chunk) | copy-start | bytes 12582916
  49.4 9.8 %collective-permute-start.1 = (bf16[64,2048]{1,0:T(8,128)(2,1)S(1)}, bf16[64,2048]{1,0:T(8,128)(2,1)S(1)}, u32[]{:S(2)}, u32[]{:S(2)}) collective-permute-start(bf16[64,2048]{1,0:T(8,128)(2,1)S(1)} %get-tuple-element.19), channel_id=1, source_target_pairs={{0,1},{1,2},{2,3},{3,0},{4,7},{5,4},{6,5},{7,6},{8,9},{9,10},{10,1... | collective-permute-start | bytes 786440 | tf_op jit(solution)/shard_map/ppermute | solution.py:302
  50.9 8.8 %collective-permute-start.5 = (bf16[64,2048]{1,0:T(8,128)(2,1)S(1)}, bf16[64,2048]{1,0:T(8,128)(2,1)S(1)}, u32[]{:S(2)}, u32[]{:S(2)}) collective-permute-start(bf16[64,2048]{1,0:T(8,128)(2,1)S(1)} %get-tuple-element.23), channel_id=1, source_target_pairs={{0,3},{1,0},{2,1},{3,2},{4,5},{5,6},{6,7},{7,4},{8,11},{9,8},{10,9... | collective-permute-start | bytes 786440 | tf_op jit(solution)/shard_map/ppermute | solution.py:305
  57.0 9.3 %collective-permute-start.3 = (bf16[64,2048]{1,0:T(8,128)(2,1)S(1)}, bf16[64,2048]{1,0:T(8,128)(2,1)S(1)}, u32[]{:S(2)}, u32[]{:S(2)}) collective-permute-start(bf16[64,2048]{1,0:T(8,128)(2,1)S(1)} %get-tuple-element.21), channel_id=1, source_target_pairs={{0,3},{1,0},{2,1},{3,2},{4,5},{5,6},{6,7},{7,4},{8,11},{9,8},{10,9... | collective-permute-start | bytes 786440 | tf_op jit(solution)/shard_map/ppermute | solution.py:305
  58.6 8.8 %collective-permute-start.4 = (bf16[64,2048]{1,0:T(8,128)(2,1)S(1)}, bf16[64,2048]{1,0:T(8,128)(2,1)S(1)}, u32[]{:S(2)}, u32[]{:S(2)}) collective-permute-start(bf16[64,2048]{1,0:T(8,128)(2,1)S(1)} %get-tuple-element.22), channel_id=1, source_target_pairs={{0,1},{1,2},{2,3},{3,0},{4,7},{5,4},{6,5},{7,6},{8,9},{9,10},{10,1... | collective-permute-start | bytes 786440 | tf_op jit(solution)/shard_map/ppermute | solution.py:302
  59.2 12.7 %collective-permute-start.2 = (bf16[64,2048]{1,0:T(8,128)(2,1)S(1)}, bf16[64,2048]{1,0:T(8,128)(2,1)S(1)}, u32[]{:S(2)}, u32[]{:S(2)}) collective-permute-start(bf16[64,2048]{1,0:T(8,128)(2,1)S(1)} %add_first.1), channel_id=1, source_target_pairs={{0,1},{1,2},{2,3},{3,0},{4,7},{5,4},{6,5},{7,6},{8,9},{9,10},{10,1... | collective-permute-start | bytes 786440 | tf_op jit(solution)/shard_map/ppermute | solution.py:302
  59.8 12.1 %collective-permute-start.6 = (bf16[64,2048]{1,0:T(8,128)(2,1)S(1)}, bf16[64,2048]{1,0:T(8,128)(2,1)S(1)}, u32[]{:S(2)}, u32[]{:S(2)}) collective-permute-start(bf16[64,2048]{1,0:T(8,128)(2,1)S(1)} %add_second.1), channel_id=1, source_target_pairs={{0,3},{1,0},{2,1},{3,2},{4,5},{5,6},{6,7},{7,4},{8,11},{9,8},{10,9... | collective-permute-start | bytes 786440 | tf_op jit(solution)/shard_map/ppermute | solution.py:305
where the time goes:
time: 73.6 us; the launch traced here: 72.8 us
  starting transfers between devices  25.6 us (35%)
  Pallas kernels  21.6 us (29%)
  waiting for transfers between devices  19.1 us (26%)
  local copies, waits for them, and re-layouts  6.35 us (9%)
    all_to_all x1, starting transfers between devices, shards(): received = lax.all_to_all(send, 'seq', 0, 0, tiled=True)  11.5 us
    all_to_all x1, waiting for transfers between devices, shards(): received = lax.all_to_all(send, 'seq', 0, 0, tiled=True)  8.18 us
    ppermute x3, starting transfers between devices, behind(): return lax.ppermute(value, ('seq', 'chan'), route(-1))  6.22 us
    ppermute x3, waiting for transfers between devices, ahead(): return lax.ppermute(value, ('seq', 'chan'), route(1))  5.55 us
    unnamed x16, local copies, waits for them, and re-layouts  5.54 us
    pallas_call x1, Pallas kernels, shards(): call(stage_kernel, (plain, plain, shape((width, size), bf16)), [scalar, l...  4.85 us
    pallas_call x1, Pallas kernels, shards(): call(near_kernel, (part,) * 4, [scalar, away, inside], 'near', [vmem((2,...  4.34 us
    all_to_all x1, starting transfers between devices, shards(): conv = lax.all_to_all(spectral, 'seq', 0, 0, tiled=True)  4.06 us
  transfers between devices with their start and end apart: 9, of which 6 were waited for; matrix products, arithmetic and copies ran while one was open for 0% of the time, Pallas kernels for 17%

commit v1 on v0

--- a/solution.py
+++ b/solution.py
@@ -9,7 +9,8 @@
 from jax.experimental.pallas import tpu as pltpu
 from jax.sharding import PartitionSpec as P
 
-GROUP = 16
+GROUP = 8
+TILE = 16
 
 
 def whole():
@@ -25,27 +26,29 @@
     back = np.concatenate([np.kron(np.cos(outer).T, eye), np.kron(-np.sin(outer).T, eye)], axis=0) / total
     inner = 2.0 * math.pi * np.outer(np.arange(length), np.arange(length)) / length
     cosine, sine = np.cos(inner), np.sin(inner)
-    inner_ahead = np.concatenate([cosine, -sine, sine, cosine], axis=1)
-    inner_back = np.concatenate([cosine, sine, -sine, cosine], axis=1)
+    inner_ahead = np.block([[cosine, -sine], [sine, cosine]])
+    inner_back = np.block([[cosine, sine], [-sine, cosine]])
     twist = 2.0 * math.pi * k1 * np.arange(length)[None, :] / total
     twist = np.concatenate([np.cos(twist), np.sin(twist)], axis=1).astype(np.float32)
     high = twist.astype(ml_dtypes.bfloat16)
     low = (twist - high.astype(np.float32)).astype(ml_dtypes.bfloat16)
-    parts = [ahead, back, inner_ahead, inner_back, np.concatenate([high, low], axis=1)]
+    parts = [ahead, back, inner_ahead, inner_back, high, low]
     return jnp.asarray(np.concatenate([part.astype(ml_dtypes.bfloat16) for part in parts], axis=0))
 
 
 def read_table(table, blocks, length):
     size = blocks * GROUP
-    at = 4 * size
-    inner_ahead = jnp.concatenate([table[at : at + length, : 2 * length], table[at : at + length, 2 * length :]], axis=0)
-    at += length
-    inner_back = jnp.concatenate([table[at : at + length, : 2 * length], table[at : at + length, 2 * length :]], axis=0)
-    at += length
-    twist = table[at : at + blocks, :].astype(jnp.float32)
-    twist = twist[:, : 2 * length] + twist[:, 2 * length :]
+    at = 4 * size + 4 * length
+    twist = table[at : at + blocks, :].astype(jnp.float32) + table[at + blocks : at + 2 * blocks, :].astype(jnp.float32)
     spread = lambda part: jnp.broadcast_to(part[:, None, :], (blocks, GROUP, length)).reshape(size, length)
-    return inner_ahead, inner_back, spread(twist[:, :length]), spread(twist[:, length:])
+    return (
+        table[: 2 * size, :],
+        (table[2 * size : 3 * size, :], table[3 * size : 4 * size, :]),
+        table[4 * size : 4 * size + 2 * length, :],
+        table[4 * size + 2 * length : at, :],
+        spread(twist[:, :length]),
+        spread(twist[:, length:]),
+    )
 
 
 def start_all(pairs, sems):
@@ -77,7 +80,7 @@
 def halo(prior, taps, feature, columns):
     row = lax.broadcasted_iota(jnp.int32, (8, 128), 0)
     before = prior[feature, :, columns].astype(jnp.float32)
-    far, near = before[0:1], before[1:2]
+    far, near = before[14:15], before[15:16]
     tap = lambda lag: taps[lag, feature : feature + 1, columns]
     first = tap(1) * near + tap(2) * far
     second = tap(2) * near
@@ -89,82 +92,136 @@
     return jnp.concatenate([value[0:8] + halo(prior, taps, feature, columns), value[8:]], axis=0)
 
 
-def mix_kernel(features, taps, long_filter, prior, send, held, held_taps, held_filter, sems):
+def handed_on(held, taps, slot, feature, columns):
+    tail = held[slot, held.shape[1] - 16 :, columns].astype(jnp.float32)[8:]
+    row = lax.broadcasted_iota(jnp.int32, tail.shape, 0)
+    tap = lambda lag: taps[lag, feature : feature + 1, columns]
+    both = tap(1) * jnp.where(row == 0, pltpu.roll(tail, 1, 0), 0.0)
+    return both + tap(2) * jnp.where(row < 2, pltpu.roll(tail, 2, 0), 0.0)
+
+
+def mix_kernel(features, taps, long_filter, send, token, held, held_taps, held_filter, edges, sems):
     width = held.shape[2]
-    lanes = send.shape[1] // 2
+    half = width // 2
+    parts, rows, length = send.shape
+    lanes = 2 * (rows // 5)
     copies = start_all(
         [(long_filter, held_filter), (taps, held_taps), (features.at[1], held.at[0]), (features.at[2], held.at[1])],
         sems,
     )
+    edges[...] = jnp.zeros_like(edges)
+    token[...] = jnp.zeros_like(token)
     copies[0].wait()
     for start in range(0, width, 128):
         store_turned(send, lanes, held_filter[:, start : start + 128], start)
     for copy in copies[1:]:
         copy.wait()
+    row = lax.broadcasted_iota(jnp.int32, (8, 128), 0)
     for start in range(0, width, 128):
         columns = slice(start, start + 128)
-        product = whole_mixed(held, prior, held_taps, 0, 1, columns) * whole_mixed(
-            held, prior, held_taps, 1, 2, columns
+        key = mixed(held, held_taps, 0, 1, columns)
+        value = mixed(held, held_taps, 1, 2, columns)
+        store_turned(send, 0, key * value, start)
+        stack = jnp.where(row < 2, key[0:8], pltpu.roll(value[0:8], 2, 0))
+        later = jnp.where(
+            row < 2,
+            handed_on(held, held_taps, 0, 1, columns),
+            pltpu.roll(handed_on(held, held_taps, 1, 2, columns), 2, 0),
         )
-        store_turned(send, 0, product, start)
-
-
-def table_kernel(token, table, out, sems):
+        stack = jnp.where(row < 4, stack, pltpu.roll(later, 4, 0))
+        top = start // half * 8
+        edges[top : top + 8, start % half : start % half + 128] = stack
+    for start in range(0, half, 128):
+        first = start // (half // parts)
+        count = 128 // (half // parts)
+        turned = edges[:, start : start + 128].T.astype(jnp.bfloat16).reshape(count, half // parts, length)
+        send[first : first + count, 2 * lanes :, :] = turned
+
+
+def tail_kernel(token, table, features, table_out, tail, sems):
     del token
-    start_all([(table, out)], sems)[0].wait()
-
-
-def stage_kernel(where, token, weight, features, taps, skip, prior, query, direct, chunk, held, held_taps, held_skip, sems):
+    rows = tail.shape[1]
+    pairs = [(table, table_out), (features.at[:, pl.ds(features.shape[1] - rows, rows), :], tail)]
+    for copy in start_all(pairs, sems):
+        copy.wait()
+
+
+def terms_kernel(token, features, taps, skip, prior, query, direct, held, held_taps, held_skip, sems):
     del token
     width = query.shape[1]
     copies = start_all([(taps, held_taps), (skip, held_skip), (features, held)], sems)
-    pieces = fetch_chunk(weight, where[0], chunk, sems, 3)
     for copy in copies:
         copy.wait()
     for start in range(0, width, 128):
         columns = slice(start, start + 128)
         part = [whole_mixed(held, prior, held_taps, i, i, columns) for i in range(3)]
-        query[:, columns] = part[0]
-        direct[:, columns] = held_skip[:, columns] * (part[1] * part[2])
-    for copy in pieces:
-        copy.wait()
-
-
-def spectrum(received, table, first, inner_ahead, cosine, sine):
+        query[:, columns] = part[0].astype(jnp.bfloat16)
+        direct[:, columns] = (held_skip[:, columns] * (part[1] * part[2])).astype(jnp.bfloat16)
+
+
+def rows_of(received, row):
     blocks, _, length = received.shape
+    return received[:, row : row + TILE, :].reshape(blocks * TILE, length).astype(jnp.float32)
+
+
+def split_groups(rows, blocks):
+    length = rows.shape[1]
+    rows = rows.reshape(blocks, TILE, length)
+    cut = lambda first: rows[:, first : first + GROUP].reshape(blocks * GROUP, length).astype(jnp.bfloat16)
+    return [cut(first) for first in range(0, TILE, GROUP)]
+
+
+def patched(received, edge_row, index):
+    signal = rows_of(received, index * TILE)
+    edge = rows_of(received, edge_row)
+    length = edge.shape[1]
+    before = jnp.concatenate([jnp.zeros((TILE, length), jnp.float32), edge[:-TILE]], axis=0)
+    joined = pltpu.roll(edge, (length - 8 * index) % length, 1) + pltpu.roll(before, length - 8 * index - 4, 1)
+    whole_edge = joined * pltpu.roll(joined, length - 2, 1)
+    lane = lax.broadcasted_iota(jnp.int32, edge.shape, 1)
+    return jnp.where(lane < 2, whole_edge, signal)
+
+
+def spectrum(groups, ahead, inner_ahead, cosine, sine):
+    size, length = groups[0].shape
+    both = jnp.dot(ahead, jnp.concatenate(groups, axis=1), preferred_element_type=jnp.float32)
+    turned = []
+    for i in range(len(groups)):
+        real, imag = both[:size, i * length : (i + 1) * length], both[size:, i * length : (i + 1) * length]
+        turned.append(jnp.concatenate([real * cosine + imag * sine, imag * cosine - real * sine], axis=1))
+    turned = jnp.concatenate(turned, axis=0).astype(jnp.bfloat16)
+    return jnp.dot(turned, inner_ahead, preferred_element_type=jnp.float32)
+
+
+def conv_kernel(token, table, received, out):
+    del token
+    blocks, lanes, length = out.shape
     size = blocks * GROUP
-    group = lambda row: received[:, row : row + GROUP, :].reshape(size, length)
-    signal = jnp.concatenate([group(first), group(first + GROUP)], axis=1)
-    both = jnp.dot(table[: 2 * size, :], signal, preferred_element_type=jnp.float32)
-    result = []
-    for columns in (slice(0, length), slice(length, 2 * length)):
-        real, imag = both[:size, columns], both[size:, columns]
-        turned = jnp.concatenate([real * cosine + imag * sine, imag * cosine - real * sine], axis=1)
-        result.append(jnp.dot(turned.astype(jnp.bfloat16), inner_ahead, preferred_element_type=jnp.float32))
-    return result
-
-
-def conv_kernel(table, received, out):
-    blocks, rows, length = received.shape
-    lanes = rows // 2
-    size = blocks * GROUP
-    inner_ahead, inner_back, cosine, sine = read_table(table, blocks, length)
+    tiles = lanes // TILE
+    ahead, (back_real, back_imag), inner_ahead, inner_back, cosine, sine = read_table(table, blocks, length)
+    groups = []
+    for i in range(tiles):
+        groups += split_groups(rows_of(received, lanes + i * TILE), blocks)
+    other = spectrum(groups, ahead, inner_ahead, cosine, sine)
+    groups = []
+    for i in range(tiles):
+        groups += split_groups(patched(received, 2 * lanes, i), blocks)
+    part = spectrum(groups, ahead, inner_ahead, cosine, sine)
+    xr, xi, hr, hi = part[:, :length], part[:, length:], other[:, :length], other[:, length:]
+    joined = jnp.concatenate([xr * hr - xi * hi, xr * hi + xi * hr], axis=1)
+    both = jnp.dot(joined.astype(jnp.bfloat16), inner_back, preferred_element_type=jnp.float32)
     reals, imags = [], []
-    signal_parts = spectrum(received, table, 0, inner_ahead, cosine, sine)
-    filter_parts = spectrum(received, table, lanes, inner_ahead, cosine, sine)
-    for part, other in zip(signal_parts, filter_parts):
-        xr, xi = part[:, :length], part[:, length:]
-        hr, hi = other[:, :length], other[:, length:]
-        joined = jnp.concatenate([xr * hr - xi * hi, xr * hi + xi * hr], axis=1)
-        both = jnp.dot(joined.astype(jnp.bfloat16), inner_back, preferred_element_type=jnp.float32)
-        real, imag = both[:, :length], both[:, length:]
+    for i in range(len(groups)):
+        real, imag = both[i * size : (i + 1) * size, :length], both[i * size : (i + 1) * size, length:]
         reals.append((real * cosine - imag * sine).astype(jnp.bfloat16))
         imags.append((real * sine + imag * cosine).astype(jnp.bfloat16))
-    both = jnp.dot(table[2 * size : 3 * size, :], jnp.concatenate(reals, axis=1), preferred_element_type=jnp.float32)
-    both += jnp.dot(table[3 * size : 4 * size, :], jnp.concatenate(imags, axis=1), preferred_element_type=jnp.float32)
-    for i in range(lanes // GROUP):
-        part = both[:, i * length : (i + 1) * length].astype(jnp.bfloat16)
-        out[:, i * GROUP : (i + 1) * GROUP, :] = part.reshape(blocks, GROUP, length)
+    both = jnp.dot(back_real, jnp.concatenate(reals, axis=1), preferred_element_type=jnp.float32)
+    both += jnp.dot(back_imag, jnp.concatenate(imags, axis=1), preferred_element_type=jnp.float32)
+    for i in range(tiles):
+        pair = []
+        for j in range(i * TILE // GROUP, (i + 1) * TILE // GROUP):
+            pair.append(both[:, j * length : (j + 1) * length].reshape(blocks, GROUP, length))
+        out[:, i * TILE : (i + 1) * TILE, :] = jnp.concatenate(pair, axis=1).astype(jnp.bfloat16)
 
 
 PIECE = 256
@@ -192,18 +249,20 @@
     return total
 
 
-def far_kernel(query, direct, chunk, conv, gated_out, first_out, second_out):
+def far_kernel(where, weight, query, direct, conv, gated_out, first_out, second_out, held, sems):
     length, width = query.shape
     parts, lanes, _ = conv.shape
     half = lanes // 2
     count = 128 // half
+    pieces = fetch_chunk(weight, where[0], held, sems, 0)
     for start in range(0, width, 128):
         columns = slice(start, start + 128)
         first = start % (parts * half) // half
         row = start // (parts * half) * half
         turned = conv[first : first + count, row : row + half, :].reshape(128, length).astype(jnp.float32).T
-        gated_out[:, columns] = (query[:, columns] * (turned + direct[:, columns])).astype(jnp.bfloat16)
-    part = jnp.dot(gated_out[...], chunk[...], preferred_element_type=jnp.float32)
+        turned += direct[:, columns].astype(jnp.float32)
+        gated_out[:, columns] = (query[:, columns].astype(jnp.float32) * turned).astype(jnp.bfloat16)
+    part = project(gated_out, held, pieces)
     top = length // 2
     first_out[...] = part[:top].astype(jnp.bfloat16)
     second_out[...] = part[top:].astype(jnp.bfloat16)
@@ -262,27 +321,40 @@
     loose = pl.BlockSpec(memory_space=pl.ANY)
     scalar = pl.BlockSpec(memory_space=pltpu.SMEM)
     inside = whole()
-    plain = shape((length, width), f32)
+    terms = shape((length, width), bf16)
     turned_shape = shape((members, lanes, length), bf16)
     vmem = lambda dims, dtype: pltpu.VMEM(dims, dtype)
     flags = lambda count: pltpu.SemaphoreType.DMA((count,))
 
-    prior = lax.ppermute(features[length - 2 :], "seq", [(i, i + 1) for i in range(members - 1)])
-    prior = jnp.transpose(prior, (1, 0, 2))
     by_feature = jnp.transpose(features, (1, 0, 2))
     skip = skip_gain[None]
-    send = call(
+    sending = shape((members, 2 * lanes + lanes // 2, length), bf16)
+    send, token = call(
         mix_kernel,
-        shape((members, 2 * lanes, length), bf16),
-        [away] * 3 + [inside],
+        (sending, shape((8, 128), f32)),
+        [away] * 3,
         "mix",
-        [vmem((2, length, width), bf16), vmem(short_taps.shape, f32), vmem((length, width), f32), flags(4)],
+        [
+            vmem((2, length, width), bf16),
+            vmem(short_taps.shape, f32),
+            vmem((length, width), f32),
+            vmem((length, width // 2), f32),
+            flags(4),
+        ],
         mebibytes=60,
-    )(by_feature, short_taps, long_filter, prior)
+    )(by_feature, short_taps, long_filter)
     received = lax.all_to_all(send, "seq", 0, 0, tiled=True)
     table = transform_table(members, length)
-    table = call(table_kernel, shape(table.shape, bf16), [loose, away], "table", [flags(1)])(send, table)
-    spectral = call(conv_kernel, turned_shape, [inside] * 2, "conv")(table, received)
+    table, tail = call(
+        tail_kernel,
+        (shape(table.shape, bf16), shape((3, TILE, width), bf16)),
+        [inside, away, away],
+        "tail",
+        [flags(2)],
+        mebibytes=50,
+    )(token, table, by_feature)
+    prior = lax.ppermute(tail, "seq", [(i, i + 1) for i in range(members - 1)])
+    spectral = call(conv_kernel, turned_shape, [loose] + [inside] * 2, "conv")(prior, table, received)
     conv = lax.all_to_all(spectral, "seq", 0, 0, tiled=True)
 
     side = lax.axis_index("seq") % 2
@@ -307,17 +379,22 @@
     part = shape((half, size), bf16)
     chunk = vmem((width, size), bf16)
     pieces = width // PIECE
-    query, direct, far_chunk = call(
-        stage_kernel,
-        (plain, plain, shape((width, size), bf16)),
-        [scalar, loose] + [away] * 4 + [inside],
-        "stage",
-        [vmem((3, length, width), bf16), vmem(short_taps.shape, f32), vmem(skip.shape, f32), flags(3 + pieces)],
-        mebibytes=48,
-    )(where, spectral, out_weight, by_feature, short_taps, skip, prior)
+    query, direct = call(
+        terms_kernel,
+        (terms, terms),
+        [loose] + [away] * 3 + [inside],
+        "terms",
+        [vmem((3, length, width), bf16), vmem(short_taps.shape, f32), vmem(skip.shape, f32), flags(3)],
+        mebibytes=50,
+    )(spectral, by_feature, short_taps, skip, prior)
     gated, far_first, far_second = call(
-        far_kernel, (shape((length, width), bf16), part, part), [inside] * 4, "far"
-    )(query, direct, far_chunk, conv)
+        far_kernel,
+        (shape((length, width), bf16), part, part),
+        [scalar, away] + [inside] * 3,
+        "far",
+        [chunk, flags(pieces)],
+        mebibytes=52,
+    )(where, out_weight, query, direct, conv)
     got_first = ahead(far_first)
     got_second = behind(far_second)
     ahead_held, ahead_out, behind_out, behind_held = call(

time: 73.6 us -> 66.5 us (0.904)
  Pallas kernels: 21.6 us -> 17.2 us
  waiting for transfers between devices: 19.1 us -> 18.1 us
  starting transfers between devices: 25.6 us -> 24.7 us
  local copies, waits for them, and re-layouts: 6.35 us -> 5.58 us
    pallas_call x5, Pallas kernels: 13.1 us -> 8.71 us  [the longest x1 3.12 us: shards(): call(far_kernel, (shape((length, width), bf16), part, part), [scalar, awa...]
    ppermute x3, starting transfers between devices: 6.22 us -> 9.43 us  [behind(): return lax.ppermute(value, ('seq', 'chan'), route(-1))]
    all_to_all x1, starting transfers between devices: 11.5 us -> 8.43 us  [shards(): received = lax.all_to_all(send, 'seq', 0, 0, tiled=True)]
    ppermute x3, starting transfers between devices: 2.55 us -> 0.08 us  [ahead(): return lax.ppermute(value, ('seq', 'chan'), route(1))]
    ppermute x3, waiting for transfers between devices: 5.55 us -> 3.28 us  [ahead(): return lax.ppermute(value, ('seq', 'chan'), route(1))]
    all_to_all x1, waiting for transfers between devices: 8.18 us -> 6.29 us  [shards(): received = lax.all_to_all(send, 'seq', 0, 0, tiled=True)]
    ppermute x3, waiting for transfers between devices: 0.59 us -> 2.17 us  [behind(): return lax.ppermute(value, ('seq', 'chan'), route(-1))]
    all_to_all x1, waiting for transfers between devices: 3.95 us -> 5.46 us  [shards(): conv = lax.all_to_all(spectral, 'seq', 0, 0, tiled=True)]
  transfers between devices with their start and end apart: 9 -> 9, of which waited for: 6 -> 7; matrix products, arithmetic and copies ran while one was open for 0% -> 0% of each run, Pallas kernels for 17% -> 13%
where the time goes in v1:
time: 66.5 us; the launch traced here: 65.8 us
  starting transfers between devices  24.7 us (37%)
  waiting for transfers between devices  18.1 us (27%)
  Pallas kernels  17.2 us (26%)
  local copies, waits for them, and re-layouts  5.58 us (8%)
    ppermute x3, starting transfers between devices, behind(): return lax.ppermute(value, ('seq', 'chan'), route(-1))  9.43 us
    all_to_all x1, starting transfers between devices, shards(): received = lax.all_to_all(send, 'seq', 0, 0, tiled=True)  8.43 us
    all_to_all x1, waiting for transfers between devices, shards(): received = lax.all_to_all(send, 'seq', 0, 0, tiled=True)  6.29 us
    unnamed x12, local copies, waits for them, and re-layouts  5.58 us
    all_to_all x1, waiting for transfers between devices, shards(): conv = lax.all_to_all(spectral, 'seq', 0, 0, tiled=True)  5.46 us
    all_to_all x1, starting transfers between devices, shards(): conv = lax.all_to_all(spectral, 'seq', 0, 0, tiled=True)  4.59 us
    pallas_call x1, Pallas kernels, shards(): call(near_kernel, (part,) * 4, [scalar, away, inside], 'near', [vmem((2,...  4.35 us
    ppermute x3, waiting for transfers between devices, ahead(): return lax.ppermute(value, ('seq', 'chan'), route(1))  3.28 us
  transfers between devices with their start and end apart: 9, of which 7 were waited for; matrix products, arithmetic and copies ran while one was open for 0% of the time, Pallas kernels for 13%

profile of v1, /device:TPU:0, one launch (start us, length us, event | category | flops | bytes accessed | tf_op | source)
XLA Modules:
  0.0 65.8 jit_solution(13791927162039776693)
XLA Ops:
  0.0 2.6 %mix.1 = (bf16[32,80,128]{2,1,0:T(8,128)(2,1)}, f32[8,128]{1,0:T(8,128)}) custom-call(bf16[3,128,1024]{2,1,0:T(8,128)(2,1)} %bitcast.6, f32[3,3,1024]{2,1,0:T(4,128)} %taps.3, f32[128,1024]{1,0:T(8,128)} %long_filter.1), custom_call_target="tpu_custom_call" | custom-call | tf_op jit(solution)/shard_map/mix/pallas_call | solution.py:332
  2.7 8.4 %all-to-all-start = ((bf16[32,80,128]{2,1,0:T(8,128)(2,1)}), bf16[32,80,128]{2,1,0:T(8,128)(2,1)S(1)}, u32[]{:S(2)}, u32[]{:S(2)}) async-start(bf16[32,80,128]{2,1,0:T(8,128)(2,1)} %get-tuple-element.21), calls=%async_computation | async-start | bytes 1310720 | tf_op jit(solution)/shard_map/all_to_all | solution.py:346
  11.1 0.0 copy-start
  11.1 1.1 %copy-done = bf16[128,3,1024]{2,0,1:T(8,128)(2,1)S(1)} copy-done((bf16[128,3,1024]{2,0,1:T(8,128)(2,1)S(1)}, bf16[128,3,1024]{2,0,1:T(8,128)(2,1)}, u32[]{:S(2)}) %copy-start) | copy-done | bytes 786456
  12.2 0.0 copy-start.2
  12.2 1.1 %copy-done.2 = bf16[1600,256]{1,0:T(8,128)(2,1)S(1)} copy-done((bf16[1600,256]{1,0:T(8,128)(2,1)S(1)}, bf16[1600,256]{1,0:T(8,128)(2,1)}, u32[]{:S(2)}) %copy-start.2) | copy-done | bytes 819224
  13.4 0.0 copy-start.5
  13.4 0.7 %copy-done.5 = f32[8,128]{1,0:T(8,128)S(1)} copy-done((f32[8,128]{1,0:T(8,128)S(1)}, f32[8,128]{1,0:T(8,128)}, u32[]{:S(2)}) %copy-start.5) | copy-done | bytes 4120
  14.1 0.2 tail.1
  14.2 2.2 %collective-permute-start = (bf16[3,16,1024]{2,1,0:T(8,128)(2,1)S(1)}, bf16[3,16,1024]{2,1,0:T(8,128)(2,1)S(1)}, u32[]{:S(2)}, u32[]{:S(2)}) collective-permute-start(bf16[3,16,1024]{2,1,0:T(8,128)(2,1)S(1)} %get-tuple-element.19), channel_id=1, source_target_pairs={{0,4},{4,8},{8,12},{12,16},{16,20},{20,24},{24,28},{28,32},{32,36}... | collective-permute-start | bytes 294920 | tf_op jit(solution)/shard_map/ppermute | solution.py:356
  16.4 0.9 %collective-permute-done.token.prior = bf16[3,16,1024]{2,1,0:T(8,128)(2,1)S(1)} collective-permute-done((bf16[3,16,1024]{2,1,0:T(8,128)(2,1)S(1)}, bf16[3,16,1024]{2,1,0:T(8,128)(2,1)S(1)}, u32[]{:S(2)}, u32[]{:S(2)}) %collective-permute-start) | collective-permute-done | bytes 98336 | tf_op jit(solution)/shard_map/ppermute | solution.py:356
  17.3 6.3 %all-to-all-done.received = bf16[32,80,128]{2,1,0:T(8,128)(2,1)S(1)} async-done(((bf16[32,80,128]{2,1,0:T(8,128)(2,1)}), bf16[32,80,128]{2,1,0:T(8,128)(2,1)S(1)}, u32[]{:S(2)}, u32[]{:S(2)}) %all-to-all-start) | async-done | bytes 655392 | tf_op jit(solution)/shard_map/all_to_all | solution.py:346
  23.6 2.0 %conv.1.token = bf16[32,32,128]{2,1,0:T(8,128)(2,1)} custom-call(bf16[3,16,1024]{2,1,0:T(8,128)(2,1)S(1)} %collective-permute-done.token.prior, bf16[1600,256]{1,0:T(8,128)(2,1)S(1)} %get-tuple-element.20.table, bf16[32,80,128]{2,1,0:T(8,128)(2,1)S(1)} %all-to-all-done.received), custom_call_target="tpu_custom_call" | custom-call | tf_op jit(solution)/shard_map/conv/pallas_call | solution.py:357
  25.7 4.6 %all-to-all-start.1 = ((bf16[32,32,128]{2,1,0:T(8,128)(2,1)}), bf16[32,32,128]{2,1,0:T(8,128)(2,1)S(1)}, u32[]{:S(2)}, u32[]{:S(2)}) async-start(bf16[32,32,128]{2,1,0:T(8,128)(2,1)} %conv.1.token), calls=%async_computation.1 | async-start | bytes 524288 | tf_op jit(solution)/shard_map/all_to_all | solution.py:358
  30.3 0.1 and_select_fusion.where
  30.4 0.0 copy-start.1
  30.4 1.1 %copy-done.1 = bf16[128,3,1024]{2,0,1:T(8,128)(2,1)S(1)} copy-done((bf16[128,3,1024]{2,0,1:T(8,128)(2,1)S(1)}, bf16[128,3,1024]{2,0,1:T(8,128)(2,1)}, u32[]{:S(2)}) %copy-start.1) | copy-done | bytes 786456
  31.5 0.0 copy-start.3
  31.5 0.8 %copy-done.3 = f32[3,3,1024]{2,1,0:T(4,128)S(1)} copy-done((f32[3,3,1024]{2,1,0:T(4,128)S(1)}, f32[3,3,1024]{2,1,0:T(4,128)}, u32[]{:S(2)}) %copy-start.3) | copy-done | bytes 36888
  32.3 0.0 copy-start.4
  32.3 0.7 %copy-done.4 = f32[1024]{0:T(1024)S(1)} copy-done((f32[1024]{0:T(1024)S(1)}, f32[1024]{0:T(1024)}, u32[]{:S(2)}) %copy-start.4) | copy-done | bytes 4120
  33.0 0.8 %terms.1 = (bf16[128,1024]{1,0:T(8,128)(2,1)S(1)}, bf16[128,1024]{1,0:T(8,128)(2,1)S(1)}) custom-call(bf16[32,32,128]{2,1,0:T(8,128)(2,1)} %conv.1.token, bf16[3,128,1024]{2,1,0:T(8,128)(2,1)S(1)} %bitcast.8, f32[3,3,1024]{2,1,0:T(4,128)S(1)} %copy-done.3, f32[1,1024]{1,0:T(1,128)S(1)} %bitcast.9, bf16[3,16,1024]{2,1,0:T(8,128)(2,1)S(1)} %collective-permute-done.token.prior), custom_call_target="tpu_custom_call" | custom-call | tf_op jit(solution)/shard_map/terms/pallas_call | solution.py:382
  33.7 5.5 %all-to-all-done.1.conv = bf16[32,32,128]{2,1,0:T(8,128)(2,1)S(1)} async-done(((bf16[32,32,128]{2,1,0:T(8,128)(2,1)}), bf16[32,32,128]{2,1,0:T(8,128)(2,1)S(1)}, u32[]{:S(2)}, u32[]{:S(2)}) %all-to-all-start.1) | async-done | bytes 262176 | tf_op jit(solution)/shard_map/all_to_all | solution.py:358
  39.2 3.1 %far.1 = (bf16[128,1024]{1,0:T(8,128)(2,1)S(1)}, bf16[64,2048]{1,0:T(8,128)(2,1)S(1)}, bf16[64,2048]{1,0:T(8,128)(2,1)S(1)}) custom-call(s32[4]{0:T(128)S(1)} %and_select_fusion.where, bf16[1024,8192]{1,0:T(8,128)(2,1)} %weight.5, bf16[128,1024]{1,0:T(8,128)(2,1)S(1)} %get-tuple-element.22.query, bf16[128,1024]{1,0:T(8,128)(2,1)S(1)} %get-tuple-element.23.direct, ...), custom_call_target="tpu_custom_call" | custom-call | tf_op jit(solution)/shard_map/far/pallas_call | solution.py:390
  42.3 2.8 %collective-permute-start.5 = (bf16[64,2048]{1,0:T(8,128)(2,1)S(1)}, bf16[64,2048]{1,0:T(8,128)(2,1)S(1)}, u32[]{:S(2)}, u32[]{:S(2)}) collective-permute-start(bf16[64,2048]{1,0:T(8,128)(2,1)S(1)} %get-tuple-element.29), channel_id=1, source_target_pairs={{0,3},{1,0},{2,1},{3,2},{4,5},{5,6},{6,7},{7,4},{8,11},{9,8},{10,9... | collective-permute-start | bytes 786440 | tf_op jit(solution)/shard_map/ppermute | solution.py:377
  45.2 0.0 collective-permute-start.1
  45.2 4.3 %near.1 = (bf16[64,2048]{1,0:T(8,128)(2,1)S(1)}, bf16[64,2048]{1,0:T(8,128)(2,1)S(1)}, bf16[64,2048]{1,0:T(8,128)(2,1)S(1)}, bf16[64,2048]{1,0:T(8,128)(2,1)S(1)}) custom-call(s32[4]{0:T(128)S(1)} %and_select_fusion.where, bf16[1024,8192]{1,0:T(8,128)(2,1)} %weight.5, bf16[128,1024]{1,0:T(8,128)(2,1)S(1)} %get-tuple-element.24.gated), custom_call_target="tpu_custom_call" | custom-call | tf_op jit(solution)/shard_map/near/pallas_call | solution.py:400
  49.5 3.3 %collective-permute-start.3 = (bf16[64,2048]{1,0:T(8,128)(2,1)S(1)}, bf16[64,2048]{1,0:T(8,128)(2,1)S(1)}, u32[]{:S(2)}, u32[]{:S(2)}) collective-permute-start(bf16[64,2048]{1,0:T(8,128)(2,1)S(1)} %get-tuple-element.27), channel_id=1, source_target_pairs={{0,3},{1,0},{2,1},{3,2},{4,5},{5,6},{6,7},{7,4},{8,11},{9,8},{10,9... | collective-permute-start | bytes 786440 | tf_op jit(solution)/shard_map/ppermute | solution.py:377
  52.8 0.0 collective-permute-start.4
  52.8 0.0 collective-permute-done.5.one
  52.8 0.1 add_second.1
  52.9 3.3 %collective-permute-start.6 = (bf16[64,2048]{1,0:T(8,128)(2,1)S(1)}, bf16[64,2048]{1,0:T(8,128)(2,1)S(1)}, u32[]{:S(2)}, u32[]{:S(2)}) collective-permute-start(bf16[64,2048]{1,0:T(8,128)(2,1)S(1)} %add_second.1), channel_id=1, source_target_pairs={{0,3},{1,0},{2,1},{3,2},{4,5},{5,6},{6,7},{7,4},{8,11},{9,8},{10,9... | collective-permute-start | bytes 786440 | tf_op jit(solution)/shard_map/ppermute | solution.py:377
  56.2 0.0 collective-permute-done.1.one
  56.2 0.1 add_first.1
  56.3 0.1 collective-permute-start.2
  56.3 3.1 %own.1 = f32[128,2048]{1,0:T(8,128)S(1)} custom-call(s32[4]{0:T(128)S(1)} %and_select_fusion.where, bf16[1024,8192]{1,0:T(8,128)(2,1)} %weight.5, bf16[128,1024]{1,0:T(8,128)(2,1)S(1)} %get-tuple-element.24.gated), custom_call_target="tpu_custom_call" | custom-call | tf_op jit(solution)/shard_map/own/pallas_call | solution.py:410
  59.4 0.1 collective-permute-done.3.first_two
  59.5 2.5 %collective-permute-done.4.second_one = bf16[64,2048]{1,0:T(8,128)(2,1)S(1)} collective-permute-done((bf16[64,2048]{1,0:T(8,128)(2,1)S(1)}, bf16[64,2048]{1,0:T(8,128)(2,1)S(1)}, u32[]{:S(2)}, u32[]{:S(2)}) %collective-permute-start.4) | collective-permute-done | bytes 262176 | tf_op jit(solution)/shard_map/ppermute | solution.py:374
  62.0 2.1 %collective-permute-done.6.second_two = bf16[64,2048]{1,0:T(8,128)(2,1)S(1)} collective-permute-done((bf16[64,2048]{1,0:T(8,128)(2,1)S(1)}, bf16[64,2048]{1,0:T(8,128)(2,1)S(1)}, u32[]{:S(2)}, u32[]{:S(2)}) %collective-permute-start.6) | collective-permute-done | bytes 262176 | tf_op jit(solution)/shard_map/ppermute | solution.py:377
  64.1 0.7 %collective-permute-done.2.first_one = bf16[64,2048]{1,0:T(8,128)(2,1)S(1)} collective-permute-done((bf16[64,2048]{1,0:T(8,128)(2,1)S(1)}, bf16[64,2048]{1,0:T(8,128)(2,1)S(1)}, u32[]{:S(2)}, u32[]{:S(2)}) %collective-permute-start.2) | collective-permute-done | bytes 262176 | tf_op jit(solution)/shard_map/ppermute | solution.py:374
  64.9 0.9 %last.1 = bf16[128,2048]{1,0:T(8,128)(2,1)} custom-call(f32[128,2048]{1,0:T(8,128)S(1)} %own.1, bf16[64,2048]{1,0:T(8,128)(2,1)S(1)} %collective-permute-done.2.first_one, bf16[64,2048]{1,0:T(8,128)(2,1)S(1)} %collective-permute-done.3.first_two, bf16[64,2048]{1,0:T(8,128)(2,1)S(1)} %collective-permute-done.4.second_one, ...), custom_call_target="tpu_custom_call" | custom-call | tf_op jit(solution)/shard_map/last/pallas_call | solution.py:415
Async XLA Ops:
  2.7 21.0 %all-to-all-start = ((bf16[32,80,128]{2,1,0:T(8,128)(2,1)}), bf16[32,80,128]{2,1,0:T(8,128)(2,1)S(1)}, u32[]{:S(2)}, u32[]{:S(2)}) async-start(bf16[32,80,128]{2,1,0:T(8,128)(2,1)} %get-tuple-element.21), calls=%async_computation | async-start | bytes 1310720 | tf_op jit(solution)/shard_map/all_to_all | solution.py:346
  11.1 1.1 %copy-start = (bf16[128,3,1024]{2,0,1:T(8,128)(2,1)S(1)}, bf16[128,3,1024]{2,0,1:T(8,128)(2,1)}, u32[]{:S(2)}) copy-start(bf16[128,3,1024]{2,0,1:T(8,128)(2,1)} %param.6) | copy-start | bytes 2359300
  12.2 1.1 %copy-start.2 = (bf16[1600,256]{1,0:T(8,128)(2,1)S(1)}, bf16[1600,256]{1,0:T(8,128)(2,1)}, u32[]{:S(2)}) copy-start(bf16[1600,256]{1,0:T(8,128)(2,1)} %constant.39.clone.table) | copy-start | bytes 2457604
  13.4 0.7 %copy-start.5 = (f32[8,128]{1,0:T(8,128)S(1)}, f32[8,128]{1,0:T(8,128)}, u32[]{:S(2)}) copy-start(f32[8,128]{1,0:T(8,128)} %get-tuple-element.18.token) | copy-start | bytes 12292
  14.2 3.1 %collective-permute-start = (bf16[3,16,1024]{2,1,0:T(8,128)(2,1)S(1)}, bf16[3,16,1024]{2,1,0:T(8,128)(2,1)S(1)}, u32[]{:S(2)}, u32[]{:S(2)}) collective-permute-start(bf16[3,16,1024]{2,1,0:T(8,128)(2,1)S(1)} %get-tuple-element.19), channel_id=1, source_target_pairs={{0,4},{4,8},{8,12},{12,16},{16,20},{20,24},{24,28},{28,32},{32,36}... | collective-permute-start | bytes 294920 | tf_op jit(solution)/shard_map/ppermute | solution.py:356
  25.7 13.5 %all-to-all-start.1 = ((bf16[32,32,128]{2,1,0:T(8,128)(2,1)}), bf16[32,32,128]{2,1,0:T(8,128)(2,1)S(1)}, u32[]{:S(2)}, u32[]{:S(2)}) async-start(bf16[32,32,128]{2,1,0:T(8,128)(2,1)} %conv.1.token), calls=%async_computation.1 | async-start | bytes 524288 | tf_op jit(solution)/shard_map/all_to_all | solution.py:358
  30.4 1.1 %copy-start.1 = (bf16[128,3,1024]{2,0,1:T(8,128)(2,1)S(1)}, bf16[128,3,1024]{2,0,1:T(8,128)(2,1)}, u32[]{:S(2)}) copy-start(bf16[128,3,1024]{2,0,1:T(8,128)(2,1)} %param.6) | copy-start | bytes 2359300
  31.5 0.8 %copy-start.3 = (f32[3,3,1024]{2,1,0:T(4,128)S(1)}, f32[3,3,1024]{2,1,0:T(4,128)}, u32[]{:S(2)}) copy-start(f32[3,3,1024]{2,1,0:T(4,128)} %taps.3) | copy-start | bytes 110596
  32.3 0.7 %copy-start.4 = (f32[1024]{0:T(1024)S(1)}, f32[1024]{0:T(1024)}, u32[]{:S(2)}) copy-start(f32[1024]{0:T(1024)} %param.8) | copy-start | bytes 12292
  42.3 10.5 %collective-permute-start.5 = (bf16[64,2048]{1,0:T(8,128)(2,1)S(1)}, bf16[64,2048]{1,0:T(8,128)(2,1)S(1)}, u32[]{:S(2)}, u32[]{:S(2)}) collective-permute-start(bf16[64,2048]{1,0:T(8,128)(2,1)S(1)} %get-tuple-element.29), channel_id=1, source_target_pairs={{0,3},{1,0},{2,1},{3,2},{4,5},{5,6},{6,7},{7,4},{8,11},{9,8},{10,9... | collective-permute-start | bytes 786440 | tf_op jit(solution)/shard_map/ppermute | solution.py:377
  45.2 11.0 %collective-permute-start.1 = (bf16[64,2048]{1,0:T(8,128)(2,1)S(1)}, bf16[64,2048]{1,0:T(8,128)(2,1)S(1)}, u32[]{:S(2)}, u32[]{:S(2)}) collective-permute-start(bf16[64,2048]{1,0:T(8,128)(2,1)S(1)} %get-tuple-element.25), channel_id=1, source_target_pairs={{0,1},{1,2},{2,3},{3,0},{4,7},{5,4},{6,5},{7,6},{8,9},{9,10},{10,1... | collective-permute-start | bytes 786440 | tf_op jit(solution)/shard_map/ppermute | solution.py:374
  49.5 10.0 %collective-permute-start.3 = (bf16[64,2048]{1,0:T(8,128)(2,1)S(1)}, bf16[64,2048]{1,0:T(8,128)(2,1)S(1)}, u32[]{:S(2)}, u32[]{:S(2)}) collective-permute-start(bf16[64,2048]{1,0:T(8,128)(2,1)S(1)} %get-tuple-element.27), channel_id=1, source_target_pairs={{0,3},{1,0},{2,1},{3,2},{4,5},{5,6},{6,7},{7,4},{8,11},{9,8},{10,9... | collective-permute-start | bytes 786440 | tf_op jit(solution)/shard_map/ppermute | solution.py:377
  52.8 9.2 %collective-permute-start.4 = (bf16[64,2048]{1,0:T(8,128)(2,1)S(1)}, bf16[64,2048]{1,0:T(8,128)(2,1)S(1)}, u32[]{:S(2)}, u32[]{:S(2)}) collective-permute-start(bf16[64,2048]{1,0:T(8,128)(2,1)S(1)} %get-tuple-element.28), channel_id=1, source_target_pairs={{0,1},{1,2},{2,3},{3,0},{4,7},{5,4},{6,5},{7,6},{8,9},{9,10},{10,1... | collective-permute-start | bytes 786440 | tf_op jit(solution)/shard_map/ppermute | solution.py:374
  52.9 11.2 %collective-permute-start.6 = (bf16[64,2048]{1,0:T(8,128)(2,1)S(1)}, bf16[64,2048]{1,0:T(8,128)(2,1)S(1)}, u32[]{:S(2)}, u32[]{:S(2)}) collective-permute-start(bf16[64,2048]{1,0:T(8,128)(2,1)S(1)} %add_second.1), channel_id=1, source_target_pairs={{0,3},{1,0},{2,1},{3,2},{4,5},{5,6},{6,7},{7,4},{8,11},{9,8},{10,9... | collective-permute-start | bytes 786440 | tf_op jit(solution)/shard_map/ppermute | solution.py:377
  56.3 8.6 %collective-permute-start.2 = (bf16[64,2048]{1,0:T(8,128)(2,1)S(1)}, bf16[64,2048]{1,0:T(8,128)(2,1)S(1)}, u32[]{:S(2)}, u32[]{:S(2)}) collective-permute-start(bf16[64,2048]{1,0:T(8,128)(2,1)S(1)} %add_first.1), channel_id=1, source_target_pairs={{0,1},{1,2},{2,3},{3,0},{4,7},{5,4},{6,5},{7,6},{8,9},{9,10},{10,1... | collective-permute-start | bytes 786440 | tf_op jit(solution)/shard_map/ppermute | solution.py:374

commit v2 on v1

--- a/solution.py
+++ b/solution.py
@@ -60,12 +60,10 @@
 
 def store_turned(target, first_row, value, start):
     parts, _, length = target.shape
-    lanes = 1024 // parts // 2
-    first = start % (parts * lanes) // lanes
-    count = 128 // lanes
-    row = first_row + start // (parts * lanes) * lanes
-    turned = value.T.astype(jnp.bfloat16).reshape(count, lanes, length)
-    target[first : first + count, row : row + lanes, :] = turned
+    first = start % (parts * GROUP) // GROUP
+    row = first_row + start // (parts * GROUP) * GROUP
+    turned = value.T.reshape(128 // GROUP, GROUP, length).astype(jnp.bfloat16)
+    target[first : first + 128 // GROUP, row : row + GROUP, :] = turned
 
 
 def mixed(features, taps, slot, feature, columns):
@@ -80,7 +78,7 @@
 def halo(prior, taps, feature, columns):
     row = lax.broadcasted_iota(jnp.int32, (8, 128), 0)
     before = prior[feature, :, columns].astype(jnp.float32)
-    far, near = before[14:15], before[15:16]
+    far, near = before[0:1], before[1:2]
     tap = lambda lag: taps[lag, feature : feature + 1, columns]
     first = tap(1) * near + tap(2) * far
     second = tap(2) * near
@@ -102,9 +100,9 @@
 
 def mix_kernel(features, taps, long_filter, send, token, held, held_taps, held_filter, edges, sems):
     width = held.shape[2]
-    half = width // 2
-    parts, rows, length = send.shape
-    lanes = 2 * (rows // 5)
+    parts = send.shape[0]
+    lanes = width // parts
+    quarter = parts * GROUP
     copies = start_all(
         [(long_filter, held_filter), (taps, held_taps), (features.at[1], held.at[0]), (features.at[2], held.at[1])],
         sems,
@@ -113,7 +111,7 @@
     token[...] = jnp.zeros_like(token)
     copies[0].wait()
     for start in range(0, width, 128):
-        store_turned(send, lanes, held_filter[:, start : start + 128], start)
+        store_turned(send, 0, held_filter[:, start : start + 128], start)
     for copy in copies[1:]:
         copy.wait()
     row = lax.broadcasted_iota(jnp.int32, (8, 128), 0)
@@ -121,7 +119,7 @@
         columns = slice(start, start + 128)
         key = mixed(held, held_taps, 0, 1, columns)
         value = mixed(held, held_taps, 1, 2, columns)
-        store_turned(send, 0, key * value, start)
+        store_turned(send, lanes, key * value, start)
         stack = jnp.where(row < 2, key[0:8], pltpu.roll(value[0:8], 2, 0))
         later = jnp.where(
             row < 2,
@@ -129,21 +127,19 @@
             pltpu.roll(handed_on(held, held_taps, 1, 2, columns), 2, 0),
         )
         stack = jnp.where(row < 4, stack, pltpu.roll(later, 4, 0))
-        top = start // half * 8
-        edges[top : top + 8, start % half : start % half + 128] = stack
-    for start in range(0, half, 128):
-        first = start // (half // parts)
-        count = 128 // (half // parts)
-        turned = edges[:, start : start + 128].T.astype(jnp.bfloat16).reshape(count, half // parts, length)
-        send[first : first + count, 2 * lanes :, :] = turned
-
-
-def tail_kernel(token, table, features, table_out, tail, sems):
+        top = start // quarter * 8
+        edges[top : top + 8, start % quarter : start % quarter + 128] = stack
+    for start in range(0, quarter, 128):
+        store_turned(send, 2 * lanes, edges[:, start : start + 128], start)
+
+
+def tail_kernel(token, table, features, table_out, tail, held, sems):
     del token
-    rows = tail.shape[1]
-    pairs = [(table, table_out), (features.at[:, pl.ds(features.shape[1] - rows, rows), :], tail)]
+    rows = held.shape[1]
+    pairs = [(table, table_out), (features.at[:, pl.ds(features.shape[1] - rows, rows), :], held)]
     for copy in start_all(pairs, sems):
         copy.wait()
+    tail[...] = held[:, rows - tail.shape[1] :, :]
 
 
 def terms_kernel(token, features, taps, skip, prior, query, direct, held, held_taps, held_skip, sems):
@@ -161,21 +157,12 @@
 
 def rows_of(received, row):
     blocks, _, length = received.shape
-    return received[:, row : row + TILE, :].reshape(blocks * TILE, length).astype(jnp.float32)
-
-
-def split_groups(rows, blocks):
-    length = rows.shape[1]
-    rows = rows.reshape(blocks, TILE, length)
-    cut = lambda first: rows[:, first : first + GROUP].reshape(blocks * GROUP, length).astype(jnp.bfloat16)
-    return [cut(first) for first in range(0, TILE, GROUP)]
-
-
-def patched(received, edge_row, index):
-    signal = rows_of(received, index * TILE)
-    edge = rows_of(received, edge_row)
+    return received[:, row : row + GROUP, :].astype(jnp.float32).reshape(blocks * GROUP, length)
+
+
+def patched(signal, edge, index):
     length = edge.shape[1]
-    before = jnp.concatenate([jnp.zeros((TILE, length), jnp.float32), edge[:-TILE]], axis=0)
+    before = jnp.concatenate([jnp.zeros((GROUP, length), jnp.float32), edge[:-GROUP]], axis=0)
     joined = pltpu.roll(edge, (length - 8 * index) % length, 1) + pltpu.roll(before, length - 8 * index - 4, 1)
     whole_edge = joined * pltpu.roll(joined, length - 2, 1)
     lane = lax.broadcasted_iota(jnp.int32, edge.shape, 1)
@@ -197,15 +184,12 @@
     del token
     blocks, lanes, length = out.shape
     size = blocks * GROUP
-    tiles = lanes // TILE
+    count = lanes // GROUP
     ahead, (back_real, back_imag), inner_ahead, inner_back, cosine, sine = read_table(table, blocks, length)
-    groups = []
-    for i in range(tiles):
-        groups += split_groups(rows_of(received, lanes + i * TILE), blocks)
+    groups = [rows_of(received, i * GROUP).astype(jnp.bfloat16) for i in range(count)]
     other = spectrum(groups, ahead, inner_ahead, cosine, sine)
-    groups = []
-    for i in range(tiles):
-        groups += split_groups(patched(received, 2 * lanes, i), blocks)
+    edge = rows_of(received, 2 * lanes)
+    groups = [patched(rows_of(received, lanes + i * GROUP), edge, i).astype(jnp.bfloat16) for i in range(count)]
     part = spectrum(groups, ahead, inner_ahead, cosine, sine)
     xr, xi, hr, hi = part[:, :length], part[:, length:], other[:, :length], other[:, length:]
     joined = jnp.concatenate([xr * hr - xi * hi, xr * hi + xi * hr], axis=1)
@@ -217,14 +201,17 @@
         imags.append((real * sine + imag * cosine).astype(jnp.bfloat16))
     both = jnp.dot(back_real, jnp.concatenate(reals, axis=1), preferred_element_type=jnp.float32)
     both += jnp.dot(back_imag, jnp.concatenate(imags, axis=1), preferred_element_type=jnp.float32)
-    for i in range(tiles):
-        pair = []
-        for j in range(i * TILE // GROUP, (i + 1) * TILE // GROUP):
-            pair.append(both[:, j * length : (j + 1) * length].reshape(blocks, GROUP, length))
-        out[:, i * TILE : (i + 1) * TILE, :] = jnp.concatenate(pair, axis=1).astype(jnp.bfloat16)
+    for i in range(count):
+        part = both[:, i * length : (i + 1) * length].reshape(blocks, GROUP, length)
+        out[:, i * GROUP : (i + 1) * GROUP, :] = part.astype(jnp.bfloat16)
 
 
 PIECE = 256
+
+
+def chunk_index(kind, groups):
+    step = 1 - 2 * (lax.axis_index("seq") % 2)
+    return (lax.axis_index("chan") + (2, step, groups - step, 0)[kind]) % groups
 
 
 def fetch_chunk(weight, index, held, sems, first_sem):
@@ -249,17 +236,17 @@
     return total
 
 
-def far_kernel(where, weight, query, direct, conv, gated_out, first_out, second_out, held, sems):
+def far_kernel(weight, query, direct, conv, gated_out, first_out, second_out, held, sems):
+    size = held.shape[1]
     length, width = query.shape
-    parts, lanes, _ = conv.shape
-    half = lanes // 2
-    count = 128 // half
-    pieces = fetch_chunk(weight, where[0], held, sems, 0)
+    quarter = conv.shape[0] * GROUP
+    pieces = fetch_chunk(weight, chunk_index(0, weight.shape[1] // size), held, sems, 0)
     for start in range(0, width, 128):
         columns = slice(start, start + 128)
-        first = start % (parts * half) // half
-        row = start // (parts * half) * half
-        turned = conv[first : first + count, row : row + half, :].reshape(128, length).astype(jnp.float32).T
+        first = start % quarter // GROUP
+        row = start // quarter * GROUP
+        turned = conv[first : first + 128 // GROUP, row : row + GROUP, :].astype(jnp.float32)
+        turned = turned.reshape(128, length).T
         turned += direct[:, columns].astype(jnp.float32)
         gated_out[:, columns] = (query[:, columns].astype(jnp.float32) * turned).astype(jnp.bfloat16)
     part = project(gated_out, held, pieces)
@@ -268,11 +255,11 @@
     second_out[...] = part[top:].astype(jnp.bfloat16)
 
 
-def near_kernel(where, weight, gated, ahead_held, ahead_out, behind_out, behind_held, held, sems):
-    half = ahead_out.shape[0]
+def near_kernel(weight, gated, ahead_held, ahead_out, behind_out, behind_held, held, sems):
+    half, size = ahead_out.shape
     count = held.shape[1] // PIECE
-    ahead_pieces = fetch_chunk(weight, where[1], held.at[0], sems, 0)
-    behind_pieces = fetch_chunk(weight, where[2], held.at[1], sems, count)
+    ahead_pieces = fetch_chunk(weight, chunk_index(1, weight.shape[1] // size), held.at[0], sems, 0)
+    behind_pieces = fetch_chunk(weight, chunk_index(2, weight.shape[1] // size), held.at[1], sems, count)
     part = project(gated, held.at[0], ahead_pieces)
     ahead_held[...] = part[:half].astype(jnp.bfloat16)
     ahead_out[...] = part[half:].astype(jnp.bfloat16)
@@ -281,8 +268,9 @@
     behind_held[...] = part[half:].astype(jnp.bfloat16)
 
 
-def own_kernel(where, weight, gated, out, held, sems):
-    out[...] = project(gated, held, fetch_chunk(weight, where[3], held, sems, 0))
+def own_kernel(weight, gated, out, held, sems):
+    size = held.shape[1]
+    out[...] = project(gated, held, fetch_chunk(weight, chunk_index(3, weight.shape[1] // size), held, sems, 0))
 
 
 def add_kernel(one, two, out):
@@ -319,7 +307,6 @@
     shape = jax.ShapeDtypeStruct
     away = pl.BlockSpec(memory_space=pltpu.HBM)
     loose = pl.BlockSpec(memory_space=pl.ANY)
-    scalar = pl.BlockSpec(memory_space=pltpu.SMEM)
     inside = whole()
     terms = shape((length, width), bf16)
     turned_shape = shape((members, lanes, length), bf16)
@@ -328,7 +315,7 @@
 
     by_feature = jnp.transpose(features, (1, 0, 2))
     skip = skip_gain[None]
-    sending = shape((members, 2 * lanes + lanes // 2, length), bf16)
+    sending = shape((members, 2 * lanes + GROUP, length), bf16)
     send, token = call(
         mix_kernel,
         (sending, shape((8, 128), f32)),
@@ -338,7 +325,7 @@
             vmem((2, length, width), bf16),
             vmem(short_taps.shape, f32),
             vmem((length, width), f32),
-            vmem((length, width // 2), f32),
+            vmem((length, members * GROUP), f32),
             flags(4),
         ],
         mebibytes=60,
@@ -347,20 +334,15 @@
     table = transform_table(members, length)
     table, tail = call(
         tail_kernel,
-        (shape(table.shape, bf16), shape((3, TILE, width), bf16)),
+        (shape(table.shape, bf16), shape((3, 2, width), bf16)),
         [inside, away, away],
         "tail",
-        [flags(2)],
+        [vmem((3, TILE, width), bf16), flags(2)],
         mebibytes=50,
     )(token, table, by_feature)
     prior = lax.ppermute(tail, "seq", [(i, i + 1) for i in range(members - 1)])
     spectral = call(conv_kernel, turned_shape, [loose] + [inside] * 2, "conv")(prior, table, received)
     conv = lax.all_to_all(spectral, "seq", 0, 0, tiled=True)
-
-    side = lax.axis_index("seq") % 2
-    me = lax.axis_index("chan")
-    step = 1 - 2 * side
-    where = jnp.stack([me + 2, me + step, me - step, me]).astype(jnp.int32) % groups
 
     def route(sign):
         pairs = []
@@ -390,26 +372,26 @@
     gated, far_first, far_second = call(
         far_kernel,
         (shape((length, width), bf16), part, part),
-        [scalar, away] + [inside] * 3,
+        [away] + [inside] * 3,
         "far",
         [chunk, flags(pieces)],
         mebibytes=52,
-    )(where, out_weight, query, direct, conv)
+    )(out_weight, query, direct, conv)
     got_first = ahead(far_first)
     got_second = behind(far_second)
     ahead_held, ahead_out, behind_out, behind_held = call(
         near_kernel,
         (part,) * 4,
-        [scalar, away, inside],
+        [away, inside],
         "near",
         [vmem((2, width, size), bf16), flags(2 * pieces)],
         mebibytes=48,
-    )(where, out_weight, gated)
+    )(out_weight, gated)
     ahead_got = ahead(ahead_out)
     behind_got = behind(behind_out)
     own = call(
-        own_kernel, shape((length, size), f32), [scalar, away, inside], "own", [chunk, flags(pieces)], mebibytes=48
-    )(where, out_weight, gated)
+        own_kernel, shape((length, size), f32), [away, inside], "own", [chunk, flags(pieces)], mebibytes=48
+    )(out_weight, gated)
     first_got = ahead(call(add_kernel, part, [inside] * 2, "add_first")(got_first, ahead_held))
     second_got = behind(call(add_kernel, part, [inside] * 2, "add_second")(got_second, behind_held))
     return call(last_kernel, shape((length, size), bf16), [inside] * 5, "last")(

time: 66.5 us -> 64.2 us (0.965)
  Pallas kernels: 17.2 us -> 15.5 us
    pallas_call x4, Pallas kernels: 10.7 us -> 9.06 us  [the longest x1 3.8 us: shards(): call(near_kernel, (part,) * 4, [away, inside], 'near', [vmem((2, width, s...]
  transfers between devices with their start and end apart: 9 -> 9, of which waited for: 7 -> 7; matrix products, arithmetic and copies ran while one was open for 0% -> 0% of each run, Pallas kernels for 13% -> 12%
where the time goes in v2:
time: 64.2 us; the launch traced here: 63.5 us
  starting transfers between devices  24.3 us (38%)
  waiting for transfers between devices  18 us (28%)
  Pallas kernels  15.5 us (24%)
  local copies, waits for them, and re-layouts  5.57 us (9%)
    ppermute x3, starting transfers between devices, behind(): return lax.ppermute(value, ('seq', 'chan'), route(-1))  9.43 us
    all_to_all x1, starting transfers between devices, shards(): received = lax.all_to_all(send, 'seq', 0, 0, tiled=True)  8.43 us
    all_to_all x1, waiting for transfers between devices, shards(): received = lax.all_to_all(send, 'seq', 0, 0, tiled=True)  5.67 us
    unnamed x12, local copies, waits for them, and re-layouts  5.57 us
    all_to_all x1, waiting for transfers between devices, shards(): conv = lax.all_to_all(spectral, 'seq', 0, 0, tiled=True)  5.57 us
    all_to_all x1, starting transfers between devices, shards(): conv = lax.all_to_all(spectral, 'seq', 0, 0, tiled=True)  4.14 us
    pallas_call x1, Pallas kernels, shards(): call(near_kernel, (part,) * 4, [away, inside], 'near', [vmem((2, width, s...  3.8 us
    ppermute x3, waiting for transfers between devices, ahead(): return lax.ppermute(value, ('seq', 'chan'), route(1))  3.28 us
  transfers between devices with their start and end apart: 9, of which 7 were waited for; matrix products, arithmetic and copies ran while one was open for 0% of the time, Pallas kernels for 12%

profile of v2, /device:TPU:0, one launch (start us, length us, event | category | flops | bytes accessed | tf_op | source)
XLA Modules:
  0.0 63.5 jit_solution(15039248828076913796)
XLA Ops:
  0.0 2.6 %mix.1 = (bf16[32,72,128]{2,1,0:T(8,128)(2,1)}, f32[8,128]{1,0:T(8,128)}) custom-call(bf16[3,128,1024]{2,1,0:T(8,128)(2,1)} %bitcast.2, f32[3,3,1024]{2,1,0:T(4,128)} %taps.3, f32[128,1024]{1,0:T(8,128)} %long_filter.1), custom_call_target="tpu_custom_call" | custom-call | tf_op jit(solution)/shard_map/mix/pallas_call | solution.py:319
  2.6 8.4 %all-to-all-start = ((bf16[32,72,128]{2,1,0:T(8,128)(2,1)}), bf16[32,72,128]{2,1,0:T(8,128)(2,1)S(1)}, u32[]{:S(2)}, u32[]{:S(2)}) async-start(bf16[32,72,128]{2,1,0:T(8,128)(2,1)} %get-tuple-element.21), calls=%async_computation | async-start | bytes 1179648 | tf_op jit(solution)/shard_map/all_to_all | solution.py:333
  11.0 0.0 copy-start
  11.0 1.1 %copy-done = bf16[128,3,1024]{2,0,1:T(8,128)(2,1)S(1)} copy-done((bf16[128,3,1024]{2,0,1:T(8,128)(2,1)S(1)}, bf16[128,3,1024]{2,0,1:T(8,128)(2,1)}, u32[]{:S(2)}) %copy-start) | copy-done | bytes 786456
  12.1 0.0 copy-start.2
  12.1 1.1 %copy-done.2 = bf16[1600,256]{1,0:T(8,128)(2,1)S(1)} copy-done((bf16[1600,256]{1,0:T(8,128)(2,1)S(1)}, bf16[1600,256]{1,0:T(8,128)(2,1)}, u32[]{:S(2)}) %copy-start.2) | copy-done | bytes 819224
  13.3 0.0 copy-start.5
  13.3 0.7 %copy-done.5 = f32[8,128]{1,0:T(8,128)S(1)} copy-done((f32[8,128]{1,0:T(8,128)S(1)}, f32[8,128]{1,0:T(8,128)}, u32[]{:S(2)}) %copy-start.5) | copy-done | bytes 4120
  14.0 0.2 tail.1
  14.1 2.2 %collective-permute-start = (bf16[3,2,1024]{2,1,0:T(2,128)(2,1)S(1)}, bf16[3,2,1024]{2,1,0:T(2,128)(2,1)S(1)}, u32[]{:S(2)}, u32[]{:S(2)}) collective-permute-start(bf16[3,2,1024]{2,1,0:T(2,128)(2,1)S(1)} %get-tuple-element.19), channel_id=1, source_target_pairs={{0,4},{4,8},{8,12},{12,16},{16,20},{20,24},{24,28},{28,32},{32,36}... | collective-permute-start | bytes 36872 | tf_op jit(solution)/shard_map/ppermute | solution.py:343
  16.3 0.8 %collective-permute-done.token.prior = bf16[3,2,1024]{2,1,0:T(2,128)(2,1)S(1)} collective-permute-done((bf16[3,2,1024]{2,1,0:T(2,128)(2,1)S(1)}, bf16[3,2,1024]{2,1,0:T(2,128)(2,1)S(1)}, u32[]{:S(2)}, u32[]{:S(2)}) %collective-permute-start) | collective-permute-done | bytes 12320 | tf_op jit(solution)/shard_map/ppermute | solution.py:343
  17.2 5.7 %all-to-all-done.received = bf16[32,72,128]{2,1,0:T(8,128)(2,1)S(1)} async-done(((bf16[32,72,128]{2,1,0:T(8,128)(2,1)}), bf16[32,72,128]{2,1,0:T(8,128)(2,1)S(1)}, u32[]{:S(2)}, u32[]{:S(2)}) %all-to-all-start) | async-done | bytes 589856 | tf_op jit(solution)/shard_map/all_to_all | solution.py:333
  22.8 2.1 %conv.1.token = bf16[32,32,128]{2,1,0:T(8,128)(2,1)} custom-call(bf16[3,2,1024]{2,1,0:T(2,128)(2,1)S(1)} %collective-permute-done.token.prior, bf16[1600,256]{1,0:T(8,128)(2,1)S(1)} %get-tuple-element.20.table, bf16[32,72,128]{2,1,0:T(8,128)(2,1)S(1)} %all-to-all-done.received), custom_call_target="tpu_custom_call" | custom-call | tf_op jit(solution)/shard_map/conv/pallas_call | solution.py:344
  24.9 4.1 %all-to-all-start.1 = ((bf16[32,32,128]{2,1,0:T(8,128)(2,1)}), bf16[32,32,128]{2,1,0:T(8,128)(2,1)S(1)}, u32[]{:S(2)}, u32[]{:S(2)}) async-start(bf16[32,32,128]{2,1,0:T(8,128)(2,1)} %conv.1.token), calls=%async_computation.1 | async-start | bytes 524288 | tf_op jit(solution)/shard_map/all_to_all | solution.py:345
  29.0 0.0 copy-start.1
  29.0 1.1 %copy-done.1 = bf16[128,3,1024]{2,0,1:T(8,128)(2,1)S(1)} copy-done((bf16[128,3,1024]{2,0,1:T(8,128)(2,1)S(1)}, bf16[128,3,1024]{2,0,1:T(8,128)(2,1)}, u32[]{:S(2)}) %copy-start.1) | copy-done | bytes 786456
  30.2 0.0 copy-start.3
  30.2 0.8 %copy-done.3 = f32[3,3,1024]{2,1,0:T(4,128)S(1)} copy-done((f32[3,3,1024]{2,1,0:T(4,128)S(1)}, f32[3,3,1024]{2,1,0:T(4,128)}, u32[]{:S(2)}) %copy-start.3) | copy-done | bytes 36888
  31.0 0.0 copy-start.4
  31.0 0.7 %copy-done.4 = f32[1024]{0:T(1024)S(1)} copy-done((f32[1024]{0:T(1024)S(1)}, f32[1024]{0:T(1024)}, u32[]{:S(2)}) %copy-start.4) | copy-done | bytes 4120
  31.7 0.7 %terms.1 = (bf16[128,1024]{1,0:T(8,128)(2,1)S(1)}, bf16[128,1024]{1,0:T(8,128)(2,1)S(1)}) custom-call(bf16[32,32,128]{2,1,0:T(8,128)(2,1)} %conv.1.token, bf16[3,128,1024]{2,1,0:T(8,128)(2,1)S(1)} %bitcast.4, f32[3,3,1024]{2,1,0:T(4,128)S(1)} %copy-done.3, f32[1,1024]{1,0:T(1,128)S(1)} %bitcast.5, bf16[3,2,1024]{2,1,0:T(2,128)(2,1)S(1)} %collective-permute-done.token.prior), custom_call_target="tpu_custom_call" | custom-call | tf_op jit(solution)/shard_map/terms/pallas_call | solution.py:364
  32.4 5.6 %all-to-all-done.1.conv = bf16[32,32,128]{2,1,0:T(8,128)(2,1)S(1)} async-done(((bf16[32,32,128]{2,1,0:T(8,128)(2,1)}), bf16[32,32,128]{2,1,0:T(8,128)(2,1)S(1)}, u32[]{:S(2)}, u32[]{:S(2)}) %all-to-all-start.1) | async-done | bytes 262176 | tf_op jit(solution)/shard_map/all_to_all | solution.py:345
  38.0 2.6 %far.1 = (bf16[128,1024]{1,0:T(8,128)(2,1)S(1)}, bf16[64,2048]{1,0:T(8,128)(2,1)S(1)}, bf16[64,2048]{1,0:T(8,128)(2,1)S(1)}) custom-call(bf16[1024,8192]{1,0:T(8,128)(2,1)} %weight.5, bf16[128,1024]{1,0:T(8,128)(2,1)S(1)} %get-tuple-element.22.query, bf16[128,1024]{1,0:T(8,128)(2,1)S(1)} %get-tuple-element.23.direct, ...), custom_call_target="tpu_custom_call" | custom-call | tf_op jit(solution)/shard_map/far/pallas_call | solution.py:372
  40.6 2.8 %collective-permute-start.5 = (bf16[64,2048]{1,0:T(8,128)(2,1)S(1)}, bf16[64,2048]{1,0:T(8,128)(2,1)S(1)}, u32[]{:S(2)}, u32[]{:S(2)}) collective-permute-start(bf16[64,2048]{1,0:T(8,128)(2,1)S(1)} %get-tuple-element.29), channel_id=1, source_target_pairs={{0,3},{1,0},{2,1},{3,2},{4,5},{5,6},{6,7},{7,4},{8,11},{9,8},{10,9... | collective-permute-start | bytes 786440 | tf_op jit(solution)/shard_map/ppermute | solution.py:359
  43.4 0.0 collective-permute-start.1
  43.4 3.8 %near.1 = (bf16[64,2048]{1,0:T(8,128)(2,1)S(1)}, bf16[64,2048]{1,0:T(8,128)(2,1)S(1)}, bf16[64,2048]{1,0:T(8,128)(2,1)S(1)}, bf16[64,2048]{1,0:T(8,128)(2,1)S(1)}) custom-call(bf16[1024,8192]{1,0:T(8,128)(2,1)} %weight.5, bf16[128,1024]{1,0:T(8,128)(2,1)S(1)} %get-tuple-element.24.gated), custom_call_target="tpu_custom_call" | custom-call | tf_op jit(solution)/shard_map/near/pallas_call | solution.py:382
  47.2 3.3 %collective-permute-start.3 = (bf16[64,2048]{1,0:T(8,128)(2,1)S(1)}, bf16[64,2048]{1,0:T(8,128)(2,1)S(1)}, u32[]{:S(2)}, u32[]{:S(2)}) collective-permute-start(bf16[64,2048]{1,0:T(8,128)(2,1)S(1)} %get-tuple-element.27), channel_id=1, source_target_pairs={{0,3},{1,0},{2,1},{3,2},{4,5},{5,6},{6,7},{7,4},{8,11},{9,8},{10,9... | collective-permute-start | bytes 786440 | tf_op jit(solution)/shard_map/ppermute | solution.py:359
  50.5 0.0 collective-permute-start.4
  50.5 0.0 collective-permute-done.5.one
  50.5 0.1 add_second.1
  50.6 3.3 %collective-permute-start.6 = (bf16[64,2048]{1,0:T(8,128)(2,1)S(1)}, bf16[64,2048]{1,0:T(8,128)(2,1)S(1)}, u32[]{:S(2)}, u32[]{:S(2)}) collective-permute-start(bf16[64,2048]{1,0:T(8,128)(2,1)S(1)} %add_second.1), channel_id=1, source_target_pairs={{0,3},{1,0},{2,1},{3,2},{4,5},{5,6},{6,7},{7,4},{8,11},{9,8},{10,9... | collective-permute-start | bytes 786440 | tf_op jit(solution)/shard_map/ppermute | solution.py:359
  53.9 0.0 collective-permute-done.1.one
  53.9 0.1 add_first.1
  53.9 0.1 collective-permute-start.2
  54.0 2.5 %own.1 = f32[128,2048]{1,0:T(8,128)S(1)} custom-call(bf16[1024,8192]{1,0:T(8,128)(2,1)} %weight.5, bf16[128,1024]{1,0:T(8,128)(2,1)S(1)} %get-tuple-element.24.gated), custom_call_target="tpu_custom_call" | custom-call | tf_op jit(solution)/shard_map/own/pallas_call | solution.py:392
  56.6 0.6 collective-permute-done.3.first_two
  57.2 2.5 %collective-permute-done.4.second_one = bf16[64,2048]{1,0:T(8,128)(2,1)S(1)} collective-permute-done((bf16[64,2048]{1,0:T(8,128)(2,1)S(1)}, bf16[64,2048]{1,0:T(8,128)(2,1)S(1)}, u32[]{:S(2)}, u32[]{:S(2)}) %collective-permute-start.4) | collective-permute-done | bytes 262176 | tf_op jit(solution)/shard_map/ppermute | solution.py:356
  59.7 2.1 %collective-permute-done.6.second_two = bf16[64,2048]{1,0:T(8,128)(2,1)S(1)} collective-permute-done((bf16[64,2048]{1,0:T(8,128)(2,1)S(1)}, bf16[64,2048]{1,0:T(8,128)(2,1)S(1)}, u32[]{:S(2)}, u32[]{:S(2)}) %collective-permute-start.6) | collective-permute-done | bytes 262176 | tf_op jit(solution)/shard_map/ppermute | solution.py:359
  61.8 0.7 %collective-permute-done.2.first_one = bf16[64,2048]{1,0:T(8,128)(2,1)S(1)} collective-permute-done((bf16[64,2048]{1,0:T(8,128)(2,1)S(1)}, bf16[64,2048]{1,0:T(8,128)(2,1)S(1)}, u32[]{:S(2)}, u32[]{:S(2)}) %collective-permute-start.2) | collective-permute-done | bytes 262176 | tf_op jit(solution)/shard_map/ppermute | solution.py:356
  62.5 0.9 %last.1 = bf16[128,2048]{1,0:T(8,128)(2,1)} custom-call(f32[128,2048]{1,0:T(8,128)S(1)} %own.1, bf16[64,2048]{1,0:T(8,128)(2,1)S(1)} %collective-permute-done.2.first_one, bf16[64,2048]{1,0:T(8,128)(2,1)S(1)} %collective-permute-done.3.first_two, bf16[64,2048]{1,0:T(8,128)(2,1)S(1)} %collective-permute-done.4.second_one, ...), custom_call_target="tpu_custom_call" | custom-call | tf_op jit(solution)/shard_map/last/pallas_call | solution.py:397
Async XLA Ops:
  2.6 20.2 %all-to-all-start = ((bf16[32,72,128]{2,1,0:T(8,128)(2,1)}), bf16[32,72,128]{2,1,0:T(8,128)(2,1)S(1)}, u32[]{:S(2)}, u32[]{:S(2)}) async-start(bf16[32,72,128]{2,1,0:T(8,128)(2,1)} %get-tuple-element.21), calls=%async_computation | async-start | bytes 1179648 | tf_op jit(solution)/shard_map/all_to_all | solution.py:333
  11.0 1.1 %copy-start = (bf16[128,3,1024]{2,0,1:T(8,128)(2,1)S(1)}, bf16[128,3,1024]{2,0,1:T(8,128)(2,1)}, u32[]{:S(2)}) copy-start(bf16[128,3,1024]{2,0,1:T(8,128)(2,1)} %param.6) | copy-start | bytes 2359300
  12.1 1.1 %copy-start.2 = (bf16[1600,256]{1,0:T(8,128)(2,1)S(1)}, bf16[1600,256]{1,0:T(8,128)(2,1)}, u32[]{:S(2)}) copy-start(bf16[1600,256]{1,0:T(8,128)(2,1)} %constant.2.clone.table) | copy-start | bytes 2457604
  13.3 0.7 %copy-start.5 = (f32[8,128]{1,0:T(8,128)S(1)}, f32[8,128]{1,0:T(8,128)}, u32[]{:S(2)}) copy-start(f32[8,128]{1,0:T(8,128)} %get-tuple-element.18.token) | copy-start | bytes 12292
  14.1 3.0 %collective-permute-start = (bf16[3,2,1024]{2,1,0:T(2,128)(2,1)S(1)}, bf16[3,2,1024]{2,1,0:T(2,128)(2,1)S(1)}, u32[]{:S(2)}, u32[]{:S(2)}) collective-permute-start(bf16[3,2,1024]{2,1,0:T(2,128)(2,1)S(1)} %get-tuple-element.19), channel_id=1, source_target_pairs={{0,4},{4,8},{8,12},{12,16},{16,20},{20,24},{24,28},{28,32},{32,36}... | collective-permute-start | bytes 36872 | tf_op jit(solution)/shard_map/ppermute | solution.py:343
  24.9 13.1 %all-to-all-start.1 = ((bf16[32,32,128]{2,1,0:T(8,128)(2,1)}), bf16[32,32,128]{2,1,0:T(8,128)(2,1)S(1)}, u32[]{:S(2)}, u32[]{:S(2)}) async-start(bf16[32,32,128]{2,1,0:T(8,128)(2,1)} %conv.1.token), calls=%async_computation.1 | async-start | bytes 524288 | tf_op jit(solution)/shard_map/all_to_all | solution.py:345
  29.0 1.1 %copy-start.1 = (bf16[128,3,1024]{2,0,1:T(8,128)(2,1)S(1)}, bf16[128,3,1024]{2,0,1:T(8,128)(2,1)}, u32[]{:S(2)}) copy-start(bf16[128,3,1024]{2,0,1:T(8,128)(2,1)} %param.6) | copy-start | bytes 2359300
  30.2 0.8 %copy-start.3 = (f32[3,3,1024]{2,1,0:T(4,128)S(1)}, f32[3,3,1024]{2,1,0:T(4,128)}, u32[]{:S(2)}) copy-start(f32[3,3,1024]{2,1,0:T(4,128)} %taps.3) | copy-start | bytes 110596
  31.0 0.7 %copy-start.4 = (f32[1024]{0:T(1024)S(1)}, f32[1024]{0:T(1024)}, u32[]{:S(2)}) copy-start(f32[1024]{0:T(1024)} %param.8) | copy-start | bytes 12292
  40.6 9.9 %collective-permute-start.5 = (bf16[64,2048]{1,0:T(8,128)(2,1)S(1)}, bf16[64,2048]{1,0:T(8,128)(2,1)S(1)}, u32[]{:S(2)}, u32[]{:S(2)}) collective-permute-start(bf16[64,2048]{1,0:T(8,128)(2,1)S(1)} %get-tuple-element.29), channel_id=1, source_target_pairs={{0,3},{1,0},{2,1},{3,2},{4,5},{5,6},{6,7},{7,4},{8,11},{9,8},{10,9... | collective-permute-start | bytes 786440 | tf_op jit(solution)/shard_map/ppermute | solution.py:359
  43.4 10.5 %collective-permute-start.1 = (bf16[64,2048]{1,0:T(8,128)(2,1)S(1)}, bf16[64,2048]{1,0:T(8,128)(2,1)S(1)}, u32[]{:S(2)}, u32[]{:S(2)}) collective-permute-start(bf16[64,2048]{1,0:T(8,128)(2,1)S(1)} %get-tuple-element.25), channel_id=1, source_target_pairs={{0,1},{1,2},{2,3},{3,0},{4,7},{5,4},{6,5},{7,6},{8,9},{9,10},{10,1... | collective-permute-start | bytes 786440 | tf_op jit(solution)/shard_map/ppermute | solution.py:356
  47.2 10.0 %collective-permute-start.3 = (bf16[64,2048]{1,0:T(8,128)(2,1)S(1)}, bf16[64,2048]{1,0:T(8,128)(2,1)S(1)}, u32[]{:S(2)}, u32[]{:S(2)}) collective-permute-start(bf16[64,2048]{1,0:T(8,128)(2,1)S(1)} %get-tuple-element.27), channel_id=1, source_target_pairs={{0,3},{1,0},{2,1},{3,2},{4,5},{5,6},{6,7},{7,4},{8,11},{9,8},{10,9... | collective-permute-start | bytes 786440 | tf_op jit(solution)/shard_map/ppermute | solution.py:359
  50.5 9.2 %collective-permute-start.4 = (bf16[64,2048]{1,0:T(8,128)(2,1)S(1)}, bf16[64,2048]{1,0:T(8,128)(2,1)S(1)}, u32[]{:S(2)}, u32[]{:S(2)}) collective-permute-start(bf16[64,2048]{1,0:T(8,128)(2,1)S(1)} %get-tuple-element.28), channel_id=1, source_target_pairs={{0,1},{1,2},{2,3},{3,0},{4,7},{5,4},{6,5},{7,6},{8,9},{9,10},{10,1... | collective-permute-start | bytes 786440 | tf_op jit(solution)/shard_map/ppermute | solution.py:356
  50.6 11.2 %collective-permute-start.6 = (bf16[64,2048]{1,0:T(8,128)(2,1)S(1)}, bf16[64,2048]{1,0:T(8,128)(2,1)S(1)}, u32[]{:S(2)}, u32[]{:S(2)}) collective-permute-start(bf16[64,2048]{1,0:T(8,128)(2,1)S(1)} %add_second.1), channel_id=1, source_target_pairs={{0,3},{1,0},{2,1},{3,2},{4,5},{5,6},{6,7},{7,4},{8,11},{9,8},{10,9... | collective-permute-start | bytes 786440 | tf_op jit(solution)/shard_map/ppermute | solution.py:359
  53.9 8.6 %collective-permute-start.2 = (bf16[64,2048]{1,0:T(8,128)(2,1)S(1)}, bf16[64,2048]{1,0:T(8,128)(2,1)S(1)}, u32[]{:S(2)}, u32[]{:S(2)}) collective-permute-start(bf16[64,2048]{1,0:T(8,128)(2,1)S(1)} %add_first.1), channel_id=1, source_target_pairs={{0,1},{1,2},{2,3},{3,0},{4,7},{5,4},{6,5},{7,6},{8,9},{9,10},{10,1... | collective-permute-start | bytes 786440 | tf_op jit(solution)/shard_map/ppermute | solution.py:356

commit v3 on v2

--- a/solution.py
+++ b/solution.py
@@ -1,3 +1,4 @@
+import functools
 import math
 
 import jax
@@ -17,10 +18,11 @@
     return pl.BlockSpec(memory_space=pltpu.VMEM)
 
 
-def transform_table(blocks, length):
+def transform_table(order, length):
+    blocks = len(order)
     total = blocks * length
     k1 = np.arange(blocks)[:, None] + 0.25
-    outer = 2.0 * math.pi * k1 * np.arange(blocks)[None, :] / blocks
+    outer = 2.0 * math.pi * k1 * np.array(order)[None, :] / blocks
     eye = np.eye(GROUP)
     ahead = np.concatenate([np.kron(np.cos(outer), eye), np.kron(-np.sin(outer), eye)], axis=0)
     back = np.concatenate([np.kron(np.cos(outer).T, eye), np.kron(-np.sin(outer).T, eye)], axis=0) / total
@@ -160,9 +162,11 @@
     return received[:, row : row + GROUP, :].astype(jnp.float32).reshape(blocks * GROUP, length)
 
 
-def patched(signal, edge, index):
+def patched(signal, edge, index, order):
     length = edge.shape[1]
-    before = jnp.concatenate([jnp.zeros((GROUP, length), jnp.float32), edge[:-GROUP]], axis=0)
+    nothing = jnp.zeros((GROUP, length), jnp.float32)
+    at = lambda block: edge[order.index(block) * GROUP : (order.index(block) + 1) * GROUP]
+    before = jnp.concatenate([at(block - 1) if block else nothing for block in order], axis=0)
     joined = pltpu.roll(edge, (length - 8 * index) % length, 1) + pltpu.roll(before, length - 8 * index - 4, 1)
     whole_edge = joined * pltpu.roll(joined, length - 2, 1)
     lane = lax.broadcasted_iota(jnp.int32, edge.shape, 1)
@@ -180,7 +184,7 @@
     return jnp.dot(turned, inner_ahead, preferred_element_type=jnp.float32)
 
 
-def conv_kernel(token, table, received, out):
+def conv_kernel(order, token, table, received, out):
     del token
     blocks, lanes, length = out.shape
     size = blocks * GROUP
@@ -189,7 +193,7 @@
     groups = [rows_of(received, i * GROUP).astype(jnp.bfloat16) for i in range(count)]
     other = spectrum(groups, ahead, inner_ahead, cosine, sine)
     edge = rows_of(received, 2 * lanes)
-    groups = [patched(rows_of(received, lanes + i * GROUP), edge, i).astype(jnp.bfloat16) for i in range(count)]
+    groups = [patched(rows_of(received, lanes + i * GROUP), edge, i, order).astype(jnp.bfloat16) for i in range(count)]
     part = spectrum(groups, ahead, inner_ahead, cosine, sine)
     xr, xi, hr, hi = part[:, :length], part[:, length:], other[:, :length], other[:, length:]
     joined = jnp.concatenate([xr * hr - xi * hi, xr * hi + xi * hr], axis=1)
@@ -209,17 +213,19 @@
 PIECE = 256
 
 
-def chunk_index(kind, groups):
+def chunk_start(kind, total):
+    groups = lax.axis_size("chan")
     step = 1 - 2 * (lax.axis_index("seq") % 2)
-    return (lax.axis_index("chan") + (2, step, groups - step, 0)[kind]) % groups
-
-
-def fetch_chunk(weight, index, held, sems, first_sem):
+    index = (lax.axis_index("chan") + (2, step, groups - step, 0)[kind]) % groups
+    return index * (total // groups)
+
+
+def fetch_columns(weight, first_column, held, sems, first_sem):
     depth, size = held.shape
     copies = []
     for piece in range(depth // PIECE):
         rows = pl.ds(piece * PIECE, PIECE)
-        columns = pl.ds(pl.multiple_of(index * size, size), size)
+        columns = pl.ds(pl.multiple_of(first_column, 128), size)
         copy = pltpu.make_async_copy(weight.at[rows, columns], held.at[rows], sems.at[first_sem + piece])
         copy.start()
         copies.append(copy)
@@ -237,10 +243,9 @@
 
 
 def far_kernel(weight, query, direct, conv, gated_out, first_out, second_out, held, sems):
-    size = held.shape[1]
     length, width = query.shape
     quarter = conv.shape[0] * GROUP
-    pieces = fetch_chunk(weight, chunk_index(0, weight.shape[1] // size), held, sems, 0)
+    pieces = fetch_columns(weight, chunk_start(0, weight.shape[1]), held, sems, 0)
     for start in range(0, width, 128):
         columns = slice(start, start + 128)
         first = start % quarter // GROUP
@@ -249,28 +254,33 @@
         turned = turned.reshape(128, length).T
         turned += direct[:, columns].astype(jnp.float32)
         gated_out[:, columns] = (query[:, columns].astype(jnp.float32) * turned).astype(jnp.bfloat16)
-    part = project(gated_out, held, pieces)
-    top = length // 2
-    first_out[...] = part[:top].astype(jnp.bfloat16)
-    second_out[...] = part[top:].astype(jnp.bfloat16)
-
-
-def near_kernel(weight, gated, ahead_held, ahead_out, behind_out, behind_held, held, sems):
-    half, size = ahead_out.shape
-    count = held.shape[1] // PIECE
-    ahead_pieces = fetch_chunk(weight, chunk_index(1, weight.shape[1] // size), held.at[0], sems, 0)
-    behind_pieces = fetch_chunk(weight, chunk_index(2, weight.shape[1] // size), held.at[1], sems, count)
-    part = project(gated, held.at[0], ahead_pieces)
-    ahead_held[...] = part[:half].astype(jnp.bfloat16)
-    ahead_out[...] = part[half:].astype(jnp.bfloat16)
-    part = project(gated, held.at[1], behind_pieces)
-    behind_out[...] = part[:half].astype(jnp.bfloat16)
-    behind_held[...] = part[half:].astype(jnp.bfloat16)
+    part = project(gated_out, held, pieces).astype(jnp.bfloat16)
+    split = second_out.shape[1]
+    second_out[...] = part[:, :split]
+    first_out[...] = part[:, split:]
+
+
+def near_kernel(weight, gated, ahead_out, behind_out, ahead_held, behind_held, sems):
+    total = weight.shape[1]
+    right = ahead_out.shape[1]
+    behind_pieces = fetch_columns(weight, chunk_start(2, total) + right, behind_held, sems, 0)
+    ahead_pieces = fetch_columns(weight, chunk_start(1, total), ahead_held, sems, len(behind_pieces))
+    behind_out[...] = project(gated, behind_held, behind_pieces).astype(jnp.bfloat16)
+    ahead_out[...] = project(gated, ahead_held, ahead_pieces).astype(jnp.bfloat16)
+
+
+def joined_kernel(weight, gated, got, ahead_out, behind_out, ahead_held, behind_held, sems):
+    total = weight.shape[1]
+    left = behind_out.shape[1]
+    behind_pieces = fetch_columns(weight, chunk_start(2, total), behind_held, sems, 0)
+    ahead_pieces = fetch_columns(weight, chunk_start(1, total) + left, ahead_held, sems, len(behind_pieces))
+    part = project(gated, behind_held, behind_pieces)
+    behind_out[...] = (part + got[...].astype(jnp.float32)).astype(jnp.bfloat16)
+    ahead_out[...] = project(gated, ahead_held, ahead_pieces).astype(jnp.bfloat16)
 
 
 def own_kernel(weight, gated, out, held, sems):
-    size = held.shape[1]
-    out[...] = project(gated, held, fetch_chunk(weight, chunk_index(3, weight.shape[1] // size), held, sems, 0))
+    out[...] = project(gated, held, fetch_columns(weight, chunk_start(3, weight.shape[1]), held, sems, 0))
 
 
 def add_kernel(one, two, out):
@@ -278,10 +288,10 @@
 
 
 def last_kernel(own, first_one, first_two, second_one, second_two, out):
-    half = out.shape[0] // 2
+    split = second_one.shape[1]
     wide = lambda ref: ref[...].astype(jnp.float32)
-    out[:half] = (own[:half] + wide(first_one) + wide(first_two)).astype(jnp.bfloat16)
-    out[half:] = (own[half:] + wide(second_one) + wide(second_two)).astype(jnp.bfloat16)
+    out[:, :split] = (own[:, :split] + wide(second_one) + wide(second_two)).astype(jnp.bfloat16)
+    out[:, split:] = (own[:, split:] + wide(first_one) + wide(first_two)).astype(jnp.bfloat16)
 
 
 def call(kernel, outs, specs, name, scratch=(), out_specs=None, mebibytes=16):
@@ -301,7 +311,6 @@
     members = lax.axis_size("seq")
     groups = lax.axis_size("chan")
     lanes = width // members
-    half = length // 2
     size = out_weight.shape[1] // groups
     bf16, f32 = jnp.bfloat16, jnp.float32
     shape = jax.ShapeDtypeStruct
@@ -312,6 +321,12 @@
     turned_shape = shape((members, lanes, length), bf16)
     vmem = lambda dims, dtype: pltpu.VMEM(dims, dtype)
     flags = lambda count: pltpu.SemaphoreType.DMA((count,))
+
+    head = 2 * members // 3
+    order = [head] + [i for i in range(members) if i != head]
+
+    def exchange(value):
+        return lax.all_to_all(value, "seq", 0, 0, axis_index_groups=[order], tiled=True)
 
     by_feature = jnp.transpose(features, (1, 0, 2))
     skip = skip_gain[None]
@@ -330,8 +345,8 @@
         ],
         mebibytes=60,
     )(by_feature, short_taps, long_filter)
-    received = lax.all_to_all(send, "seq", 0, 0, tiled=True)
-    table = transform_table(members, length)
+    received = exchange(send)
+    table = transform_table(order, length)
     table, tail = call(
         tail_kernel,
         (shape(table.shape, bf16), shape((3, 2, width), bf16)),
@@ -341,8 +356,8 @@
         mebibytes=50,
     )(token, table, by_feature)
     prior = lax.ppermute(tail, "seq", [(i, i + 1) for i in range(members - 1)])
-    spectral = call(conv_kernel, turned_shape, [loose] + [inside] * 2, "conv")(prior, table, received)
-    conv = lax.all_to_all(spectral, "seq", 0, 0, tiled=True)
+    spectral = call(functools.partial(conv_kernel, order), turned_shape, [loose] + [inside] * 2, "conv")(prior, table, received)
+    conv = exchange(spectral)
 
     def route(sign):
         pairs = []
@@ -358,7 +373,8 @@
     def behind(value):
         return lax.ppermute(value, ("seq", "chan"), route(-1))
 
-    part = shape((half, size), bf16)
+    split = size // 2
+    left, right = shape((length, split), bf16), shape((length, size - split), bf16)
     chunk = vmem((width, size), bf16)
     pieces = width // PIECE
     query, direct = call(
@@ -371,7 +387,7 @@
     )(spectral, by_feature, short_taps, skip, prior)
     gated, far_first, far_second = call(
         far_kernel,
-        (shape((length, width), bf16), part, part),
+        (shape((length, width), bf16), right, left),
         [away] + [inside] * 3,
         "far",
         [chunk, flags(pieces)],
@@ -379,21 +395,26 @@
     )(out_weight, query, direct, conv)
     got_first = ahead(far_first)
     got_second = behind(far_second)
-    ahead_held, ahead_out, behind_out, behind_held = call(
-        near_kernel,
-        (part,) * 4,
-        [away, inside],
-        "near",
-        [vmem((2, width, size), bf16), flags(2 * pieces)],
-        mebibytes=48,
-    )(out_weight, gated)
+
+    def pair(kernel, ahead_shape, behind_shape, name, *more):
+        return call(
+            kernel,
+            (ahead_shape, behind_shape),
+            [away] + [inside] * (1 + len(more)),
+            name,
+            [vmem((width, ahead_shape.shape[1]), bf16), vmem((width, behind_shape.shape[1]), bf16), flags(2 * pieces)],
+            mebibytes=48,
+        )(out_weight, gated, *more)
+
+    ahead_out, behind_out = pair(near_kernel, left, right, "near")
+    behind_got = behind(behind_out)
     ahead_got = ahead(ahead_out)
-    behind_got = behind(behind_out)
+    ahead_held, joined = pair(joined_kernel, right, left, "joined", got_second)
+    second_got = behind(joined)
     own = call(
         own_kernel, shape((length, size), f32), [away, inside], "own", [chunk, flags(pieces)], mebibytes=48
     )(out_weight, gated)
-    first_got = ahead(call(add_kernel, part, [inside] * 2, "add_first")(got_first, ahead_held))
-    second_got = behind(call(add_kernel, part, [inside] * 2, "add_second")(got_second, behind_held))
+    first_got = ahead(call(add_kernel, right, [inside] * 2, "add")(got_first, ahead_held))
     return call(last_kernel, shape((length, size), bf16), [inside] * 5, "last")(
         own, first_got, behind_got, ahead_got, second_got
     )

time: 64.2 us -> 61.1 us (0.952)
  waiting for transfers between devices: 18 us -> 8.68 us
  starting transfers between devices: 24.3 us -> 29.5 us
  Pallas kernels: 15.5 us -> 16.6 us
    all_to_all x2, waiting for transfers between devices: 11.2 us -> 3.07 us  [exchange(): lax.all_to_all(value, 'seq', 0, 0, axis_index_groups=[order], tiled=True)]
    all_to_all x2, starting transfers between devices: 12.6 us -> 18 us  [exchange(): lax.all_to_all(value, 'seq', 0, 0, axis_index_groups=[order], tiled=True)]
    ppermute x3, waiting for transfers between devices: 2.7 us -> 0.6 us  [behind(): return lax.ppermute(value, ('seq', 'chan'), route(-1))]
    ppermute x3, starting transfers between devices: 9.43 us -> 8.11 us  [behind(): return lax.ppermute(value, ('seq', 'chan'), route(-1))]
    ppermute x3, starting transfers between devices: 0.08 us -> 1.35 us  [ahead(): return lax.ppermute(value, ('seq', 'chan'), route(1))]
    pallas_call x5, Pallas kernels: 8.56 us -> 9.64 us  [the longest x2 4.93 us: pair(): call(kernel, (ahead_shape, behind_shape), [away] + [inside] * (1 + len(mo...]
    ppermute x3, waiting for transfers between devices: 3.28 us -> 4.19 us  [ahead(): return lax.ppermute(value, ('seq', 'chan'), route(1))]
  transfers between devices with their start and end apart: 9 -> 9, of which waited for: 7 -> 6; matrix products, arithmetic and copies ran while one was open for 0% -> 0% of each run, Pallas kernels for 12% -> 14%
where the time goes in v3:
time: 61.1 us; the launch traced here: 60.5 us
  starting transfers between devices  29.5 us (48%)
  Pallas kernels  16.6 us (27%)
  waiting for transfers between devices  8.68 us (14%)
  local copies, waits for them, and re-layouts  5.57 us (9%)
    all_to_all x2, starting transfers between devices, exchange(): lax.all_to_all(value, 'seq', 0, 0, axis_index_groups=[order], tiled=True)  18 us
    ppermute x3, starting transfers between devices, behind(): return lax.ppermute(value, ('seq', 'chan'), route(-1))  8.11 us
    unnamed x12, local copies, waits for them, and re-layouts  5.57 us
    pallas_call x2, Pallas kernels, pair(): call(kernel, (ahead_shape, behind_shape), [away] + [inside] * (1 + len(mo...  4.93 us
    ppermute x3, waiting for transfers between devices, ahead(): return lax.ppermute(value, ('seq', 'chan'), route(1))  4.19 us
    all_to_all x2, waiting for transfers between devices, exchange(): lax.all_to_all(value, 'seq', 0, 0, axis_index_groups=[order], tiled=True)  3.07 us
    pallas_call x1, Pallas kernels, shards(): call(far_kernel, (shape((length, width), bf16), right, left), [away] + [i...  2.56 us
    pallas_call x1, Pallas kernels, shards(): call(mix_kernel, (sending, shape((8, 128), f32)), [away] * 3, 'mix', [vme...  2.56 us
  transfers between devices with their start and end apart: 9, of which 6 were waited for; matrix products, arithmetic and copies ran while one was open for 0% of the time, Pallas kernels for 14%

profile of v3, /device:TPU:0, one launch (start us, length us, event | category | flops | bytes accessed | tf_op | source)
XLA Modules:
  0.0 60.5 jit_solution(16810244370326210120)
XLA Ops:
  0.0 2.6 %mix.1 = (bf16[32,72,128]{2,1,0:T(8,128)(2,1)}, f32[8,128]{1,0:T(8,128)}) custom-call(bf16[3,128,1024]{2,1,0:T(8,128)(2,1)} %bitcast.2, f32[3,3,1024]{2,1,0:T(4,128)} %taps.3, f32[128,1024]{1,0:T(8,128)} %long_filter.1), custom_call_target="tpu_custom_call" | custom-call | tf_op jit(solution)/shard_map/mix/pallas_call | solution.py:334
  2.6 10.1 %all-to-all-start = ((bf16[32,72,128]{2,1,0:T(8,128)(2,1)}), bf16[32,72,128]{2,1,0:T(8,128)(2,1)S(1)}, u32[]{:S(2)}, u32[]{:S(2)}) async-start(bf16[32,72,128]{2,1,0:T(8,128)(2,1)} %get-tuple-element.21), calls=%async_computation | async-start | bytes 1179648 | tf_op jit(solution)/shard_map/all_to_all | solution.py:329
  12.7 0.0 copy-start
  12.7 1.1 %copy-done = bf16[128,3,1024]{2,0,1:T(8,128)(2,1)S(1)} copy-done((bf16[128,3,1024]{2,0,1:T(8,128)(2,1)S(1)}, bf16[128,3,1024]{2,0,1:T(8,128)(2,1)}, u32[]{:S(2)}) %copy-start) | copy-done | bytes 786456
  13.8 0.0 copy-start.2
  13.8 1.1 %copy-done.2 = bf16[1600,256]{1,0:T(8,128)(2,1)S(1)} copy-done((bf16[1600,256]{1,0:T(8,128)(2,1)S(1)}, bf16[1600,256]{1,0:T(8,128)(2,1)}, u32[]{:S(2)}) %copy-start.2) | copy-done | bytes 819224
  15.0 0.0 copy-start.5
  15.0 0.7 %copy-done.5 = f32[8,128]{1,0:T(8,128)S(1)} copy-done((f32[8,128]{1,0:T(8,128)S(1)}, f32[8,128]{1,0:T(8,128)}, u32[]{:S(2)}) %copy-start.5) | copy-done | bytes 4120
  15.6 0.2 tail.1
  15.8 2.1 %collective-permute-start = (bf16[3,2,1024]{2,1,0:T(2,128)(2,1)S(1)}, bf16[3,2,1024]{2,1,0:T(2,128)(2,1)S(1)}, u32[]{:S(2)}, u32[]{:S(2)}) collective-permute-start(bf16[3,2,1024]{2,1,0:T(2,128)(2,1)S(1)} %get-tuple-element.19), channel_id=1, source_target_pairs={{0,4},{4,8},{8,12},{12,16},{16,20},{20,24},{24,28},{28,32},{32,36}... | collective-permute-start | bytes 36872 | tf_op jit(solution)/shard_map/ppermute | solution.py:358
  17.9 0.8 %collective-permute-done.token.prior = bf16[3,2,1024]{2,1,0:T(2,128)(2,1)S(1)} collective-permute-done((bf16[3,2,1024]{2,1,0:T(2,128)(2,1)S(1)}, bf16[3,2,1024]{2,1,0:T(2,128)(2,1)S(1)}, u32[]{:S(2)}, u32[]{:S(2)}) %collective-permute-start) | collective-permute-done | bytes 12320 | tf_op jit(solution)/shard_map/ppermute | solution.py:358
  18.7 2.0 %all-to-all-done.received = bf16[32,72,128]{2,1,0:T(8,128)(2,1)S(1)} async-done(((bf16[32,72,128]{2,1,0:T(8,128)(2,1)}), bf16[32,72,128]{2,1,0:T(8,128)(2,1)S(1)}, u32[]{:S(2)}, u32[]{:S(2)}) %all-to-all-start) | async-done | bytes 589856 | tf_op jit(solution)/shard_map/all_to_all | solution.py:329
  20.7 2.1 %conv.1.token = bf16[32,32,128]{2,1,0:T(8,128)(2,1)} custom-call(bf16[3,2,1024]{2,1,0:T(2,128)(2,1)S(1)} %collective-permute-done.token.prior, bf16[1600,256]{1,0:T(8,128)(2,1)S(1)} %get-tuple-element.20.table, bf16[32,72,128]{2,1,0:T(8,128)(2,1)S(1)} %all-to-all-done.received), custom_call_target="tpu_custom_call" | custom-call | tf_op jit(solution)/shard_map/conv/pallas_call | solution.py:359
  22.7 7.9 %all-to-all-start.1 = ((bf16[32,32,128]{2,1,0:T(8,128)(2,1)}), bf16[32,32,128]{2,1,0:T(8,128)(2,1)S(1)}, u32[]{:S(2)}, u32[]{:S(2)}) async-start(bf16[32,32,128]{2,1,0:T(8,128)(2,1)} %conv.1.token), calls=%async_computation.1 | async-start | bytes 524288 | tf_op jit(solution)/shard_map/all_to_all | solution.py:329
  30.6 0.0 copy-start.1
  30.7 1.1 %copy-done.1 = bf16[128,3,1024]{2,0,1:T(8,128)(2,1)S(1)} copy-done((bf16[128,3,1024]{2,0,1:T(8,128)(2,1)S(1)}, bf16[128,3,1024]{2,0,1:T(8,128)(2,1)}, u32[]{:S(2)}) %copy-start.1) | copy-done | bytes 786456
  31.8 0.0 copy-start.3
  31.8 0.8 %copy-done.3 = f32[3,3,1024]{2,1,0:T(4,128)S(1)} copy-done((f32[3,3,1024]{2,1,0:T(4,128)S(1)}, f32[3,3,1024]{2,1,0:T(4,128)}, u32[]{:S(2)}) %copy-start.3) | copy-done | bytes 36888
  32.6 0.0 copy-start.4
  32.6 0.7 %copy-done.4 = f32[1024]{0:T(1024)S(1)} copy-done((f32[1024]{0:T(1024)S(1)}, f32[1024]{0:T(1024)}, u32[]{:S(2)}) %copy-start.4) | copy-done | bytes 4120
  33.3 0.7 %terms.1 = (bf16[128,1024]{1,0:T(8,128)(2,1)S(1)}, bf16[128,1024]{1,0:T(8,128)(2,1)S(1)}) custom-call(bf16[32,32,128]{2,1,0:T(8,128)(2,1)} %conv.1.token, bf16[3,128,1024]{2,1,0:T(8,128)(2,1)S(1)} %bitcast.4, f32[3,3,1024]{2,1,0:T(4,128)S(1)} %copy-done.3, f32[1,1024]{1,0:T(1,128)S(1)} %bitcast.5, bf16[3,2,1024]{2,1,0:T(2,128)(2,1)S(1)} %collective-permute-done.token.prior), custom_call_target="tpu_custom_call" | custom-call | tf_op jit(solution)/shard_map/terms/pallas_call | solution.py:380
  34.0 1.1 %all-to-all-done.1.conv = bf16[32,32,128]{2,1,0:T(8,128)(2,1)S(1)} async-done(((bf16[32,32,128]{2,1,0:T(8,128)(2,1)}), bf16[32,32,128]{2,1,0:T(8,128)(2,1)S(1)}, u32[]{:S(2)}, u32[]{:S(2)}) %all-to-all-start.1) | async-done | bytes 262176 | tf_op jit(solution)/shard_map/all_to_all | solution.py:329
  35.1 2.6 %far.1 = (bf16[128,1024]{1,0:T(8,128)(2,1)S(1)}, bf16[128,1024]{1,0:T(8,128)(2,1)S(1)}, bf16[128,1024]{1,0:T(8,128)(2,1)S(1)}) custom-call(bf16[1024,8192]{1,0:T(8,128)(2,1)} %weight.7, bf16[128,1024]{1,0:T(8,128)(2,1)S(1)} %get-tuple-element.22.query, bf16[128,1024]{1,0:T(8,128)(2,1)S(1)} %get-tuple-element.23.direct, ...), custom_call_target="tpu_custom_call" | custom-call | tf_op jit(solution)/shard_map/far/pallas_call | solution.py:388
  37.7 2.8 %collective-permute-start.2 = (bf16[128,1024]{1,0:T(8,128)(2,1)S(1)}, bf16[128,1024]{1,0:T(8,128)(2,1)S(1)}, u32[]{:S(2)}, u32[]{:S(2)}) collective-permute-start(bf16[128,1024]{1,0:T(8,128)(2,1)S(1)} %get-tuple-element.26), channel_id=1, source_target_pairs={{0,3},{1,0},{2,1},{3,2},{4,5},{5,6},{6,7},{7,4},{8,11},{9,8},{10,9... | collective-permute-start | bytes 786440 | tf_op jit(solution)/shard_map/ppermute | solution.py:374
  40.5 0.0 collective-permute-start.1
  40.5 2.5 %near.1 = (bf16[128,1024]{1,0:T(8,128)(2,1)S(1)}, bf16[128,1024]{1,0:T(8,128)(2,1)S(1)}) custom-call(bf16[1024,8192]{1,0:T(8,128)(2,1)} %weight.7, bf16[128,1024]{1,0:T(8,128)(2,1)S(1)} %get-tuple-element.24.gated), custom_call_target="tpu_custom_call" | custom-call | tf_op jit(solution)/shard_map/near/pallas_call | solution.py:400
  43.0 3.3 %collective-permute-start.4 = (bf16[128,1024]{1,0:T(8,128)(2,1)S(1)}, bf16[128,1024]{1,0:T(8,128)(2,1)S(1)}, u32[]{:S(2)}, u32[]{:S(2)}) collective-permute-start(bf16[128,1024]{1,0:T(8,128)(2,1)S(1)} %get-tuple-element.28), channel_id=1, source_target_pairs={{0,3},{1,0},{2,1},{3,2},{4,5},{5,6},{6,7},{7,4},{8,11},{9,8},{10,9... | collective-permute-start | bytes 786440 | tf_op jit(solution)/shard_map/ppermute | solution.py:374
  46.3 0.0 collective-permute-start.5
  46.3 0.6 collective-permute-done.2.got
  46.9 2.5 %joined.1 = (bf16[128,1024]{1,0:T(8,128)(2,1)S(1)}, bf16[128,1024]{1,0:T(8,128)(2,1)S(1)}) custom-call(bf16[1024,8192]{1,0:T(8,128)(2,1)} %weight.7, bf16[128,1024]{1,0:T(8,128)(2,1)S(1)} %get-tuple-element.24.gated, bf16[128,1024]{1,0:T(8,128)(2,1)S(1)} %collective-permute-done.2.got), custom_call_target="tpu_custom_call" | custom-call | tf_op jit(solution)/shard_map/joined/pallas_call | solution.py:400
  49.4 0.2 collective-permute-done.1.one
  49.6 0.1 add.1
  49.7 1.3 %collective-permute-start.3 = (bf16[128,1024]{1,0:T(8,128)(2,1)S(1)}, bf16[128,1024]{1,0:T(8,128)(2,1)S(1)}, u32[]{:S(2)}, u32[]{:S(2)}) collective-permute-start(bf16[128,1024]{1,0:T(8,128)(2,1)S(1)} %add.1), channel_id=1, source_target_pairs={{0,1},{1,2},{2,3},{3,0},{4,7},{5,4},{6,5},{7,6},{8,9},{9,10},{10,1... | collective-permute-start | bytes 786440 | tf_op jit(solution)/shard_map/ppermute | solution.py:371
  51.0 2.0 %collective-permute-start.6 = (bf16[128,1024]{1,0:T(8,128)(2,1)S(1)}, bf16[128,1024]{1,0:T(8,128)(2,1)S(1)}, u32[]{:S(2)}, u32[]{:S(2)}) collective-permute-start(bf16[128,1024]{1,0:T(8,128)(2,1)S(1)} %get-tuple-element.30), channel_id=1, source_target_pairs={{0,3},{1,0},{2,1},{3,2},{4,5},{5,6},{6,7},{7,4},{8,11},{9,8},{10,9... | collective-permute-start | bytes 786440 | tf_op jit(solution)/shard_map/ppermute | solution.py:374
  53.0 2.5 %own.1 = f32[128,2048]{1,0:T(8,128)S(1)} custom-call(bf16[1024,8192]{1,0:T(8,128)(2,1)} %weight.7, bf16[128,1024]{1,0:T(8,128)(2,1)S(1)} %get-tuple-element.24.gated), custom_call_target="tpu_custom_call" | custom-call | tf_op jit(solution)/shard_map/own/pallas_call | solution.py:414
  55.5 0.0 collective-permute-done.4.first_two
  55.5 0.0 collective-permute-done.5.second_one
  55.5 4.0 %collective-permute-done.3.first_one = bf16[128,1024]{1,0:T(8,128)(2,1)S(1)} collective-permute-done((bf16[128,1024]{1,0:T(8,128)(2,1)S(1)}, bf16[128,1024]{1,0:T(8,128)(2,1)S(1)}, u32[]{:S(2)}, u32[]{:S(2)}) %collective-permute-start.3) | collective-permute-done | bytes 262176 | tf_op jit(solution)/shard_map/ppermute | solution.py:371
  59.5 0.0 collective-permute-done.6.second_two
  59.5 0.9 %last.1 = bf16[128,2048]{1,0:T(8,128)(2,1)} custom-call(f32[128,2048]{1,0:T(8,128)S(1)} %own.1, bf16[128,1024]{1,0:T(8,128)(2,1)S(1)} %collective-permute-done.3.first_one, bf16[128,1024]{1,0:T(8,128)(2,1)S(1)} %collective-permute-done.4.first_two, bf16[128,1024]{1,0:T(8,128)(2,1)S(1)} %collective-permute-done.5.second_one, ...), custom_call_target="tpu_custom_call" | custom-call | tf_op jit(solution)/shard_map/last/pallas_call | solution.py:418
Async XLA Ops:
  2.6 18.1 %all-to-all-start = ((bf16[32,72,128]{2,1,0:T(8,128)(2,1)}), bf16[32,72,128]{2,1,0:T(8,128)(2,1)S(1)}, u32[]{:S(2)}, u32[]{:S(2)}) async-start(bf16[32,72,128]{2,1,0:T(8,128)(2,1)} %get-tuple-element.21), calls=%async_computation | async-start | bytes 1179648 | tf_op jit(solution)/shard_map/all_to_all | solution.py:329
  12.7 1.1 %copy-start = (bf16[128,3,1024]{2,0,1:T(8,128)(2,1)S(1)}, bf16[128,3,1024]{2,0,1:T(8,128)(2,1)}, u32[]{:S(2)}) copy-start(bf16[128,3,1024]{2,0,1:T(8,128)(2,1)} %param.6) | copy-start | bytes 2359300
  13.8 1.1 %copy-start.2 = (bf16[1600,256]{1,0:T(8,128)(2,1)S(1)}, bf16[1600,256]{1,0:T(8,128)(2,1)}, u32[]{:S(2)}) copy-start(bf16[1600,256]{1,0:T(8,128)(2,1)} %constant.2.clone.table) | copy-start | bytes 2457604
  15.0 0.7 %copy-start.5 = (f32[8,128]{1,0:T(8,128)S(1)}, f32[8,128]{1,0:T(8,128)}, u32[]{:S(2)}) copy-start(f32[8,128]{1,0:T(8,128)} %get-tuple-element.18.token) | copy-start | bytes 12292
  15.8 2.9 %collective-permute-start = (bf16[3,2,1024]{2,1,0:T(2,128)(2,1)S(1)}, bf16[3,2,1024]{2,1,0:T(2,128)(2,1)S(1)}, u32[]{:S(2)}, u32[]{:S(2)}) collective-permute-start(bf16[3,2,1024]{2,1,0:T(2,128)(2,1)S(1)} %get-tuple-element.19), channel_id=1, source_target_pairs={{0,4},{4,8},{8,12},{12,16},{16,20},{20,24},{24,28},{28,32},{32,36}... | collective-permute-start | bytes 36872 | tf_op jit(solution)/shard_map/ppermute | solution.py:358
  22.7 12.4 %all-to-all-start.1 = ((bf16[32,32,128]{2,1,0:T(8,128)(2,1)}), bf16[32,32,128]{2,1,0:T(8,128)(2,1)S(1)}, u32[]{:S(2)}, u32[]{:S(2)}) async-start(bf16[32,32,128]{2,1,0:T(8,128)(2,1)} %conv.1.token), calls=%async_computation.1 | async-start | bytes 524288 | tf_op jit(solution)/shard_map/all_to_all | solution.py:329
  30.6 1.1 %copy-start.1 = (bf16[128,3,1024]{2,0,1:T(8,128)(2,1)S(1)}, bf16[128,3,1024]{2,0,1:T(8,128)(2,1)}, u32[]{:S(2)}) copy-start(bf16[128,3,1024]{2,0,1:T(8,128)(2,1)} %param.6) | copy-start | bytes 2359300
  31.8 0.8 %copy-start.3 = (f32[3,3,1024]{2,1,0:T(4,128)S(1)}, f32[3,3,1024]{2,1,0:T(4,128)}, u32[]{:S(2)}) copy-start(f32[3,3,1024]{2,1,0:T(4,128)} %taps.3) | copy-start | bytes 110596
  32.6 0.7 %copy-start.4 = (f32[1024]{0:T(1024)S(1)}, f32[1024]{0:T(1024)}, u32[]{:S(2)}) copy-start(f32[1024]{0:T(1024)} %param.8) | copy-start | bytes 12292
  37.7 9.2 %collective-permute-start.2 = (bf16[128,1024]{1,0:T(8,128)(2,1)S(1)}, bf16[128,1024]{1,0:T(8,128)(2,1)S(1)}, u32[]{:S(2)}, u32[]{:S(2)}) collective-permute-start(bf16[128,1024]{1,0:T(8,128)(2,1)S(1)} %get-tuple-element.26), channel_id=1, source_target_pairs={{0,3},{1,0},{2,1},{3,2},{4,5},{5,6},{6,7},{7,4},{8,11},{9,8},{10,9... | collective-permute-start | bytes 786440 | tf_op jit(solution)/shard_map/ppermute | solution.py:374
  40.5 9.1 %collective-permute-start.1 = (bf16[128,1024]{1,0:T(8,128)(2,1)S(1)}, bf16[128,1024]{1,0:T(8,128)(2,1)S(1)}, u32[]{:S(2)}, u32[]{:S(2)}) collective-permute-start(bf16[128,1024]{1,0:T(8,128)(2,1)S(1)} %get-tuple-element.25), channel_id=1, source_target_pairs={{0,1},{1,2},{2,3},{3,0},{4,7},{5,4},{6,5},{7,6},{8,9},{9,10},{10,1... | collective-permute-start | bytes 786440 | tf_op jit(solution)/shard_map/ppermute | solution.py:371
  43.0 12.5 %collective-permute-start.4 = (bf16[128,1024]{1,0:T(8,128)(2,1)S(1)}, bf16[128,1024]{1,0:T(8,128)(2,1)S(1)}, u32[]{:S(2)}, u32[]{:S(2)}) collective-permute-start(bf16[128,1024]{1,0:T(8,128)(2,1)S(1)} %get-tuple-element.28), channel_id=1, source_target_pairs={{0,3},{1,0},{2,1},{3,2},{4,5},{5,6},{6,7},{7,4},{8,11},{9,8},{10,9... | collective-permute-start | bytes 786440 | tf_op jit(solution)/shard_map/ppermute | solution.py:374
  46.3 9.2 %collective-permute-start.5 = (bf16[128,1024]{1,0:T(8,128)(2,1)S(1)}, bf16[128,1024]{1,0:T(8,128)(2,1)S(1)}, u32[]{:S(2)}, u32[]{:S(2)}) collective-permute-start(bf16[128,1024]{1,0:T(8,128)(2,1)S(1)} %get-tuple-element.29), channel_id=1, source_target_pairs={{0,1},{1,2},{2,3},{3,0},{4,7},{5,4},{6,5},{7,6},{8,9},{9,10},{10,1... | collective-permute-start | bytes 786440 | tf_op jit(solution)/shard_map/ppermute | solution.py:371
  49.7 9.9 %collective-permute-start.3 = (bf16[128,1024]{1,0:T(8,128)(2,1)S(1)}, bf16[128,1024]{1,0:T(8,128)(2,1)S(1)}, u32[]{:S(2)}, u32[]{:S(2)}) collective-permute-start(bf16[128,1024]{1,0:T(8,128)(2,1)S(1)} %add.1), channel_id=1, source_target_pairs={{0,1},{1,2},{2,3},{3,0},{4,7},{5,4},{6,5},{7,6},{8,9},{9,10},{10,1... | collective-permute-start | bytes 786440 | tf_op jit(solution)/shard_map/ppermute | solution.py:371
  51.0 8.5 %collective-permute-start.6 = (bf16[128,1024]{1,0:T(8,128)(2,1)S(1)}, bf16[128,1024]{1,0:T(8,128)(2,1)S(1)}, u32[]{:S(2)}, u32[]{:S(2)}) collective-permute-start(bf16[128,1024]{1,0:T(8,128)(2,1)S(1)} %get-tuple-element.30), channel_id=1, source_target_pairs={{0,3},{1,0},{2,1},{3,2},{4,5},{5,6},{6,7},{7,4},{8,11},{9,8},{10,9... | collective-permute-start | bytes 786440 | tf_op jit(solution)/shard_map/ppermute | solution.py:374

commit v4 on v3

--- a/solution.py
+++ b/solution.py
@@ -100,13 +100,20 @@
     return both + tap(2) * jnp.where(row < 2, pltpu.roll(tail, 2, 0), 0.0)
 
 
-def mix_kernel(features, taps, long_filter, send, token, held, held_taps, held_filter, edges, sems):
+def mix_kernel(features, taps, long_filter, send, tail, token, held, held_last, held_taps, held_filter, edges, sems):
     width = held.shape[2]
+    last = held_last.shape[0]
     parts = send.shape[0]
     lanes = width // parts
     quarter = parts * GROUP
     copies = start_all(
-        [(long_filter, held_filter), (taps, held_taps), (features.at[1], held.at[0]), (features.at[2], held.at[1])],
+        [
+            (long_filter, held_filter),
+            (taps, held_taps),
+            (features.at[1], held.at[0]),
+            (features.at[2], held.at[1]),
+            (features.at[0, pl.ds(features.shape[1] - last, last)], held_last),
+        ],
         sems,
     )
     edges[...] = jnp.zeros_like(edges)
@@ -116,6 +123,9 @@
         store_turned(send, 0, held_filter[:, start : start + 128], start)
     for copy in copies[1:]:
         copy.wait()
+    rows = tail.shape[1]
+    tail[0] = held_last[last - rows :]
+    tail[1:] = held[:, held.shape[1] - rows :]
     row = lax.broadcasted_iota(jnp.int32, (8, 128), 0)
     for start in range(0, width, 128):
         columns = slice(start, start + 128)
@@ -135,13 +145,9 @@
         store_turned(send, 2 * lanes, edges[:, start : start + 128], start)
 
 
-def tail_kernel(token, table, features, table_out, tail, held, sems):
+def table_kernel(token, table, out, sems):
     del token
-    rows = held.shape[1]
-    pairs = [(table, table_out), (features.at[:, pl.ds(features.shape[1] - rows, rows), :], held)]
-    for copy in start_all(pairs, sems):
-        copy.wait()
-    tail[...] = held[:, rows - tail.shape[1] :, :]
+    start_all([(table, out)], sems)[0].wait()
 
 
 def terms_kernel(token, features, taps, skip, prior, query, direct, held, held_taps, held_skip, sems):
@@ -162,15 +168,20 @@
     return received[:, row : row + GROUP, :].astype(jnp.float32).reshape(blocks * GROUP, length)
 
 
-def patched(signal, edge, index, order):
+def whole_edges(edge, order):
     length = edge.shape[1]
     nothing = jnp.zeros((GROUP, length), jnp.float32)
     at = lambda block: edge[order.index(block) * GROUP : (order.index(block) + 1) * GROUP]
     before = jnp.concatenate([at(block - 1) if block else nothing for block in order], axis=0)
-    joined = pltpu.roll(edge, (length - 8 * index) % length, 1) + pltpu.roll(before, length - 8 * index - 4, 1)
-    whole_edge = joined * pltpu.roll(joined, length - 2, 1)
-    lane = lax.broadcasted_iota(jnp.int32, edge.shape, 1)
-    return jnp.where(lane < 2, whole_edge, signal)
+    joined = edge + pltpu.roll(before, length - 4, 1)
+    return joined * pltpu.roll(joined, length - 2, 1)
+
+
+def patched(signal, edges, index):
+    if index:
+        edges = pltpu.roll(edges, signal.shape[1] - 8 * index, 1)
+    lane = lax.broadcasted_iota(jnp.int32, signal.shape, 1)
+    return jnp.where(lane < 2, edges, signal)
 
 
 def spectrum(groups, ahead, inner_ahead, cosine, sine):
@@ -192,8 +203,8 @@
     ahead, (back_real, back_imag), inner_ahead, inner_back, cosine, sine = read_table(table, blocks, length)
     groups = [rows_of(received, i * GROUP).astype(jnp.bfloat16) for i in range(count)]
     other = spectrum(groups, ahead, inner_ahead, cosine, sine)
-    edge = rows_of(received, 2 * lanes)
-    groups = [patched(rows_of(received, lanes + i * GROUP), edge, i, order).astype(jnp.bfloat16) for i in range(count)]
+    edges = whole_edges(rows_of(received, 2 * lanes), order)
+    groups = [patched(rows_of(received, lanes + i * GROUP), edges, i).astype(jnp.bfloat16) for i in range(count)]
     part = spectrum(groups, ahead, inner_ahead, cosine, sine)
     xr, xi, hr, hi = part[:, :length], part[:, length:], other[:, :length], other[:, length:]
     joined = jnp.concatenate([xr * hr - xi * hi, xr * hi + xi * hr], axis=1)
@@ -331,31 +342,25 @@
     by_feature = jnp.transpose(features, (1, 0, 2))
     skip = skip_gain[None]
     sending = shape((members, 2 * lanes + GROUP, length), bf16)
-    send, token = call(
+    send, tail, token = call(
         mix_kernel,
-        (sending, shape((8, 128), f32)),
+        (sending, shape((3, 2, width), bf16), shape((8, 128), f32)),
         [away] * 3,
         "mix",
         [
             vmem((2, length, width), bf16),
+            vmem((TILE, width), bf16),
             vmem(short_taps.shape, f32),
             vmem((length, width), f32),
             vmem((length, members * GROUP), f32),
-            flags(4),
+            flags(5),
         ],
         mebibytes=60,
     )(by_feature, short_taps, long_filter)
     received = exchange(send)
+    prior = lax.ppermute(tail, "seq", [(i, i + 1) for i in range(members - 1)])
     table = transform_table(order, length)
-    table, tail = call(
-        tail_kernel,
-        (shape(table.shape, bf16), shape((3, 2, width), bf16)),
-        [inside, away, away],
-        "tail",
-        [vmem((3, TILE, width), bf16), flags(2)],
-        mebibytes=50,
-    )(token, table, by_feature)
-    prior = lax.ppermute(tail, "seq", [(i, i + 1) for i in range(members - 1)])
+    table = call(table_kernel, shape(table.shape, bf16), [inside, away], "table", [flags(1)])(token, table)
     spectral = call(functools.partial(conv_kernel, order), turned_shape, [loose] + [inside] * 2, "conv")(prior, table, received)
     conv = exchange(spectral)
 

time: 61.1 us -> 60.6 us (level)
  waiting for transfers between devices: 8.68 us -> 9.88 us
  local copies, waits for them, and re-layouts: 5.57 us -> 4.43 us
    all_to_all x2, waiting for transfers between devices: 3.07 us -> 5.09 us  [exchange(): lax.all_to_all(value, 'seq', 0, 0, axis_index_groups=[order], tiled=True)]
    unnamed x12 -> x10, local copies, waits for them, and re-layouts: 5.57 us -> 4.43 us
    ppermute x1, waiting for transfers between devices: 0.82 us -> 0.01 us  [shards(): prior = lax.ppermute(tail, 'seq', [(i, i + 1) for i in range(members - 1)])]
  transfers between devices with their start and end apart: 9 -> 9, of which waited for: 6 -> 5; matrix products, arithmetic and copies ran while one was open for 0% -> 0% of each run, Pallas kernels for 14% -> 14%
where the time goes in v4:
time: 60.6 us; the launch traced here: 60.1 us
  starting transfers between devices  29.1 us (48%)
  Pallas kernels  16.5 us (27%)
  waiting for transfers between devices  9.88 us (16%)
  local copies, waits for them, and re-layouts  4.43 us (7%)
    all_to_all x2, starting transfers between devices, exchange(): lax.all_to_all(value, 'seq', 0, 0, axis_index_groups=[order], tiled=True)  17.6 us
    ppermute x3, starting transfers between devices, behind(): return lax.ppermute(value, ('seq', 'chan'), route(-1))  8.06 us
    all_to_all x2, waiting for transfers between devices, exchange(): lax.all_to_all(value, 'seq', 0, 0, axis_index_groups=[order], tiled=True)  5.09 us
    pallas_call x2, Pallas kernels, pair(): call(kernel, (ahead_shape, behind_shape), [away] + [inside] * (1 + len(mo...  4.94 us
    unnamed x10, local copies, waits for them, and re-layouts  4.43 us
    ppermute x3, waiting for transfers between devices, ahead(): return lax.ppermute(value, ('seq', 'chan'), route(1))  4.18 us
    pallas_call x1, Pallas kernels, shards(): call(mix_kernel, (sending, shape((3, 2, width), bf16), shape((8, 128), f3...  2.58 us
    pallas_call x1, Pallas kernels, shards(): call(far_kernel, (shape((length, width), bf16), right, left), [away] + [i...  2.57 us
  transfers between devices with their start and end apart: 9, of which 5 were waited for; matrix products, arithmetic and copies ran while one was open for 0% of the time, Pallas kernels for 14%

profile of v4, /device:TPU:0, one launch (start us, length us, event | category | flops | bytes accessed | tf_op | source)
XLA Modules:
  0.0 60.1 jit_solution(5817376875970361880)
XLA Ops:
  0.0 2.6 %mix.1 = (bf16[32,72,128]{2,1,0:T(8,128)(2,1)}, bf16[3,2,1024]{2,1,0:T(2,128)(2,1)}, f32[8,128]{1,0:T(8,128)}) custom-call(bf16[3,128,1024]{2,1,0:T(8,128)(2,1)} %bitcast.2, f32[3,3,1024]{2,1,0:T(4,128)} %taps.3, f32[128,1024]{1,0:T(8,128)} %long_filter.1), custom_call_target="tpu_custom_call" | custom-call | tf_op jit(solution)/shard_map/mix/pallas_call | solution.py:345
  2.6 10.1 %all-to-all-start = ((bf16[32,72,128]{2,1,0:T(8,128)(2,1)}), bf16[32,72,128]{2,1,0:T(8,128)(2,1)S(1)}, u32[]{:S(2)}, u32[]{:S(2)}) async-start(bf16[32,72,128]{2,1,0:T(8,128)(2,1)} %get-tuple-element.19), calls=%async_computation | async-start | bytes 1179648 | tf_op jit(solution)/shard_map/all_to_all | solution.py:340
  12.7 2.1 %collective-permute-start = (bf16[3,2,1024]{2,1,0:T(2,128)(2,1)}, bf16[3,2,1024]{2,1,0:T(2,128)(2,1)S(1)}, u32[]{:S(2)}, u32[]{:S(2)}) collective-permute-start(bf16[3,2,1024]{2,1,0:T(2,128)(2,1)} %get-tuple-element.17), channel_id=1, source_target_pairs={{0,4},{4,8},{8,12},{12,16},{16,20},{20,24},{24,28},{28,32},{32,36}... | collective-permute-start | bytes 36872 | tf_op jit(solution)/shard_map/ppermute | solution.py:361
  14.8 0.0 copy-start.1
  14.8 1.1 %copy-done.1 = bf16[1600,256]{1,0:T(8,128)(2,1)S(1)} copy-done((bf16[1600,256]{1,0:T(8,128)(2,1)S(1)}, bf16[1600,256]{1,0:T(8,128)(2,1)}, u32[]{:S(2)}) %copy-start.1) | copy-done | bytes 819224
  15.9 0.0 copy-start.4
  15.9 0.7 %copy-done.4 = f32[8,128]{1,0:T(8,128)S(1)} copy-done((f32[8,128]{1,0:T(8,128)S(1)}, f32[8,128]{1,0:T(8,128)}, u32[]{:S(2)}) %copy-start.4) | copy-done | bytes 4120
  16.6 0.1 table.2
  16.7 0.0 collective-permute-done.token.prior
  16.7 4.0 %all-to-all-done.received = bf16[32,72,128]{2,1,0:T(8,128)(2,1)S(1)} async-done(((bf16[32,72,128]{2,1,0:T(8,128)(2,1)}), bf16[32,72,128]{2,1,0:T(8,128)(2,1)S(1)}, u32[]{:S(2)}, u32[]{:S(2)}) %all-to-all-start) | async-done | bytes 589856 | tf_op jit(solution)/shard_map/all_to_all | solution.py:340
  20.7 2.1 %conv.1.token = bf16[32,32,128]{2,1,0:T(8,128)(2,1)} custom-call(bf16[3,2,1024]{2,1,0:T(2,128)(2,1)S(1)} %collective-permute-done.token.prior, bf16[1600,256]{1,0:T(8,128)(2,1)S(1)} %table.2, bf16[32,72,128]{2,1,0:T(8,128)(2,1)S(1)} %all-to-all-done.received), custom_call_target="tpu_custom_call" | custom-call | tf_op jit(solution)/shard_map/conv/pallas_call | solution.py:364
  22.8 7.5 %all-to-all-start.1 = ((bf16[32,32,128]{2,1,0:T(8,128)(2,1)}), bf16[32,32,128]{2,1,0:T(8,128)(2,1)S(1)}, u32[]{:S(2)}, u32[]{:S(2)}) async-start(bf16[32,32,128]{2,1,0:T(8,128)(2,1)} %conv.1.token), calls=%async_computation.1 | async-start | bytes 524288 | tf_op jit(solution)/shard_map/all_to_all | solution.py:340
  30.3 0.0 copy-start
  30.3 1.1 %copy-done = bf16[128,3,1024]{2,0,1:T(8,128)(2,1)S(1)} copy-done((bf16[128,3,1024]{2,0,1:T(8,128)(2,1)S(1)}, bf16[128,3,1024]{2,0,1:T(8,128)(2,1)}, u32[]{:S(2)}) %copy-start) | copy-done | bytes 786456
  31.4 0.0 copy-start.2
  31.4 0.8 %copy-done.2 = f32[3,3,1024]{2,1,0:T(4,128)S(1)} copy-done((f32[3,3,1024]{2,1,0:T(4,128)S(1)}, f32[3,3,1024]{2,1,0:T(4,128)}, u32[]{:S(2)}) %copy-start.2) | copy-done | bytes 36888
  32.2 0.0 copy-start.3
  32.2 0.7 %copy-done.3 = f32[1024]{0:T(1024)S(1)} copy-done((f32[1024]{0:T(1024)S(1)}, f32[1024]{0:T(1024)}, u32[]{:S(2)}) %copy-start.3) | copy-done | bytes 4120
  32.9 0.7 %terms.1 = (bf16[128,1024]{1,0:T(8,128)(2,1)S(1)}, bf16[128,1024]{1,0:T(8,128)(2,1)S(1)}) custom-call(bf16[32,32,128]{2,1,0:T(8,128)(2,1)} %conv.1.token, bf16[3,128,1024]{2,1,0:T(8,128)(2,1)S(1)} %bitcast.3, f32[3,3,1024]{2,1,0:T(4,128)S(1)} %copy-done.2, f32[1,1024]{1,0:T(1,128)S(1)} %bitcast.4, bf16[3,2,1024]{2,1,0:T(2,128)(2,1)S(1)} %collective-permute-done.token.prior), custom_call_target="tpu_custom_call" | custom-call | tf_op jit(solution)/shard_map/terms/pallas_call | solution.py:385
  33.6 1.1 %all-to-all-done.1.conv = bf16[32,32,128]{2,1,0:T(8,128)(2,1)S(1)} async-done(((bf16[32,32,128]{2,1,0:T(8,128)(2,1)}), bf16[32,32,128]{2,1,0:T(8,128)(2,1)S(1)}, u32[]{:S(2)}, u32[]{:S(2)}) %all-to-all-start.1) | async-done | bytes 262176 | tf_op jit(solution)/shard_map/all_to_all | solution.py:340
  34.7 2.6 %far.1 = (bf16[128,1024]{1,0:T(8,128)(2,1)S(1)}, bf16[128,1024]{1,0:T(8,128)(2,1)S(1)}, bf16[128,1024]{1,0:T(8,128)(2,1)S(1)}) custom-call(bf16[1024,8192]{1,0:T(8,128)(2,1)} %weight.7, bf16[128,1024]{1,0:T(8,128)(2,1)S(1)} %get-tuple-element.20.query, bf16[128,1024]{1,0:T(8,128)(2,1)S(1)} %get-tuple-element.21.direct, ...), custom_call_target="tpu_custom_call" | custom-call | tf_op jit(solution)/shard_map/far/pallas_call | solution.py:393
  37.3 2.8 %collective-permute-start.2 = (bf16[128,1024]{1,0:T(8,128)(2,1)S(1)}, bf16[128,1024]{1,0:T(8,128)(2,1)S(1)}, u32[]{:S(2)}, u32[]{:S(2)}) collective-permute-start(bf16[128,1024]{1,0:T(8,128)(2,1)S(1)} %get-tuple-element.24), channel_id=1, source_target_pairs={{0,3},{1,0},{2,1},{3,2},{4,5},{5,6},{6,7},{7,4},{8,11},{9,8},{10,9... | collective-permute-start | bytes 786440 | tf_op jit(solution)/shard_map/ppermute | solution.py:379
  40.1 0.0 collective-permute-start.1
  40.1 2.5 %near.1 = (bf16[128,1024]{1,0:T(8,128)(2,1)S(1)}, bf16[128,1024]{1,0:T(8,128)(2,1)S(1)}) custom-call(bf16[1024,8192]{1,0:T(8,128)(2,1)} %weight.7, bf16[128,1024]{1,0:T(8,128)(2,1)S(1)} %get-tuple-element.22.gated), custom_call_target="tpu_custom_call" | custom-call | tf_op jit(solution)/shard_map/near/pallas_call | solution.py:405
  42.6 3.3 %collective-permute-start.4 = (bf16[128,1024]{1,0:T(8,128)(2,1)S(1)}, bf16[128,1024]{1,0:T(8,128)(2,1)S(1)}, u32[]{:S(2)}, u32[]{:S(2)}) collective-permute-start(bf16[128,1024]{1,0:T(8,128)(2,1)S(1)} %get-tuple-element.26), channel_id=1, source_target_pairs={{0,3},{1,0},{2,1},{3,2},{4,5},{5,6},{6,7},{7,4},{8,11},{9,8},{10,9... | collective-permute-start | bytes 786440 | tf_op jit(solution)/shard_map/ppermute | solution.py:379
  45.9 0.0 collective-permute-start.5
  45.9 0.6 %collective-permute-done.2.got = bf16[128,1024]{1,0:T(8,128)(2,1)S(1)} collective-permute-done((bf16[128,1024]{1,0:T(8,128)(2,1)S(1)}, bf16[128,1024]{1,0:T(8,128)(2,1)S(1)}, u32[]{:S(2)}, u32[]{:S(2)}) %collective-permute-start.2) | collective-permute-done | bytes 262176 | tf_op jit(solution)/shard_map/ppermute | solution.py:379
  46.5 2.5 %joined.1 = (bf16[128,1024]{1,0:T(8,128)(2,1)S(1)}, bf16[128,1024]{1,0:T(8,128)(2,1)S(1)}) custom-call(bf16[1024,8192]{1,0:T(8,128)(2,1)} %weight.7, bf16[128,1024]{1,0:T(8,128)(2,1)S(1)} %get-tuple-element.22.gated, bf16[128,1024]{1,0:T(8,128)(2,1)S(1)} %collective-permute-done.2.got), custom_call_target="tpu_custom_call" | custom-call | tf_op jit(solution)/shard_map/joined/pallas_call | solution.py:405
  49.0 0.2 collective-permute-done.1.one
  49.2 0.1 add.1
  49.3 1.4 %collective-permute-start.3 = (bf16[128,1024]{1,0:T(8,128)(2,1)S(1)}, bf16[128,1024]{1,0:T(8,128)(2,1)S(1)}, u32[]{:S(2)}, u32[]{:S(2)}) collective-permute-start(bf16[128,1024]{1,0:T(8,128)(2,1)S(1)} %add.1), channel_id=1, source_target_pairs={{0,1},{1,2},{2,3},{3,0},{4,7},{5,4},{6,5},{7,6},{8,9},{9,10},{10,1... | collective-permute-start | bytes 786440 | tf_op jit(solution)/shard_map/ppermute | solution.py:376
  50.6 1.9 %collective-permute-start.6 = (bf16[128,1024]{1,0:T(8,128)(2,1)S(1)}, bf16[128,1024]{1,0:T(8,128)(2,1)S(1)}, u32[]{:S(2)}, u32[]{:S(2)}) collective-permute-start(bf16[128,1024]{1,0:T(8,128)(2,1)S(1)} %get-tuple-element.28), channel_id=1, source_target_pairs={{0,3},{1,0},{2,1},{3,2},{4,5},{5,6},{6,7},{7,4},{8,11},{9,8},{10,9... | collective-permute-start | bytes 786440 | tf_op jit(solution)/shard_map/ppermute | solution.py:379
  52.6 2.5 %own.1 = f32[128,2048]{1,0:T(8,128)S(1)} custom-call(bf16[1024,8192]{1,0:T(8,128)(2,1)} %weight.7, bf16[128,1024]{1,0:T(8,128)(2,1)S(1)} %get-tuple-element.22.gated), custom_call_target="tpu_custom_call" | custom-call | tf_op jit(solution)/shard_map/own/pallas_call | solution.py:419
  55.1 0.0 collective-permute-done.4.first_two
  55.1 0.0 collective-permute-done.5.second_one
  55.1 4.0 %collective-permute-done.3.first_one = bf16[128,1024]{1,0:T(8,128)(2,1)S(1)} collective-permute-done((bf16[128,1024]{1,0:T(8,128)(2,1)S(1)}, bf16[128,1024]{1,0:T(8,128)(2,1)S(1)}, u32[]{:S(2)}, u32[]{:S(2)}) %collective-permute-start.3) | collective-permute-done | bytes 262176 | tf_op jit(solution)/shard_map/ppermute | solution.py:376
  59.1 0.0 collective-permute-done.6.second_two
  59.1 0.9 %last.1 = bf16[128,2048]{1,0:T(8,128)(2,1)} custom-call(f32[128,2048]{1,0:T(8,128)S(1)} %own.1, bf16[128,1024]{1,0:T(8,128)(2,1)S(1)} %collective-permute-done.3.first_one, bf16[128,1024]{1,0:T(8,128)(2,1)S(1)} %collective-permute-done.4.first_two, bf16[128,1024]{1,0:T(8,128)(2,1)S(1)} %collective-permute-done.5.second_one, ...), custom_call_target="tpu_custom_call" | custom-call | tf_op jit(solution)/shard_map/last/pallas_call | solution.py:423
Async XLA Ops:
  2.6 18.1 %all-to-all-start = ((bf16[32,72,128]{2,1,0:T(8,128)(2,1)}), bf16[32,72,128]{2,1,0:T(8,128)(2,1)S(1)}, u32[]{:S(2)}, u32[]{:S(2)}) async-start(bf16[32,72,128]{2,1,0:T(8,128)(2,1)} %get-tuple-element.19), calls=%async_computation | async-start | bytes 1179648 | tf_op jit(solution)/shard_map/all_to_all | solution.py:340
  12.7 4.0 %collective-permute-start = (bf16[3,2,1024]{2,1,0:T(2,128)(2,1)}, bf16[3,2,1024]{2,1,0:T(2,128)(2,1)S(1)}, u32[]{:S(2)}, u32[]{:S(2)}) collective-permute-start(bf16[3,2,1024]{2,1,0:T(2,128)(2,1)} %get-tuple-element.17), channel_id=1, source_target_pairs={{0,4},{4,8},{8,12},{12,16},{16,20},{20,24},{24,28},{28,32},{32,36}... | collective-permute-start | bytes 36872 | tf_op jit(solution)/shard_map/ppermute | solution.py:361
  14.8 1.1 %copy-start.1 = (bf16[1600,256]{1,0:T(8,128)(2,1)S(1)}, bf16[1600,256]{1,0:T(8,128)(2,1)}, u32[]{:S(2)}) copy-start(bf16[1600,256]{1,0:T(8,128)(2,1)} %constant.2.clone.table) | copy-start | bytes 2457604
  15.9 0.7 %copy-start.4 = (f32[8,128]{1,0:T(8,128)S(1)}, f32[8,128]{1,0:T(8,128)}, u32[]{:S(2)}) copy-start(f32[8,128]{1,0:T(8,128)} %get-tuple-element.18.token) | copy-start | bytes 12292
  22.8 12.0 %all-to-all-start.1 = ((bf16[32,32,128]{2,1,0:T(8,128)(2,1)}), bf16[32,32,128]{2,1,0:T(8,128)(2,1)S(1)}, u32[]{:S(2)}, u32[]{:S(2)}) async-start(bf16[32,32,128]{2,1,0:T(8,128)(2,1)} %conv.1.token), calls=%async_computation.1 | async-start | bytes 524288 | tf_op jit(solution)/shard_map/all_to_all | solution.py:340
  30.3 1.1 %copy-start = (bf16[128,3,1024]{2,0,1:T(8,128)(2,1)S(1)}, bf16[128,3,1024]{2,0,1:T(8,128)(2,1)}, u32[]{:S(2)}) copy-start(bf16[128,3,1024]{2,0,1:T(8,128)(2,1)} %param.6) | copy-start | bytes 2359300
  31.4 0.8 %copy-start.2 = (f32[3,3,1024]{2,1,0:T(4,128)S(1)}, f32[3,3,1024]{2,1,0:T(4,128)}, u32[]{:S(2)}) copy-start(f32[3,3,1024]{2,1,0:T(4,128)} %taps.3) | copy-start | bytes 110596
  32.2 0.7 %copy-start.3 = (f32[1024]{0:T(1024)S(1)}, f32[1024]{0:T(1024)}, u32[]{:S(2)}) copy-start(f32[1024]{0:T(1024)} %param.8) | copy-start | bytes 12292
  37.3 9.2 %collective-permute-start.2 = (bf16[128,1024]{1,0:T(8,128)(2,1)S(1)}, bf16[128,1024]{1,0:T(8,128)(2,1)S(1)}, u32[]{:S(2)}, u32[]{:S(2)}) collective-permute-start(bf16[128,1024]{1,0:T(8,128)(2,1)S(1)} %get-tuple-element.24), channel_id=1, source_target_pairs={{0,3},{1,0},{2,1},{3,2},{4,5},{5,6},{6,7},{7,4},{8,11},{9,8},{10,9... | collective-permute-start | bytes 786440 | tf_op jit(solution)/shard_map/ppermute | solution.py:379
  40.1 9.1 %collective-permute-start.1 = (bf16[128,1024]{1,0:T(8,128)(2,1)S(1)}, bf16[128,1024]{1,0:T(8,128)(2,1)S(1)}, u32[]{:S(2)}, u32[]{:S(2)}) collective-permute-start(bf16[128,1024]{1,0:T(8,128)(2,1)S(1)} %get-tuple-element.23), channel_id=1, source_target_pairs={{0,1},{1,2},{2,3},{3,0},{4,7},{5,4},{6,5},{7,6},{8,9},{9,10},{10,1... | collective-permute-start | bytes 786440 | tf_op jit(solution)/shard_map/ppermute | solution.py:376
  42.6 12.5 %collective-permute-start.4 = (bf16[128,1024]{1,0:T(8,128)(2,1)S(1)}, bf16[128,1024]{1,0:T(8,128)(2,1)S(1)}, u32[]{:S(2)}, u32[]{:S(2)}) collective-permute-start(bf16[128,1024]{1,0:T(8,128)(2,1)S(1)} %get-tuple-element.26), channel_id=1, source_target_pairs={{0,3},{1,0},{2,1},{3,2},{4,5},{5,6},{6,7},{7,4},{8,11},{9,8},{10,9... | collective-permute-start | bytes 786440 | tf_op jit(solution)/shard_map/ppermute | solution.py:379
  45.9 9.2 %collective-permute-start.5 = (bf16[128,1024]{1,0:T(8,128)(2,1)S(1)}, bf16[128,1024]{1,0:T(8,128)(2,1)S(1)}, u32[]{:S(2)}, u32[]{:S(2)}) collective-permute-start(bf16[128,1024]{1,0:T(8,128)(2,1)S(1)} %get-tuple-element.27), channel_id=1, source_target_pairs={{0,1},{1,2},{2,3},{3,0},{4,7},{5,4},{6,5},{7,6},{8,9},{9,10},{10,1... | collective-permute-start | bytes 786440 | tf_op jit(solution)/shard_map/ppermute | solution.py:376
  49.3 9.8 %collective-permute-start.3 = (bf16[128,1024]{1,0:T(8,128)(2,1)S(1)}, bf16[128,1024]{1,0:T(8,128)(2,1)S(1)}, u32[]{:S(2)}, u32[]{:S(2)}) collective-permute-start(bf16[128,1024]{1,0:T(8,128)(2,1)S(1)} %add.1), channel_id=1, source_target_pairs={{0,1},{1,2},{2,3},{3,0},{4,7},{5,4},{6,5},{7,6},{8,9},{9,10},{10,1... | collective-permute-start | bytes 786440 | tf_op jit(solution)/shard_map/ppermute | solution.py:376
  50.6 8.5 %collective-permute-start.6 = (bf16[128,1024]{1,0:T(8,128)(2,1)S(1)}, bf16[128,1024]{1,0:T(8,128)(2,1)S(1)}, u32[]{:S(2)}, u32[]{:S(2)}) collective-permute-start(bf16[128,1024]{1,0:T(8,128)(2,1)S(1)} %get-tuple-element.28), channel_id=1, source_target_pairs={{0,3},{1,0},{2,1},{3,2},{4,5},{5,6},{6,7},{7,4},{8,11},{9,8},{10,9... | collective-permute-start | bytes 786440 | tf_op jit(solution)/shard_map/ppermute | solution.py:379

commit v5 on v4

--- a/solution.py
+++ b/solution.py
@@ -100,7 +100,10 @@
     return both + tap(2) * jnp.where(row < 2, pltpu.roll(tail, 2, 0), 0.0)
 
 
-def mix_kernel(features, taps, long_filter, send, tail, token, held, held_last, held_taps, held_filter, edges, sems):
+def mix_kernel(
+    features, taps, long_filter, send_out, tail_out, send, tail, held, held_last, held_taps,
+    held_filter, edges, sems
+):
     width = held.shape[2]
     last = held_last.shape[0]
     parts = send.shape[0]
@@ -117,10 +120,11 @@
         sems,
     )
     edges[...] = jnp.zeros_like(edges)
-    token[...] = jnp.zeros_like(token)
     copies[0].wait()
     for start in range(0, width, 128):
         store_turned(send, 0, held_filter[:, start : start + 128], start)
+    outs = [pltpu.make_async_copy(send.at[:, pl.ds(0, lanes)], send_out.at[:, pl.ds(0, lanes)], sems.at[5])]
+    outs[0].start()
     for copy in copies[1:]:
         copy.wait()
     rows = tail.shape[1]
@@ -143,6 +147,13 @@
         edges[top : top + 8, start % quarter : start % quarter + 128] = stack
     for start in range(0, quarter, 128):
         store_turned(send, 2 * lanes, edges[:, start : start + 128], start)
+    rest = pl.ds(lanes, send.shape[1] - lanes)
+    outs.append(pltpu.make_async_copy(send.at[:, rest], send_out.at[:, rest], sems.at[6]))
+    outs.append(pltpu.make_async_copy(tail, tail_out, sems.at[7]))
+    for copy in outs[1:]:
+        copy.start()
+    for copy in outs:
+        copy.wait()
 
 
 def table_kernel(token, table, out, sems):
@@ -298,11 +309,18 @@
     out[...] = (one[...].astype(jnp.float32) + two[...].astype(jnp.float32)).astype(jnp.bfloat16)
 
 
-def last_kernel(own, first_one, first_two, second_one, second_two, out):
+def last_kernel(own, first_one, first_two, second_one, second_two, out, held, sems):
     split = second_one.shape[1]
     wide = lambda ref: ref[...].astype(jnp.float32)
-    out[:, :split] = (own[:, :split] + wide(second_one) + wide(second_two)).astype(jnp.bfloat16)
-    out[:, split:] = (own[:, split:] + wide(first_one) + wide(first_two)).astype(jnp.bfloat16)
+    held[:, :split] = (own[:, :split] + wide(second_one) + wide(second_two)).astype(jnp.bfloat16)
+    left = pltpu.make_async_copy(held.at[:, pl.ds(0, split)], out.at[:, pl.ds(0, split)], sems.at[0])
+    left.start()
+    held[:, split:] = (own[:, split:] + wide(first_one) + wide(first_two)).astype(jnp.bfloat16)
+    rest = pl.ds(split, out.shape[1] - split)
+    right = pltpu.make_async_copy(held.at[:, rest], out.at[:, rest], sems.at[1])
+    right.start()
+    left.wait()
+    right.wait()
 
 
 def call(kernel, outs, specs, name, scratch=(), out_specs=None, mebibytes=16):
@@ -342,25 +360,28 @@
     by_feature = jnp.transpose(features, (1, 0, 2))
     skip = skip_gain[None]
     sending = shape((members, 2 * lanes + GROUP, length), bf16)
-    send, tail, token = call(
+    send, tail = call(
         mix_kernel,
-        (sending, shape((3, 2, width), bf16), shape((8, 128), f32)),
+        (sending, shape((3, 2, width), bf16)),
         [away] * 3,
         "mix",
         [
+            vmem(sending.shape, bf16),
+            vmem((3, 2, width), bf16),
             vmem((2, length, width), bf16),
             vmem((TILE, width), bf16),
             vmem(short_taps.shape, f32),
             vmem((length, width), f32),
             vmem((length, members * GROUP), f32),
-            flags(5),
+            flags(8),
         ],
-        mebibytes=60,
+        (away,) * 2,
+        60,
     )(by_feature, short_taps, long_filter)
     received = exchange(send)
     prior = lax.ppermute(tail, "seq", [(i, i + 1) for i in range(members - 1)])
     table = transform_table(order, length)
-    table = call(table_kernel, shape(table.shape, bf16), [inside, away], "table", [flags(1)])(token, table)
+    table = call(table_kernel, shape(table.shape, bf16), [loose, away], "table", [flags(1)])(tail, table)
     spectral = call(functools.partial(conv_kernel, order), turned_shape, [loose] + [inside] * 2, "conv")(prior, table, received)
     conv = exchange(spectral)
 
@@ -420,7 +441,8 @@
         own_kernel, shape((length, size), f32), [away, inside], "own", [chunk, flags(pieces)], mebibytes=48
     )(out_weight, gated)
     first_got = ahead(call(add_kernel, right, [inside] * 2, "add")(got_first, ahead_held))
-    return call(last_kernel, shape((length, size), bf16), [inside] * 5, "last")(
+    out = shape((length, size), bf16)
+    return call(last_kernel, out, [inside] * 5, "last", [vmem(out.shape, bf16), flags(2)], away)(
         own, first_got, behind_got, ahead_got, second_got
     )
 

time: 60.6 us -> 60.5 us (level)
  no operation moved by 1% of the time
where the time goes in v5:
time: 60.5 us; the launch traced here: 60 us
  starting transfers between devices  29.1 us (48%)
  Pallas kernels  16.4 us (27%)
  waiting for transfers between devices  9.86 us (16%)
  local copies, waits for them, and re-layouts  4.46 us (7%)
    all_to_all x2, starting transfers between devices, exchange(): lax.all_to_all(value, 'seq', 0, 0, axis_index_groups=[order], tiled=True)  17.6 us
    ppermute x3, starting transfers between devices, behind(): return lax.ppermute(value, ('seq', 'chan'), route(-1))  8.08 us
    all_to_all x2, waiting for transfers between devices, exchange(): lax.all_to_all(value, 'seq', 0, 0, axis_index_groups=[order], tiled=True)  5.06 us
    pallas_call x2, Pallas kernels, pair(): call(kernel, (ahead_shape, behind_shape), [away] + [inside] * (1 + len(mo...  4.94 us
    unnamed x10, local copies, waits for them, and re-layouts  4.46 us
    ppermute x3, waiting for transfers between devices, ahead(): return lax.ppermute(value, ('seq', 'chan'), route(1))  4.2 us
    pallas_call x1, Pallas kernels, shards(): call(far_kernel, (shape((length, width), bf16), right, left), [away] + [i...  2.56 us
    pallas_call x1, Pallas kernels, shards(): call(mix_kernel, (sending, shape((3, 2, width), bf16)), [away] * 3, 'mix'...  2.54 us
  transfers between devices with their start and end apart: 9, of which 5 were waited for; matrix products, arithmetic and copies ran while one was open for 0% of the time, Pallas kernels for 14%

profile of v5, /device:TPU:0, one launch (start us, length us, event | category | flops | bytes accessed | tf_op | source)
XLA Modules:
  0.0 60.0 jit_solution(10064000922463891841)
XLA Ops:
  0.0 2.5 %mix.1 = (bf16[32,72,128]{2,1,0:T(8,128)(2,1)}, bf16[3,2,1024]{2,1,0:T(2,128)(2,1)}) custom-call(bf16[3,128,1024]{2,1,0:T(8,128)(2,1)} %bitcast.2, f32[3,3,1024]{2,1,0:T(4,128)} %taps.3, f32[128,1024]{1,0:T(8,128)} %long_filter.1), custom_call_target="tpu_custom_call" | custom-call | tf_op jit(solution)/shard_map/mix/pallas_call | solution.py:363
  2.6 10.1 %all-to-all-start = ((bf16[32,72,128]{2,1,0:T(8,128)(2,1)}), bf16[32,72,128]{2,1,0:T(8,128)(2,1)S(1)}, u32[]{:S(2)}, u32[]{:S(2)}) async-start(bf16[32,72,128]{2,1,0:T(8,128)(2,1)} %get-tuple-element.17), calls=%async_computation | async-start | bytes 1179648 | tf_op jit(solution)/shard_map/all_to_all | solution.py:358
  12.7 2.1 %collective-permute-start = (bf16[3,2,1024]{2,1,0:T(2,128)(2,1)}, bf16[3,2,1024]{2,1,0:T(2,128)(2,1)S(1)}, u32[]{:S(2)}, u32[]{:S(2)}) collective-permute-start(bf16[3,2,1024]{2,1,0:T(2,128)(2,1)} %get-tuple-element.16.token), channel_id=1, source_target_pairs={{0,4},{4,8},{8,12},{12,16},{16,20},{20,24},{24,28},{28,32},{32,36}... | collective-permute-start | bytes 36872 | tf_op jit(solution)/shard_map/ppermute | solution.py:382
  14.7 0.0 copy-start.1
  14.7 1.1 %copy-done.1 = bf16[1600,256]{1,0:T(8,128)(2,1)S(1)} copy-done((bf16[1600,256]{1,0:T(8,128)(2,1)S(1)}, bf16[1600,256]{1,0:T(8,128)(2,1)}, u32[]{:S(2)}) %copy-start.1) | copy-done | bytes 819224
  15.9 0.0 copy-start.3
  15.9 0.7 %copy-done.3 = bf16[3,2,1024]{2,1,0:T(2,128)(2,1)S(1)} copy-done((bf16[3,2,1024]{2,1,0:T(2,128)(2,1)S(1)}, bf16[3,2,1024]{2,1,0:T(2,128)(2,1)}, u32[]{:S(2)}) %copy-start.3) | copy-done | bytes 12312
  16.6 0.1 table.2
  16.7 0.0 collective-permute-done.token.prior
  16.7 4.0 %all-to-all-done.received = bf16[32,72,128]{2,1,0:T(8,128)(2,1)S(1)} async-done(((bf16[32,72,128]{2,1,0:T(8,128)(2,1)}), bf16[32,72,128]{2,1,0:T(8,128)(2,1)S(1)}, u32[]{:S(2)}, u32[]{:S(2)}) %all-to-all-start) | async-done | bytes 589856 | tf_op jit(solution)/shard_map/all_to_all | solution.py:358
  20.6 2.1 %conv.1.token = bf16[32,32,128]{2,1,0:T(8,128)(2,1)} custom-call(bf16[3,2,1024]{2,1,0:T(2,128)(2,1)S(1)} %collective-permute-done.token.prior, bf16[1600,256]{1,0:T(8,128)(2,1)S(1)} %table.2, bf16[32,72,128]{2,1,0:T(8,128)(2,1)S(1)} %all-to-all-done.received), custom_call_target="tpu_custom_call" | custom-call | tf_op jit(solution)/shard_map/conv/pallas_call | solution.py:385
  22.7 7.5 %all-to-all-start.1 = ((bf16[32,32,128]{2,1,0:T(8,128)(2,1)}), bf16[32,32,128]{2,1,0:T(8,128)(2,1)S(1)}, u32[]{:S(2)}, u32[]{:S(2)}) async-start(bf16[32,32,128]{2,1,0:T(8,128)(2,1)} %conv.1.token), calls=%async_computation.1 | async-start | bytes 524288 | tf_op jit(solution)/shard_map/all_to_all | solution.py:358
  30.2 0.0 copy-start
  30.2 1.1 %copy-done = bf16[128,3,1024]{2,0,1:T(8,128)(2,1)S(1)} copy-done((bf16[128,3,1024]{2,0,1:T(8,128)(2,1)S(1)}, bf16[128,3,1024]{2,0,1:T(8,128)(2,1)}, u32[]{:S(2)}) %copy-start) | copy-done | bytes 786456
  31.4 0.0 copy-start.2
  31.4 0.8 %copy-done.2 = f32[3,3,1024]{2,1,0:T(4,128)S(1)} copy-done((f32[3,3,1024]{2,1,0:T(4,128)S(1)}, f32[3,3,1024]{2,1,0:T(4,128)}, u32[]{:S(2)}) %copy-start.2) | copy-done | bytes 36888
  32.2 0.0 copy-start.4
  32.2 0.7 %copy-done.4 = f32[1024]{0:T(1024)S(1)} copy-done((f32[1024]{0:T(1024)S(1)}, f32[1024]{0:T(1024)}, u32[]{:S(2)}) %copy-start.4) | copy-done | bytes 4120
  32.8 0.7 %terms.1 = (bf16[128,1024]{1,0:T(8,128)(2,1)S(1)}, bf16[128,1024]{1,0:T(8,128)(2,1)S(1)}) custom-call(bf16[32,32,128]{2,1,0:T(8,128)(2,1)} %conv.1.token, bf16[3,128,1024]{2,1,0:T(8,128)(2,1)S(1)} %bitcast.3, f32[3,3,1024]{2,1,0:T(4,128)S(1)} %copy-done.2, f32[1,1024]{1,0:T(1,128)S(1)} %bitcast.4, bf16[3,2,1024]{2,1,0:T(2,128)(2,1)S(1)} %collective-permute-done.token.prior), custom_call_target="tpu_custom_call" | custom-call | tf_op jit(solution)/shard_map/terms/pallas_call | solution.py:406
  33.6 1.1 %all-to-all-done.1.conv = bf16[32,32,128]{2,1,0:T(8,128)(2,1)S(1)} async-done(((bf16[32,32,128]{2,1,0:T(8,128)(2,1)}), bf16[32,32,128]{2,1,0:T(8,128)(2,1)S(1)}, u32[]{:S(2)}, u32[]{:S(2)}) %all-to-all-start.1) | async-done | bytes 262176 | tf_op jit(solution)/shard_map/all_to_all | solution.py:358
  34.7 2.6 %far.1 = (bf16[128,1024]{1,0:T(8,128)(2,1)S(1)}, bf16[128,1024]{1,0:T(8,128)(2,1)S(1)}, bf16[128,1024]{1,0:T(8,128)(2,1)S(1)}) custom-call(bf16[1024,8192]{1,0:T(8,128)(2,1)} %weight.7, bf16[128,1024]{1,0:T(8,128)(2,1)S(1)} %get-tuple-element.18.query, bf16[128,1024]{1,0:T(8,128)(2,1)S(1)} %get-tuple-element.19.direct, ...), custom_call_target="tpu_custom_call" | custom-call | tf_op jit(solution)/shard_map/far/pallas_call | solution.py:414
  37.3 2.8 %collective-permute-start.2 = (bf16[128,1024]{1,0:T(8,128)(2,1)S(1)}, bf16[128,1024]{1,0:T(8,128)(2,1)S(1)}, u32[]{:S(2)}, u32[]{:S(2)}) collective-permute-start(bf16[128,1024]{1,0:T(8,128)(2,1)S(1)} %get-tuple-element.22), channel_id=1, source_target_pairs={{0,3},{1,0},{2,1},{3,2},{4,5},{5,6},{6,7},{7,4},{8,11},{9,8},{10,9... | collective-permute-start | bytes 786440 | tf_op jit(solution)/shard_map/ppermute | solution.py:400
  40.1 0.0 collective-permute-start.1
  40.1 2.5 %near.1 = (bf16[128,1024]{1,0:T(8,128)(2,1)S(1)}, bf16[128,1024]{1,0:T(8,128)(2,1)S(1)}) custom-call(bf16[1024,8192]{1,0:T(8,128)(2,1)} %weight.7, bf16[128,1024]{1,0:T(8,128)(2,1)S(1)} %get-tuple-element.20.gated), custom_call_target="tpu_custom_call" | custom-call | tf_op jit(solution)/shard_map/near/pallas_call | solution.py:426
  42.6 3.3 %collective-permute-start.4 = (bf16[128,1024]{1,0:T(8,128)(2,1)S(1)}, bf16[128,1024]{1,0:T(8,128)(2,1)S(1)}, u32[]{:S(2)}, u32[]{:S(2)}) collective-permute-start(bf16[128,1024]{1,0:T(8,128)(2,1)S(1)} %get-tuple-element.24), channel_id=1, source_target_pairs={{0,3},{1,0},{2,1},{3,2},{4,5},{5,6},{6,7},{7,4},{8,11},{9,8},{10,9... | collective-permute-start | bytes 786440 | tf_op jit(solution)/shard_map/ppermute | solution.py:400
  45.9 0.0 collective-permute-start.5
  45.9 0.6 collective-permute-done.2.got
  46.5 2.5 %joined.1 = (bf16[128,1024]{1,0:T(8,128)(2,1)S(1)}, bf16[128,1024]{1,0:T(8,128)(2,1)S(1)}) custom-call(bf16[1024,8192]{1,0:T(8,128)(2,1)} %weight.7, bf16[128,1024]{1,0:T(8,128)(2,1)S(1)} %get-tuple-element.20.gated, bf16[128,1024]{1,0:T(8,128)(2,1)S(1)} %collective-permute-done.2.got), custom_call_target="tpu_custom_call" | custom-call | tf_op jit(solution)/shard_map/joined/pallas_call | solution.py:426
  49.0 0.2 collective-permute-done.1.one
  49.2 0.1 add.1
  49.2 1.4 %collective-permute-start.3 = (bf16[128,1024]{1,0:T(8,128)(2,1)S(1)}, bf16[128,1024]{1,0:T(8,128)(2,1)S(1)}, u32[]{:S(2)}, u32[]{:S(2)}) collective-permute-start(bf16[128,1024]{1,0:T(8,128)(2,1)S(1)} %add.1), channel_id=1, source_target_pairs={{0,1},{1,2},{2,3},{3,0},{4,7},{5,4},{6,5},{7,6},{8,9},{9,10},{10,1... | collective-permute-start | bytes 786440 | tf_op jit(solution)/shard_map/ppermute | solution.py:397
  50.6 1.9 %collective-permute-start.6 = (bf16[128,1024]{1,0:T(8,128)(2,1)S(1)}, bf16[128,1024]{1,0:T(8,128)(2,1)S(1)}, u32[]{:S(2)}, u32[]{:S(2)}) collective-permute-start(bf16[128,1024]{1,0:T(8,128)(2,1)S(1)} %get-tuple-element.26), channel_id=1, source_target_pairs={{0,3},{1,0},{2,1},{3,2},{4,5},{5,6},{6,7},{7,4},{8,11},{9,8},{10,9... | collective-permute-start | bytes 786440 | tf_op jit(solution)/shard_map/ppermute | solution.py:400
  52.5 2.5 %own.1 = f32[128,2048]{1,0:T(8,128)S(1)} custom-call(bf16[1024,8192]{1,0:T(8,128)(2,1)} %weight.7, bf16[128,1024]{1,0:T(8,128)(2,1)S(1)} %get-tuple-element.20.gated), custom_call_target="tpu_custom_call" | custom-call | tf_op jit(solution)/shard_map/own/pallas_call | solution.py:440
  55.1 0.0 collective-permute-done.4.first_two
  55.1 0.0 collective-permute-done.5.second_one
  55.1 4.0 %collective-permute-done.3.first_one = bf16[128,1024]{1,0:T(8,128)(2,1)S(1)} collective-permute-done((bf16[128,1024]{1,0:T(8,128)(2,1)S(1)}, bf16[128,1024]{1,0:T(8,128)(2,1)S(1)}, u32[]{:S(2)}, u32[]{:S(2)}) %collective-permute-start.3) | collective-permute-done | bytes 262176 | tf_op jit(solution)/shard_map/ppermute | solution.py:397
  59.1 0.0 collective-permute-done.6.second_two
  59.1 0.9 %last.1 = bf16[128,2048]{1,0:T(8,128)(2,1)} custom-call(f32[128,2048]{1,0:T(8,128)S(1)} %own.1, bf16[128,1024]{1,0:T(8,128)(2,1)S(1)} %collective-permute-done.3.first_one, bf16[128,1024]{1,0:T(8,128)(2,1)S(1)} %collective-permute-done.4.first_two, bf16[128,1024]{1,0:T(8,128)(2,1)S(1)} %collective-permute-done.5.second_one, ...), custom_call_target="tpu_custom_call" | custom-call | tf_op jit(solution)/shard_map/last/pallas_call | solution.py:445
Async XLA Ops:
  2.6 18.1 %all-to-all-start = ((bf16[32,72,128]{2,1,0:T(8,128)(2,1)}), bf16[32,72,128]{2,1,0:T(8,128)(2,1)S(1)}, u32[]{:S(2)}, u32[]{:S(2)}) async-start(bf16[32,72,128]{2,1,0:T(8,128)(2,1)} %get-tuple-element.17), calls=%async_computation | async-start | bytes 1179648 | tf_op jit(solution)/shard_map/all_to_all | solution.py:358
  12.7 4.0 %collective-permute-start = (bf16[3,2,1024]{2,1,0:T(2,128)(2,1)}, bf16[3,2,1024]{2,1,0:T(2,128)(2,1)S(1)}, u32[]{:S(2)}, u32[]{:S(2)}) collective-permute-start(bf16[3,2,1024]{2,1,0:T(2,128)(2,1)} %get-tuple-element.16.token), channel_id=1, source_target_pairs={{0,4},{4,8},{8,12},{12,16},{16,20},{20,24},{24,28},{28,32},{32,36}... | collective-permute-start | bytes 36872 | tf_op jit(solution)/shard_map/ppermute | solution.py:382
  14.7 1.1 %copy-start.1 = (bf16[1600,256]{1,0:T(8,128)(2,1)S(1)}, bf16[1600,256]{1,0:T(8,128)(2,1)}, u32[]{:S(2)}) copy-start(bf16[1600,256]{1,0:T(8,128)(2,1)} %constant.2.clone.table) | copy-start | bytes 2457604
  15.9 0.7 %copy-start.3 = (bf16[3,2,1024]{2,1,0:T(2,128)(2,1)S(1)}, bf16[3,2,1024]{2,1,0:T(2,128)(2,1)}, u32[]{:S(2)}) copy-start(bf16[3,2,1024]{2,1,0:T(2,128)(2,1)} %get-tuple-element.16.token) | copy-start | bytes 36868
  22.7 12.0 %all-to-all-start.1 = ((bf16[32,32,128]{2,1,0:T(8,128)(2,1)}), bf16[32,32,128]{2,1,0:T(8,128)(2,1)S(1)}, u32[]{:S(2)}, u32[]{:S(2)}) async-start(bf16[32,32,128]{2,1,0:T(8,128)(2,1)} %conv.1.token), calls=%async_computation.1 | async-start | bytes 524288 | tf_op jit(solution)/shard_map/all_to_all | solution.py:358
  30.2 1.1 %copy-start = (bf16[128,3,1024]{2,0,1:T(8,128)(2,1)S(1)}, bf16[128,3,1024]{2,0,1:T(8,128)(2,1)}, u32[]{:S(2)}) copy-start(bf16[128,3,1024]{2,0,1:T(8,128)(2,1)} %param.6) | copy-start | bytes 2359300
  31.4 0.8 %copy-start.2 = (f32[3,3,1024]{2,1,0:T(4,128)S(1)}, f32[3,3,1024]{2,1,0:T(4,128)}, u32[]{:S(2)}) copy-start(f32[3,3,1024]{2,1,0:T(4,128)} %taps.3) | copy-start | bytes 110596
  32.2 0.7 %copy-start.4 = (f32[1024]{0:T(1024)S(1)}, f32[1024]{0:T(1024)}, u32[]{:S(2)}) copy-start(f32[1024]{0:T(1024)} %param.8) | copy-start | bytes 12292
  37.3 9.2 %collective-permute-start.2 = (bf16[128,1024]{1,0:T(8,128)(2,1)S(1)}, bf16[128,1024]{1,0:T(8,128)(2,1)S(1)}, u32[]{:S(2)}, u32[]{:S(2)}) collective-permute-start(bf16[128,1024]{1,0:T(8,128)(2,1)S(1)} %get-tuple-element.22), channel_id=1, source_target_pairs={{0,3},{1,0},{2,1},{3,2},{4,5},{5,6},{6,7},{7,4},{8,11},{9,8},{10,9... | collective-permute-start | bytes 786440 | tf_op jit(solution)/shard_map/ppermute | solution.py:400
  40.1 9.1 %collective-permute-start.1 = (bf16[128,1024]{1,0:T(8,128)(2,1)S(1)}, bf16[128,1024]{1,0:T(8,128)(2,1)S(1)}, u32[]{:S(2)}, u32[]{:S(2)}) collective-permute-start(bf16[128,1024]{1,0:T(8,128)(2,1)S(1)} %get-tuple-element.21), channel_id=1, source_target_pairs={{0,1},{1,2},{2,3},{3,0},{4,7},{5,4},{6,5},{7,6},{8,9},{9,10},{10,1... | collective-permute-start | bytes 786440 | tf_op jit(solution)/shard_map/ppermute | solution.py:397
  42.6 12.5 %collective-permute-start.4 = (bf16[128,1024]{1,0:T(8,128)(2,1)S(1)}, bf16[128,1024]{1,0:T(8,128)(2,1)S(1)}, u32[]{:S(2)}, u32[]{:S(2)}) collective-permute-start(bf16[128,1024]{1,0:T(8,128)(2,1)S(1)} %get-tuple-element.24), channel_id=1, source_target_pairs={{0,3},{1,0},{2,1},{3,2},{4,5},{5,6},{6,7},{7,4},{8,11},{9,8},{10,9... | collective-permute-start | bytes 786440 | tf_op jit(solution)/shard_map/ppermute | solution.py:400
  45.9 9.2 %collective-permute-start.5 = (bf16[128,1024]{1,0:T(8,128)(2,1)S(1)}, bf16[128,1024]{1,0:T(8,128)(2,1)S(1)}, u32[]{:S(2)}, u32[]{:S(2)}) collective-permute-start(bf16[128,1024]{1,0:T(8,128)(2,1)S(1)} %get-tuple-element.25), channel_id=1, source_target_pairs={{0,1},{1,2},{2,3},{3,0},{4,7},{5,4},{6,5},{7,6},{8,9},{9,10},{10,1... | collective-permute-start | bytes 786440 | tf_op jit(solution)/shard_map/ppermute | solution.py:397
  49.2 9.8 %collective-permute-start.3 = (bf16[128,1024]{1,0:T(8,128)(2,1)S(1)}, bf16[128,1024]{1,0:T(8,128)(2,1)S(1)}, u32[]{:S(2)}, u32[]{:S(2)}) collective-permute-start(bf16[128,1024]{1,0:T(8,128)(2,1)S(1)} %add.1), channel_id=1, source_target_pairs={{0,1},{1,2},{2,3},{3,0},{4,7},{5,4},{6,5},{7,6},{8,9},{9,10},{10,1... | collective-permute-start | bytes 786440 | tf_op jit(solution)/shard_map/ppermute | solution.py:397
  50.6 8.5 %collective-permute-start.6 = (bf16[128,1024]{1,0:T(8,128)(2,1)S(1)}, bf16[128,1024]{1,0:T(8,128)(2,1)S(1)}, u32[]{:S(2)}, u32[]{:S(2)}) collective-permute-start(bf16[128,1024]{1,0:T(8,128)(2,1)S(1)} %get-tuple-element.26), channel_id=1, source_target_pairs={{0,3},{1,0},{2,1},{3,2},{4,5},{5,6},{6,7},{7,4},{8,11},{9,8},{10,9... | collective-permute-start | bytes 786440 | tf_op jit(solution)/shard_map/ppermute | solution.py:400

commit v6 on v5

--- a/solution.py
+++ b/solution.py
@@ -156,22 +156,21 @@
         copy.wait()
 
 
-def table_kernel(token, table, out, sems):
+def table_kernel(token, table, taps, skip, table_out, taps_out, skip_out, sems):
     del token
-    start_all([(table, out)], sems)[0].wait()
-
-
-def terms_kernel(token, features, taps, skip, prior, query, direct, held, held_taps, held_skip, sems):
+    for copy in start_all([(table, table_out), (taps, taps_out), (skip, skip_out)], sems):
+        copy.wait()
+
+
+def terms_kernel(token, features, taps, skip, prior, query, direct, held, sems):
     del token
     width = query.shape[1]
-    copies = start_all([(taps, held_taps), (skip, held_skip), (features, held)], sems)
-    for copy in copies:
-        copy.wait()
+    start_all([(features, held)], sems)[0].wait()
     for start in range(0, width, 128):
         columns = slice(start, start + 128)
-        part = [whole_mixed(held, prior, held_taps, i, i, columns) for i in range(3)]
+        part = [whole_mixed(held, prior, taps, i, i, columns) for i in range(3)]
         query[:, columns] = part[0].astype(jnp.bfloat16)
-        direct[:, columns] = (held_skip[:, columns] * (part[1] * part[2])).astype(jnp.bfloat16)
+        direct[:, columns] = (skip[:, columns] * (part[1] * part[2])).astype(jnp.bfloat16)
 
 
 def rows_of(received, row):
@@ -381,7 +380,13 @@
     received = exchange(send)
     prior = lax.ppermute(tail, "seq", [(i, i + 1) for i in range(members - 1)])
     table = transform_table(order, length)
-    table = call(table_kernel, shape(table.shape, bf16), [loose, away], "table", [flags(1)])(tail, table)
+    table, taps, skip = call(
+        table_kernel,
+        (shape(table.shape, bf16), shape(short_taps.shape, f32), shape(skip.shape, f32)),
+        [loose] + [away] * 3,
+        "table",
+        [flags(3)],
+    )(tail, table, short_taps, skip)
     spectral = call(functools.partial(conv_kernel, order), turned_shape, [loose] + [inside] * 2, "conv")(prior, table, received)
     conv = exchange(spectral)
 
@@ -406,11 +411,11 @@
     query, direct = call(
         terms_kernel,
         (terms, terms),
-        [loose] + [away] * 3 + [inside],
+        [loose, away] + [inside] * 3,
         "terms",
-        [vmem((3, length, width), bf16), vmem(short_taps.shape, f32), vmem(skip.shape, f32), flags(3)],
+        [vmem((3, length, width), bf16), flags(1)],
         mebibytes=50,
-    )(spectral, by_feature, short_taps, skip, prior)
+    )(spectral, by_feature, taps, skip, prior)
     gated, far_first, far_second = call(
         far_kernel,
         (shape((length, width), bf16), right, left),

time: 60.5 us -> 60.5 us (level)
  no operation moved by 1% of the time
where the time goes in v6:
time: 60.5 us; the launch traced here: 59.9 us
  starting transfers between devices  29.1 us (48%)
  Pallas kernels  16.4 us (27%)
  waiting for transfers between devices  9.81 us (16%)
  local copies, waits for them, and re-layouts  4.46 us (7%)
    all_to_all x2, starting transfers between devices, exchange(): lax.all_to_all(value, 'seq', 0, 0, axis_index_groups=[order], tiled=True)  17.6 us
    ppermute x3, starting transfers between devices, behind(): return lax.ppermute(value, ('seq', 'chan'), route(-1))  8.08 us
    all_to_all x2, waiting for transfers between devices, exchange(): lax.all_to_all(value, 'seq', 0, 0, axis_index_groups=[order], tiled=True)  5.02 us
    pallas_call x2, Pallas kernels, pair(): call(kernel, (ahead_shape, behind_shape), [away] + [inside] * (1 + len(mo...  4.94 us
    unnamed x10, local copies, waits for them, and re-layouts  4.46 us
    ppermute x3, waiting for transfers between devices, ahead(): return lax.ppermute(value, ('seq', 'chan'), route(1))  4.18 us
    pallas_call x1, Pallas kernels, shards(): call(far_kernel, (shape((length, width), bf16), right, left), [away] + [i...  2.56 us
    pallas_call x1, Pallas kernels, shards(): call(own_kernel, shape((length, size), f32), [away, inside], 'own', [chun...  2.52 us
  transfers between devices with their start and end apart: 9, of which 5 were waited for; matrix products, arithmetic and copies ran while one was open for 0% of the time, Pallas kernels for 14%

profile of v6, /device:TPU:0, one launch (start us, length us, event | category | flops | bytes accessed | tf_op | source)
XLA Modules:
  0.0 59.9 jit_solution(2576166347966448798)
XLA Ops:
  0.0 2.5 %mix.1 = (bf16[32,72,128]{2,1,0:T(8,128)(2,1)}, bf16[3,2,1024]{2,1,0:T(2,128)(2,1)}) custom-call(bf16[3,128,1024]{2,1,0:T(8,128)(2,1)} %bitcast.2, f32[3,3,1024]{2,1,0:T(4,128)} %taps.3, f32[128,1024]{1,0:T(8,128)} %long_filter.1), custom_call_target="tpu_custom_call" | custom-call | tf_op jit(solution)/shard_map/mix/pallas_call | solution.py:362
  2.5 10.1 %all-to-all-start = ((bf16[32,72,128]{2,1,0:T(8,128)(2,1)}), bf16[32,72,128]{2,1,0:T(8,128)(2,1)S(1)}, u32[]{:S(2)}, u32[]{:S(2)}) async-start(bf16[32,72,128]{2,1,0:T(8,128)(2,1)} %get-tuple-element.21), calls=%async_computation | async-start | bytes 1179648 | tf_op jit(solution)/shard_map/all_to_all | solution.py:357
  12.6 2.1 %collective-permute-start = (bf16[3,2,1024]{2,1,0:T(2,128)(2,1)}, bf16[3,2,1024]{2,1,0:T(2,128)(2,1)S(1)}, u32[]{:S(2)}, u32[]{:S(2)}) collective-permute-start(bf16[3,2,1024]{2,1,0:T(2,128)(2,1)} %get-tuple-element.19.token), channel_id=1, source_target_pairs={{0,4},{4,8},{8,12},{12,16},{16,20},{20,24},{24,28},{28,32},{32,36}... | collective-permute-start | bytes 36872 | tf_op jit(solution)/shard_map/ppermute | solution.py:381
  14.7 0.0 copy-start.1
  14.7 1.1 %copy-done.1 = bf16[1600,256]{1,0:T(8,128)(2,1)S(1)} copy-done((bf16[1600,256]{1,0:T(8,128)(2,1)S(1)}, bf16[1600,256]{1,0:T(8,128)(2,1)}, u32[]{:S(2)}) %copy-start.1) | copy-done | bytes 819224
  15.8 0.0 copy-start.2
  15.8 0.8 %copy-done.2 = f32[3,3,1024]{2,1,0:T(4,128)S(1)} copy-done((f32[3,3,1024]{2,1,0:T(4,128)S(1)}, f32[3,3,1024]{2,1,0:T(4,128)}, u32[]{:S(2)}) %copy-start.2) | copy-done | bytes 36888
  16.6 0.0 copy-start.3
  16.6 0.7 %copy-done.3 = bf16[3,2,1024]{2,1,0:T(2,128)(2,1)S(1)} copy-done((bf16[3,2,1024]{2,1,0:T(2,128)(2,1)S(1)}, bf16[3,2,1024]{2,1,0:T(2,128)(2,1)}, u32[]{:S(2)}) %copy-start.3) | copy-done | bytes 12312
  17.3 0.0 copy-start.4
  17.3 0.7 %copy-done.4 = f32[1024]{0:T(1024)S(1)} copy-done((f32[1024]{0:T(1024)S(1)}, f32[1024]{0:T(1024)}, u32[]{:S(2)}) %copy-start.4) | copy-done | bytes 4120
  18.0 0.2 table.2
  18.2 0.0 collective-permute-done.token.prior
  18.2 2.4 %all-to-all-done.received = bf16[32,72,128]{2,1,0:T(8,128)(2,1)S(1)} async-done(((bf16[32,72,128]{2,1,0:T(8,128)(2,1)}), bf16[32,72,128]{2,1,0:T(8,128)(2,1)S(1)}, u32[]{:S(2)}, u32[]{:S(2)}) %all-to-all-start) | async-done | bytes 589856 | tf_op jit(solution)/shard_map/all_to_all | solution.py:357
  20.6 2.1 %conv.1.token = bf16[32,32,128]{2,1,0:T(8,128)(2,1)} custom-call(bf16[3,2,1024]{2,1,0:T(2,128)(2,1)S(1)} %collective-permute-done.token.prior, bf16[1600,256]{1,0:T(8,128)(2,1)S(1)} %get-tuple-element.20.table, bf16[32,72,128]{2,1,0:T(8,128)(2,1)S(1)} %all-to-all-done.received), custom_call_target="tpu_custom_call" | custom-call | tf_op jit(solution)/shard_map/conv/pallas_call | solution.py:390
  22.7 7.5 %all-to-all-start.1 = ((bf16[32,32,128]{2,1,0:T(8,128)(2,1)}), bf16[32,32,128]{2,1,0:T(8,128)(2,1)S(1)}, u32[]{:S(2)}, u32[]{:S(2)}) async-start(bf16[32,32,128]{2,1,0:T(8,128)(2,1)} %conv.1.token), calls=%async_computation.1 | async-start | bytes 524288 | tf_op jit(solution)/shard_map/all_to_all | solution.py:357
  30.2 0.0 copy-start
  30.2 1.1 %copy-done = bf16[128,3,1024]{2,0,1:T(8,128)(2,1)S(1)} copy-done((bf16[128,3,1024]{2,0,1:T(8,128)(2,1)S(1)}, bf16[128,3,1024]{2,0,1:T(8,128)(2,1)}, u32[]{:S(2)}) %copy-start) | copy-done | bytes 786456
  31.3 0.7 %terms.1 = (bf16[128,1024]{1,0:T(8,128)(2,1)S(1)}, bf16[128,1024]{1,0:T(8,128)(2,1)S(1)}) custom-call(bf16[32,32,128]{2,1,0:T(8,128)(2,1)} %conv.1.token, bf16[3,128,1024]{2,1,0:T(8,128)(2,1)S(1)} %bitcast.3, f32[3,3,1024]{2,1,0:T(4,128)S(1)} %get-tuple-element.22.taps, f32[1,1024]{1,0:T(1,128)S(1)} %get-tuple-element.23.skip, ...), custom_call_target="tpu_custom_call" | custom-call | tf_op jit(solution)/shard_map/terms/pallas_call | solution.py:411
  32.0 2.6 %all-to-all-done.1.conv = bf16[32,32,128]{2,1,0:T(8,128)(2,1)S(1)} async-done(((bf16[32,32,128]{2,1,0:T(8,128)(2,1)}), bf16[32,32,128]{2,1,0:T(8,128)(2,1)S(1)}, u32[]{:S(2)}, u32[]{:S(2)}) %all-to-all-start.1) | async-done | bytes 262176 | tf_op jit(solution)/shard_map/all_to_all | solution.py:357
  34.6 2.6 %far.1 = (bf16[128,1024]{1,0:T(8,128)(2,1)S(1)}, bf16[128,1024]{1,0:T(8,128)(2,1)S(1)}, bf16[128,1024]{1,0:T(8,128)(2,1)S(1)}) custom-call(bf16[1024,8192]{1,0:T(8,128)(2,1)} %weight.7, bf16[128,1024]{1,0:T(8,128)(2,1)S(1)} %get-tuple-element.24.query, bf16[128,1024]{1,0:T(8,128)(2,1)S(1)} %get-tuple-element.25.direct, ...), custom_call_target="tpu_custom_call" | custom-call | tf_op jit(solution)/shard_map/far/pallas_call | solution.py:419
  37.2 2.8 %collective-permute-start.2 = (bf16[128,1024]{1,0:T(8,128)(2,1)S(1)}, bf16[128,1024]{1,0:T(8,128)(2,1)S(1)}, u32[]{:S(2)}, u32[]{:S(2)}) collective-permute-start(bf16[128,1024]{1,0:T(8,128)(2,1)S(1)} %get-tuple-element.28), channel_id=1, source_target_pairs={{0,3},{1,0},{2,1},{3,2},{4,5},{5,6},{6,7},{7,4},{8,11},{9,8},{10,9... | collective-permute-start | bytes 786440 | tf_op jit(solution)/shard_map/ppermute | solution.py:405
  40.0 0.0 collective-permute-start.1
  40.0 2.5 %near.1 = (bf16[128,1024]{1,0:T(8,128)(2,1)S(1)}, bf16[128,1024]{1,0:T(8,128)(2,1)S(1)}) custom-call(bf16[1024,8192]{1,0:T(8,128)(2,1)} %weight.7, bf16[128,1024]{1,0:T(8,128)(2,1)S(1)} %get-tuple-element.26.gated), custom_call_target="tpu_custom_call" | custom-call | tf_op jit(solution)/shard_map/near/pallas_call | solution.py:431
  42.5 3.3 %collective-permute-start.4 = (bf16[128,1024]{1,0:T(8,128)(2,1)S(1)}, bf16[128,1024]{1,0:T(8,128)(2,1)S(1)}, u32[]{:S(2)}, u32[]{:S(2)}) collective-permute-start(bf16[128,1024]{1,0:T(8,128)(2,1)S(1)} %get-tuple-element.30), channel_id=1, source_target_pairs={{0,3},{1,0},{2,1},{3,2},{4,5},{5,6},{6,7},{7,4},{8,11},{9,8},{10,9... | collective-permute-start | bytes 786440 | tf_op jit(solution)/shard_map/ppermute | solution.py:405
  45.8 0.0 collective-permute-start.5
  45.8 0.6 collective-permute-done.2.got
  46.4 2.5 %joined.1 = (bf16[128,1024]{1,0:T(8,128)(2,1)S(1)}, bf16[128,1024]{1,0:T(8,128)(2,1)S(1)}) custom-call(bf16[1024,8192]{1,0:T(8,128)(2,1)} %weight.7, bf16[128,1024]{1,0:T(8,128)(2,1)S(1)} %get-tuple-element.26.gated, bf16[128,1024]{1,0:T(8,128)(2,1)S(1)} %collective-permute-done.2.got), custom_call_target="tpu_custom_call" | custom-call | tf_op jit(solution)/shard_map/joined/pallas_call | solution.py:431
  48.9 0.2 collective-permute-done.1.one
  49.1 0.1 add.1
  49.2 1.4 %collective-permute-start.3 = (bf16[128,1024]{1,0:T(8,128)(2,1)S(1)}, bf16[128,1024]{1,0:T(8,128)(2,1)S(1)}, u32[]{:S(2)}, u32[]{:S(2)}) collective-permute-start(bf16[128,1024]{1,0:T(8,128)(2,1)S(1)} %add.1), channel_id=1, source_target_pairs={{0,1},{1,2},{2,3},{3,0},{4,7},{5,4},{6,5},{7,6},{8,9},{9,10},{10,1... | collective-permute-start | bytes 786440 | tf_op jit(solution)/shard_map/ppermute | solution.py:402
  50.5 2.0 %collective-permute-start.6 = (bf16[128,1024]{1,0:T(8,128)(2,1)S(1)}, bf16[128,1024]{1,0:T(8,128)(2,1)S(1)}, u32[]{:S(2)}, u32[]{:S(2)}) collective-permute-start(bf16[128,1024]{1,0:T(8,128)(2,1)S(1)} %get-tuple-element.32), channel_id=1, source_target_pairs={{0,3},{1,0},{2,1},{3,2},{4,5},{5,6},{6,7},{7,4},{8,11},{9,8},{10,9... | collective-permute-start | bytes 786440 | tf_op jit(solution)/shard_map/ppermute | solution.py:405
  52.5 2.5 %own.1 = f32[128,2048]{1,0:T(8,128)S(1)} custom-call(bf16[1024,8192]{1,0:T(8,128)(2,1)} %weight.7, bf16[128,1024]{1,0:T(8,128)(2,1)S(1)} %get-tuple-element.26.gated), custom_call_target="tpu_custom_call" | custom-call | tf_op jit(solution)/shard_map/own/pallas_call | solution.py:445
  55.0 0.0 collective-permute-done.4.first_two
  55.0 0.0 collective-permute-done.5.second_one
  55.0 4.0 %collective-permute-done.3.first_one = bf16[128,1024]{1,0:T(8,128)(2,1)S(1)} collective-permute-done((bf16[128,1024]{1,0:T(8,128)(2,1)S(1)}, bf16[128,1024]{1,0:T(8,128)(2,1)S(1)}, u32[]{:S(2)}, u32[]{:S(2)}) %collective-permute-start.3) | collective-permute-done | bytes 262176 | tf_op jit(solution)/shard_map/ppermute | solution.py:402
  59.0 0.0 collective-permute-done.6.second_two
  59.0 0.9 %last.1 = bf16[128,2048]{1,0:T(8,128)(2,1)} custom-call(f32[128,2048]{1,0:T(8,128)S(1)} %own.1, bf16[128,1024]{1,0:T(8,128)(2,1)S(1)} %collective-permute-done.3.first_one, bf16[128,1024]{1,0:T(8,128)(2,1)S(1)} %collective-permute-done.4.first_two, bf16[128,1024]{1,0:T(8,128)(2,1)S(1)} %collective-permute-done.5.second_one, ...), custom_call_target="tpu_custom_call" | custom-call | tf_op jit(solution)/shard_map/last/pallas_call | solution.py:450
Async XLA Ops:
  2.5 18.1 %all-to-all-start = ((bf16[32,72,128]{2,1,0:T(8,128)(2,1)}), bf16[32,72,128]{2,1,0:T(8,128)(2,1)S(1)}, u32[]{:S(2)}, u32[]{:S(2)}) async-start(bf16[32,72,128]{2,1,0:T(8,128)(2,1)} %get-tuple-element.21), calls=%async_computation | async-start | bytes 1179648 | tf_op jit(solution)/shard_map/all_to_all | solution.py:357
  12.6 5.6 %collective-permute-start = (bf16[3,2,1024]{2,1,0:T(2,128)(2,1)}, bf16[3,2,1024]{2,1,0:T(2,128)(2,1)S(1)}, u32[]{:S(2)}, u32[]{:S(2)}) collective-permute-start(bf16[3,2,1024]{2,1,0:T(2,128)(2,1)} %get-tuple-element.19.token), channel_id=1, source_target_pairs={{0,4},{4,8},{8,12},{12,16},{16,20},{20,24},{24,28},{28,32},{32,36}... | collective-permute-start | bytes 36872 | tf_op jit(solution)/shard_map/ppermute | solution.py:381
  14.7 1.1 %copy-start.1 = (bf16[1600,256]{1,0:T(8,128)(2,1)S(1)}, bf16[1600,256]{1,0:T(8,128)(2,1)}, u32[]{:S(2)}) copy-start(bf16[1600,256]{1,0:T(8,128)(2,1)} %constant.2.clone.table) | copy-start | bytes 2457604
  15.8 0.8 %copy-start.2 = (f32[3,3,1024]{2,1,0:T(4,128)S(1)}, f32[3,3,1024]{2,1,0:T(4,128)}, u32[]{:S(2)}) copy-start(f32[3,3,1024]{2,1,0:T(4,128)} %taps.3) | copy-start | bytes 110596
  16.6 0.7 %copy-start.3 = (bf16[3,2,1024]{2,1,0:T(2,128)(2,1)S(1)}, bf16[3,2,1024]{2,1,0:T(2,128)(2,1)}, u32[]{:S(2)}) copy-start(bf16[3,2,1024]{2,1,0:T(2,128)(2,1)} %get-tuple-element.19.token) | copy-start | bytes 36868
  17.3 0.7 %copy-start.4 = (f32[1024]{0:T(1024)S(1)}, f32[1024]{0:T(1024)}, u32[]{:S(2)}) copy-start(f32[1024]{0:T(1024)} %param.8) | copy-start | bytes 12292
  22.7 12.0 %all-to-all-start.1 = ((bf16[32,32,128]{2,1,0:T(8,128)(2,1)}), bf16[32,32,128]{2,1,0:T(8,128)(2,1)S(1)}, u32[]{:S(2)}, u32[]{:S(2)}) async-start(bf16[32,32,128]{2,1,0:T(8,128)(2,1)} %conv.1.token), calls=%async_computation.1 | async-start | bytes 524288 | tf_op jit(solution)/shard_map/all_to_all | solution.py:357
  30.2 1.1 %copy-start = (bf16[128,3,1024]{2,0,1:T(8,128)(2,1)S(1)}, bf16[128,3,1024]{2,0,1:T(8,128)(2,1)}, u32[]{:S(2)}) copy-start(bf16[128,3,1024]{2,0,1:T(8,128)(2,1)} %param.6) | copy-start | bytes 2359300
  37.2 9.2 %collective-permute-start.2 = (bf16[128,1024]{1,0:T(8,128)(2,1)S(1)}, bf16[128,1024]{1,0:T(8,128)(2,1)S(1)}, u32[]{:S(2)}, u32[]{:S(2)}) collective-permute-start(bf16[128,1024]{1,0:T(8,128)(2,1)S(1)} %get-tuple-element.28), channel_id=1, source_target_pairs={{0,3},{1,0},{2,1},{3,2},{4,5},{5,6},{6,7},{7,4},{8,11},{9,8},{10,9... | collective-permute-start | bytes 786440 | tf_op jit(solution)/shard_map/ppermute | solution.py:405
  40.0 9.1 %collective-permute-start.1 = (bf16[128,1024]{1,0:T(8,128)(2,1)S(1)}, bf16[128,1024]{1,0:T(8,128)(2,1)S(1)}, u32[]{:S(2)}, u32[]{:S(2)}) collective-permute-start(bf16[128,1024]{1,0:T(8,128)(2,1)S(1)} %get-tuple-element.27), channel_id=1, source_target_pairs={{0,1},{1,2},{2,3},{3,0},{4,7},{5,4},{6,5},{7,6},{8,9},{9,10},{10,1... | collective-permute-start | bytes 786440 | tf_op jit(solution)/shard_map/ppermute | solution.py:402
  42.5 12.5 %collective-permute-start.4 = (bf16[128,1024]{1,0:T(8,128)(2,1)S(1)}, bf16[128,1024]{1,0:T(8,128)(2,1)S(1)}, u32[]{:S(2)}, u32[]{:S(2)}) collective-permute-start(bf16[128,1024]{1,0:T(8,128)(2,1)S(1)} %get-tuple-element.30), channel_id=1, source_target_pairs={{0,3},{1,0},{2,1},{3,2},{4,5},{5,6},{6,7},{7,4},{8,11},{9,8},{10,9... | collective-permute-start | bytes 786440 | tf_op jit(solution)/shard_map/ppermute | solution.py:405
  45.8 9.2 %collective-permute-start.5 = (bf16[128,1024]{1,0:T(8,128)(2,1)S(1)}, bf16[128,1024]{1,0:T(8,128)(2,1)S(1)}, u32[]{:S(2)}, u32[]{:S(2)}) collective-permute-start(bf16[128,1024]{1,0:T(8,128)(2,1)S(1)} %get-tuple-element.31), channel_id=1, source_target_pairs={{0,1},{1,2},{2,3},{3,0},{4,7},{5,4},{6,5},{7,6},{8,9},{9,10},{10,1... | collective-permute-start | bytes 786440 | tf_op jit(solution)/shard_map/ppermute | solution.py:402
  49.2 9.9 %collective-permute-start.3 = (bf16[128,1024]{1,0:T(8,128)(2,1)S(1)}, bf16[128,1024]{1,0:T(8,128)(2,1)S(1)}, u32[]{:S(2)}, u32[]{:S(2)}) collective-permute-start(bf16[128,1024]{1,0:T(8,128)(2,1)S(1)} %add.1), channel_id=1, source_target_pairs={{0,1},{1,2},{2,3},{3,0},{4,7},{5,4},{6,5},{7,6},{8,9},{9,10},{10,1... | collective-permute-start | bytes 786440 | tf_op jit(solution)/shard_map/ppermute | solution.py:402
  50.5 8.5 %collective-permute-start.6 = (bf16[128,1024]{1,0:T(8,128)(2,1)S(1)}, bf16[128,1024]{1,0:T(8,128)(2,1)S(1)}, u32[]{:S(2)}, u32[]{:S(2)}) collective-permute-start(bf16[128,1024]{1,0:T(8,128)(2,1)S(1)} %get-tuple-element.32), channel_id=1, source_target_pairs={{0,3},{1,0},{2,1},{3,2},{4,5},{5,6},{6,7},{7,4},{8,11},{9,8},{10,9... | collective-permute-start | bytes 786440 | tf_op jit(solution)/shard_map/ppermute | solution.py:405
